TPU v7x, 512 devices: a whole 4x8x8 slice. The times are simulated.
512 devices in a mesh: freq: 8 (over y), tile: 64 (over z, x, core).
Axes of the slice: x: 4, y: 8, z: 8, core: 2. Of those that a mesh axis runs over, the one named last changes fastest.
Arguments:
- source: float32 [6, 256, 16, 128], P(None, 'tile'), may hold values from -6 to 6
- conductivity: float32 [256, 16, 128], P('tile'), may hold values from 0.3 to 3.3
- freq_factor: float32 [8], P('freq'), may hold values from 0.5 to 8
- observed: float32 [8, 6, 32768], P('freq', None, 'tile'), may hold values from -6 to 6
- slot_cells: int32 [32768], P('tile'), may hold values from 0 to 8191
- block_counts: int32 [4096], P('tile'), may hold values from 0 to 8, as said below
Outputs:
- field: float32 [8, 6, 256, 16, 128], P('freq', None, 'tile')
- gradient: float32 [256, 16, 128], P('tile')
Inputs may be any that keep to these rules, and one draw needn't show every extreme that they name: block_counts[s * 64 + d] is the number of live slots in the block that tile s holds for tile d; in every draw some tile receives 8 live records from every tile.
All inputs are finite; a program needn't handle non-finite values.
Results may differ from a plain program's by a relative error of at most 0.0001.
Values sent between devices are 32-bit elements; how exact they have to be, the bound alone decides.
No kernel may reach another device: no remote copies, remote signals or barrier semaphores. Data moves between devices by JAX's collectives and lax.ppermute only.
A program may use at most 64 MiB of HBM per device.

v0:
```python
import jax
import jax.numpy as jnp
from jax import lax
from jax.sharding import PartitionSpec as P

SWEEPS = 4


DAMPING = 0.8


def extended(cells, sides, width):
    for axis, dim in sides:
        count = lax.axis_size(axis)
        ends = count - 1
        head = lax.slice_in_dim(cells, 0, width, axis=dim)
        tail = lax.slice_in_dim(cells, cells.shape[dim] - width, cells.shape[dim], axis=dim)
        cells = jnp.concatenate(
            [
                lax.ppermute(tail, axis, [(i, (i + 1) % count) for i in range(ends)]),
                cells,
                lax.ppermute(head, axis, [((i + 1) % count, i) for i in range(ends)]),
            ],
            axis=dim,
        )
    return cells


def relax(field, conductance, source, factor):
    middle = field[:, 1:-1]
    beside = field[:, 2:] + field[:, :-2]
    padded_y = jnp.pad(middle, ((0, 0), (0, 0), (1, 1), (0, 0)))
    beside = beside + padded_y[:, :, 2:] + padded_y[:, :, :-2]
    padded_z = jnp.pad(middle, ((0, 0), (0, 0), (0, 0), (1, 1)))
    beside = beside + padded_z[:, :, :, 2:] + padded_z[:, :, :, :-2]
    laplace_term = 6.0 * middle - beside
    absorb = factor * conductance
    applied_re = laplace_term[:3] - absorb * middle[3:]
    applied_im = laplace_term[3:] + absorb * middle[:3]
    resid_re = source[:3] - applied_re
    resid_im = source[3:] - applied_im
    divisor = 36.0 + absorb * absorb
    delta_re = DAMPING * (6.0 * resid_re + absorb * resid_im) / divisor
    delta_im = DAMPING * (6.0 * resid_im - absorb * resid_re) / divisor
    return middle + jnp.concatenate([delta_re, delta_im], 0)


def solve(source, conductivity, factor):
    field = jnp.zeros_like(source)
    for sweep_index in range(SWEEPS):
        padded = extended(field, (("tile", 1),), 1)
        field = relax(padded, conductivity, source, factor)
    return field


def body(source, conductivity, freq_factor, observed, slot_cells, block_counts):
    factor = freq_factor[0]
    field = solve(source, conductivity, factor)
    tiles = lax.axis_size("tile")
    slots = slot_cells.shape[0] // tiles
    values_in = lax.all_to_all(observed[0], "tile", split_axis=1, concat_axis=1, tiled=True)
    cells_in, counts_in = (
        lax.all_to_all(slot_cells, "tile", split_axis=0, concat_axis=0, tiled=True),
        lax.all_to_all(block_counts, "tile", split_axis=0, concat_axis=0, tiled=True),
    )
    within = jnp.arange(slots, dtype=jnp.int32)[None, :]
    live = (within < counts_in[:, None]).astype(jnp.float32).reshape(-1)
    flat = field.reshape(6, -1)
    misfit = (flat[:, cells_in] - values_in) * live[None, :]
    adjoint_source = jnp.zeros_like(flat).at[:, cells_in].add(misfit).reshape(field.shape)
    adjoint = solve(adjoint_source, conductivity, factor)
    term = factor * jnp.sum(adjoint[:3] * field[3:] + adjoint[3:] * field[:3], axis=0)
    gradient = lax.psum(term, "freq")
    return (field[None], gradient)


def solution(mesh):
    in_specs = (
        P(None, "tile", None, None),
        P("tile", None, None),
        P("freq"),
        P("freq", None, "tile"),
        P("tile"),
        P("tile"),
    )
    out_specs = (P("freq", None, "tile", None, None), P("tile", None, None))
    return jax.shard_map(body, mesh=mesh, in_specs=in_specs, out_specs=out_specs, check_vma=False)
```

profile of v0, /device:TPU:256, one launch (start us, length us, event | category | flops | bytes accessed | tf_op | source)
XLA Modules:
  0.0 182.1 jit_solution(9455473573731177131)
XLA Ops:
  0.7 2.1 %collective-permute-start.1 = (f32[6,1,16,128]{3,2,1,0:T(8,128)S(1)}, f32[6,1,16,128]{3,2,1,0:T(8,128)S(1)}, u32[]{:S(2)}, u32[]{:S(2)}) collective-permute-start(f32[6,1,16,128]{3,2,1,0:T(8,128)S(1)} %broadcast.81), channel_id=1, source_target_pairs={{0,1},{1,2},{2,3},{3,4},{4,5},{5,6},{6,7},{7,8},{8,9},{9,10},{10,1... | collective-permute-start | bytes 147464 | tf_op jit(solution)/shard_map/ppermute | solution.py:20
  2.7 7.0 %collective-permute-start = (f32[6,1,16,128]{3,2,1,0:T(8,128)S(1)}, f32[6,1,16,128]{3,2,1,0:T(8,128)S(1)}, u32[]{:S(2)}, u32[]{:S(2)}) collective-permute-start(f32[6,1,16,128]{3,2,1,0:T(8,128)S(1)} %broadcast.81), channel_id=1, source_target_pairs={{1,0},{2,1},{3,2},{4,3},{5,4},{6,5},{7,6},{8,7},{9,8},{10,9},{11,1... | collective-permute-start | bytes 147464 | tf_op jit(solution)/shard_map/ppermute | solution.py:22
  9.7 1.4 copy.78
  11.0 7.9 %all-to-all-start.2 = ((s32[64,1,1]{2,1,0:T(1,128)}), s32[64,1,1]{2,1,0:T(1,128)S(1)}, u32[]{:S(2)}, u32[]{:S(2)}) async-start(s32[64,1,1]{2,1,0:T(1,128)} %copy.78), calls=%async_computation.2 | async-start | bytes 65536 | tf_op jit(solution)/shard_map/all_to_all | solution.py:64
  19.6 0.8 broadcast_multiply_fusion
  20.3 1.4 all_to_all.22
  21.7 0.7 reduce.1
  22.5 0.1 all_to_all.25
  22.6 0.8 copy.76
  23.4 0.2 all-to-all-done.2
  23.6 10.1 %all-to-all-start = ((s32[64,8,1]{1,2,0:T(1,128)}), s32[64,8,1]{1,2,0:T(1,128)S(1)}, u32[]{:S(2)}, u32[]{:S(2)}) async-start(s32[64,8,1]{1,2,0:T(1,128)} %bitcast.9), calls=%async_computation | async-start | bytes 65536 | tf_op jit(solution)/shard_map/all_to_all | solution.py:63
  33.7 1.2 reduce.2
  34.9 0.1 fusion.83
  35.0 0.1 reshape.185
  35.1 3.3 %all-to-all-done = s32[64,8,1]{1,2,0:T(1,128)S(1)} async-done(((s32[64,8,1]{1,2,0:T(1,128)}), s32[64,8,1]{1,2,0:T(1,128)S(1)}, u32[]{:S(2)}, u32[]{:S(2)}) %all-to-all-start) | async-done | bytes 2080 | tf_op jit(solution)/shard_map/all_to_all | solution.py:63
  38.5 9.4 %all-to-all-start.1 = ((f32[6,64,8]{2,0,1:T(8,128)}), f32[6,64,8]{2,0,1:T(8,128)S(1)}, u32[]{:S(2)}, u32[]{:S(2)}) async-start(f32[6,64,8]{2,0,1:T(8,128)} %copy.76), calls=%async_computation.1 | async-start | bytes 524288 | tf_op jit(solution)/shard_map/all_to_all | solution.py:61
  47.9 0.5 broadcast.140
  48.4 0.7 reduce.5
  49.1 0.1 all_to_all.24
  49.2 7.9 %all-to-all-done.1 = f32[6,64,8]{2,0,1:T(8,128)S(1)} async-done(((f32[6,64,8]{2,0,1:T(8,128)}), f32[6,64,8]{2,0,1:T(8,128)S(1)}, u32[]{:S(2)}, u32[]{:S(2)}) %all-to-all-start.1) | async-done | bytes 12320 | tf_op jit(solution)/shard_map/all_to_all | solution.py:61
  57.1 0.4 copy.77
  57.6 0.2 fusion.13
  57.7 1.0 multiply_divide_fusion.15
  58.8 4.4 %collective-permute-start.2 = (f32[6,1,16,128]{3,2,1,0:T(8,128)S(1)}, f32[6,1,16,128]{3,2,1,0:T(8,128)S(1)}, u32[]{:S(2)}, u32[]{:S(2)}) collective-permute-start(f32[6,1,16,128]{3,2,1,0:T(8,128)S(1)} %get-tuple-element.32), channel_id=1, source_target_pairs={{1,0},{2,1},{3,2},{4,3},{5,4},{6,5},{7,6},{8,7},{9,8},{10,9},{11,1... | collective-permute-start | bytes 147464 | tf_op jit(solution)/shard_map/ppermute | solution.py:22
  63.2 1.9 %collective-permute-start.3 = (f32[6,1,16,128]{3,2,1,0:T(8,128)S(1)}, f32[6,1,16,128]{3,2,1,0:T(8,128)S(1)}, u32[]{:S(2)}, u32[]{:S(2)}) collective-permute-start(f32[6,1,16,128]{3,2,1,0:T(8,128)S(1)} %get-tuple-element.33), channel_id=1, source_target_pairs={{0,1},{1,2},{2,3},{3,4},{4,5},{5,6},{6,7},{7,8},{8,9},{9,10},{10,1... | collective-permute-start | bytes 147464 | tf_op jit(solution)/shard_map/ppermute | solution.py:20
  65.1 0.1 copy_bitcast_fusion.6
  65.3 6.6 %collective-permute-done.3 = f32[6,1,16,128]{3,2,1,0:T(8,128)S(1)} collective-permute-done((f32[6,1,16,128]{3,2,1,0:T(8,128)S(1)}, f32[6,1,16,128]{3,2,1,0:T(8,128)S(1)}, u32[]{:S(2)}, u32[]{:S(2)}) %collective-permute-start.3) | collective-permute-done | bytes 49184 | tf_op jit(solution)/shard_map/ppermute | solution.py:20
  71.9 0.2 fusion.18
  72.1 0.1 multiply_divide_fusion.13
  72.2 1.9 %collective-permute-start.4 = (f32[6,1,16,128]{3,2,1,0:T(8,128)S(1)}, f32[6,1,16,128]{3,2,1,0:T(8,128)S(1)}, u32[]{:S(2)}, u32[]{:S(2)}) collective-permute-start(f32[6,1,16,128]{3,2,1,0:T(8,128)S(1)} %get-tuple-element.30), channel_id=1, source_target_pairs={{1,0},{2,1},{3,2},{4,3},{5,4},{6,5},{7,6},{8,7},{9,8},{10,9},{11,1... | collective-permute-start | bytes 147464 | tf_op jit(solution)/shard_map/ppermute | solution.py:22
  74.1 2.4 %collective-permute-start.5 = (f32[6,1,16,128]{3,2,1,0:T(8,128)S(1)}, f32[6,1,16,128]{3,2,1,0:T(8,128)S(1)}, u32[]{:S(2)}, u32[]{:S(2)}) collective-permute-start(f32[6,1,16,128]{3,2,1,0:T(8,128)S(1)} %get-tuple-element.31), channel_id=1, source_target_pairs={{0,1},{1,2},{2,3},{3,4},{4,5},{5,6},{6,7},{7,8},{8,9},{9,10},{10,1... | collective-permute-start | bytes 147464 | tf_op jit(solution)/shard_map/ppermute | solution.py:20
  76.6 0.1 copy_bitcast_fusion.4
  76.7 6.2 %collective-permute-done.5 = f32[6,1,16,128]{3,2,1,0:T(8,128)S(1)} collective-permute-done((f32[6,1,16,128]{3,2,1,0:T(8,128)S(1)}, f32[6,1,16,128]{3,2,1,0:T(8,128)S(1)}, u32[]{:S(2)}, u32[]{:S(2)}) %collective-permute-start.5) | collective-permute-done | bytes 49184 | tf_op jit(solution)/shard_map/ppermute | solution.py:20
  82.9 0.2 fusion.23
  83.0 0.1 multiply_divide_fusion.11
  83.2 1.9 %collective-permute-start.6 = (f32[6,1,16,128]{3,2,1,0:T(8,128)S(1)}, f32[6,1,16,128]{3,2,1,0:T(8,128)S(1)}, u32[]{:S(2)}, u32[]{:S(2)}) collective-permute-start(f32[6,1,16,128]{3,2,1,0:T(8,128)S(1)} %get-tuple-element.28), channel_id=1, source_target_pairs={{1,0},{2,1},{3,2},{4,3},{5,4},{6,5},{7,6},{8,7},{9,8},{10,9},{11,1... | collective-permute-start | bytes 147464 | tf_op jit(solution)/shard_map/ppermute | solution.py:22
  85.1 2.4 %collective-permute-start.7 = (f32[6,1,16,128]{3,2,1,0:T(8,128)S(1)}, f32[6,1,16,128]{3,2,1,0:T(8,128)S(1)}, u32[]{:S(2)}, u32[]{:S(2)}) collective-permute-start(f32[6,1,16,128]{3,2,1,0:T(8,128)S(1)} %get-tuple-element.29), channel_id=1, source_target_pairs={{0,1},{1,2},{2,3},{3,4},{4,5},{5,6},{6,7},{7,8},{8,9},{9,10},{10,1... | collective-permute-start | bytes 147464 | tf_op jit(solution)/shard_map/ppermute | solution.py:20
  87.5 0.1 copy_bitcast_fusion.2
  87.7 6.2 %collective-permute-done.7 = f32[6,1,16,128]{3,2,1,0:T(8,128)S(1)} collective-permute-done((f32[6,1,16,128]{3,2,1,0:T(8,128)S(1)}, f32[6,1,16,128]{3,2,1,0:T(8,128)S(1)}, u32[]{:S(2)}, u32[]{:S(2)}) %collective-permute-start.7) | collective-permute-done | bytes 49184 | tf_op jit(solution)/shard_map/ppermute | solution.py:20
  93.8 0.2 fusion.28
  94.0 0.1 multiply_divide_fusion.9
  94.1 0.1 copy_bitcast_fusion
  94.2 0.2 fusion.3
  94.4 2.7 %copy.75 = f32[6,8192]{0,1:T(8,128)} copy(f32[6,8192]{1,0:T(8,128)S(1)} %fusion.3) | data formatting | bytes 393216 | tf_op jit(solution)/shard_map/add | solution.py:45
  97.1 7.4 %scatter_custom_fusion = f32[6,8192]{0,1:T(8,128)} fusion(s32[512]{0:T(512)S(1)} %bitcast.83, f32[]{:T(128)} %constant.6.clone.1, f32[6,64,8]{0,2,1:T(8,128)S(1)} %copy.77, f32[512]{0:T(512)S(1)} %reshape.185, f32[6,8192]{0,1:T(8,128)} %copy.75, s32[1024]{0:T(1024)S(1)} %pad_clamp_fusion), kind=kCustom, calls=%fused_computation.2 | custom fusion | flops 9216 | bytes 661508 | tf_op jit(solution)/shard_map/scatter-add | solution.py:70
  104.5 7.9 %fusion.85 = (f32[3,8192]{0,1:T(8,128)}, f32[3,8192]{0,1:T(8,128)}) fusion(f32[6,8192]{0,1:T(8,128)} %scatter_custom_fusion), kind=kLoop, calls=%fused_computation.198 | loop fusion | bytes 393216 | tf_op jit(solution)/shard_map/slice | solution.py:41
  112.4 2.8 %copy.80 = f32[3,4,16,128]{3,2,1,0:T(8,128)S(1)} copy(f32[3,4,16,128]{0,3,2,1:T(8,128)} %bitcast.65) | data formatting | bytes 196608 | tf_op jit(solution)/shard_map/slice | solution.py:41
  115.3 2.9 %copy.79 = f32[3,4,16,128]{3,2,1,0:T(8,128)S(1)} copy(f32[3,4,16,128]{0,3,2,1:T(8,128)} %bitcast.64) | data formatting | bytes 196608 | tf_op jit(solution)/shard_map/slice | solution.py:40
  118.2 1.9 %collective-permute-start.8 = (f32[6,1,16,128]{3,2,1,0:T(8,128)S(1)}, f32[6,1,16,128]{3,2,1,0:T(8,128)S(1)}, u32[]{:S(2)}, u32[]{:S(2)}) collective-permute-start(f32[6,1,16,128]{3,2,1,0:T(8,128)S(1)} %get-tuple-element.26), channel_id=1, source_target_pairs={{1,0},{2,1},{3,2},{4,3},{5,4},{6,5},{7,6},{8,7},{9,8},{10,9},{11,1... | collective-permute-start | bytes 147464 | tf_op jit(solution)/shard_map/ppermute | solution.py:22
  120.1 2.4 %collective-permute-start.9 = (f32[6,1,16,128]{3,2,1,0:T(8,128)S(1)}, f32[6,1,16,128]{3,2,1,0:T(8,128)S(1)}, u32[]{:S(2)}, u32[]{:S(2)}) collective-permute-start(f32[6,1,16,128]{3,2,1,0:T(8,128)S(1)} %get-tuple-element.27), channel_id=1, source_target_pairs={{0,1},{1,2},{2,3},{3,4},{4,5},{5,6},{6,7},{7,8},{8,9},{9,10},{10,1... | collective-permute-start | bytes 147464 | tf_op jit(solution)/shard_map/ppermute | solution.py:20
  122.6 6.3 %collective-permute-done.9 = f32[6,1,16,128]{3,2,1,0:T(8,128)S(1)} collective-permute-done((f32[6,1,16,128]{3,2,1,0:T(8,128)S(1)}, f32[6,1,16,128]{3,2,1,0:T(8,128)S(1)}, u32[]{:S(2)}, u32[]{:S(2)}) %collective-permute-start.9) | collective-permute-done | bytes 49184 | tf_op jit(solution)/shard_map/ppermute | solution.py:20
  128.9 0.2 fusion.33
  129.0 0.1 multiply_divide_fusion.5
  129.2 1.9 %collective-permute-start.10 = (f32[6,1,16,128]{3,2,1,0:T(8,128)S(1)}, f32[6,1,16,128]{3,2,1,0:T(8,128)S(1)}, u32[]{:S(2)}, u32[]{:S(2)}) collective-permute-start(f32[6,1,16,128]{3,2,1,0:T(8,128)S(1)} %get-tuple-element.24), channel_id=1, source_target_pairs={{1,0},{2,1},{3,2},{4,3},{5,4},{6,5},{7,6},{8,7},{9,8},{10,9},{11,1... | collective-permute-start | bytes 147464 | tf_op jit(solution)/shard_map/ppermute | solution.py:22
  131.1 2.4 %collective-permute-start.11 = (f32[6,1,16,128]{3,2,1,0:T(8,128)S(1)}, f32[6,1,16,128]{3,2,1,0:T(8,128)S(1)}, u32[]{:S(2)}, u32[]{:S(2)}) collective-permute-start(f32[6,1,16,128]{3,2,1,0:T(8,128)S(1)} %get-tuple-element.25), channel_id=1, source_target_pairs={{0,1},{1,2},{2,3},{3,4},{4,5},{5,6},{6,7},{7,8},{8,9},{9,10},{10,1... | collective-permute-start | bytes 147464 | tf_op jit(solution)/shard_map/ppermute | solution.py:20
  133.5 6.3 %collective-permute-done.11 = f32[6,1,16,128]{3,2,1,0:T(8,128)S(1)} collective-permute-done((f32[6,1,16,128]{3,2,1,0:T(8,128)S(1)}, f32[6,1,16,128]{3,2,1,0:T(8,128)S(1)}, u32[]{:S(2)}, u32[]{:S(2)}) %collective-permute-start.11) | collective-permute-done | bytes 49184 | tf_op jit(solution)/shard_map/ppermute | solution.py:20
  139.8 0.2 fusion.38
  140.0 0.1 multiply_divide_fusion.3
  140.1 1.9 %collective-permute-start.12 = (f32[6,1,16,128]{3,2,1,0:T(8,128)S(1)}, f32[6,1,16,128]{3,2,1,0:T(8,128)S(1)}, u32[]{:S(2)}, u32[]{:S(2)}) collective-permute-start(f32[6,1,16,128]{3,2,1,0:T(8,128)S(1)} %get-tuple-element.22), channel_id=1, source_target_pairs={{1,0},{2,1},{3,2},{4,3},{5,4},{6,5},{7,6},{8,7},{9,8},{10,9},{11,1... | collective-permute-start | bytes 147464 | tf_op jit(solution)/shard_map/ppermute | solution.py:22
  142.0 2.4 %collective-permute-start.13 = (f32[6,1,16,128]{3,2,1,0:T(8,128)S(1)}, f32[6,1,16,128]{3,2,1,0:T(8,128)S(1)}, u32[]{:S(2)}, u32[]{:S(2)}) collective-permute-start(f32[6,1,16,128]{3,2,1,0:T(8,128)S(1)} %get-tuple-element.23), channel_id=1, source_target_pairs={{0,1},{1,2},{2,3},{3,4},{4,5},{5,6},{6,7},{7,8},{8,9},{9,10},{10,1... | collective-permute-start | bytes 147464 | tf_op jit(solution)/shard_map/ppermute | solution.py:20
  144.5 0.7 fusion.51
  145.2 5.6 %collective-permute-done.13 = f32[6,1,16,128]{3,2,1,0:T(8,128)S(1)} collective-permute-done((f32[6,1,16,128]{3,2,1,0:T(8,128)S(1)}, f32[6,1,16,128]{3,2,1,0:T(8,128)S(1)}, u32[]{:S(2)}, u32[]{:S(2)}) %collective-permute-start.13) | collective-permute-done | bytes 49184 | tf_op jit(solution)/shard_map/ppermute | solution.py:20
  150.8 0.2 fusion.43
  151.1 31.0 %psum.7 = f32[4,16,128]{2,1,0:T(8,128)} all-reduce(f32[4,16,128]{2,1,0:T(8,128)S(1)} %broadcast_multiply_fusion.1), channel_id=1, replica_groups=mesh['freq'=8,'tile'=64] {'freq'}, use_global_device_ids=true, to_apply=%region_2.3 | all-reduce | flops 8192 | bytes 65536 | tf_op jit(solution)/shard_map/psum | solution.py:73
  (33 shorter events, 0.5 us)
Async XLA Ops:
  0.6 71.4 %copy-start = (f32[6,4,16,128]{3,2,1,0:T(8,128)S(1)}, f32[6,4,16,128]{3,2,1,0:T(8,128)}, u32[]{:S(2)}) copy-start(f32[6,4,16,128]{3,2,1,0:T(8,128)} %param.6) | copy-start | bytes 589828
  0.7 56.9 %collective-permute-start.1 = (f32[6,1,16,128]{3,2,1,0:T(8,128)S(1)}, f32[6,1,16,128]{3,2,1,0:T(8,128)S(1)}, u32[]{:S(2)}, u32[]{:S(2)}) collective-permute-start(f32[6,1,16,128]{3,2,1,0:T(8,128)S(1)} %broadcast.81), channel_id=1, source_target_pairs={{0,1},{1,2},{2,3},{3,4},{4,5},{5,6},{6,7},{7,8},{8,9},{9,10},{10,1... | collective-permute-start | bytes 147464 | tf_op jit(solution)/shard_map/ppermute | solution.py:20
  2.7 54.8 %collective-permute-start = (f32[6,1,16,128]{3,2,1,0:T(8,128)S(1)}, f32[6,1,16,128]{3,2,1,0:T(8,128)S(1)}, u32[]{:S(2)}, u32[]{:S(2)}) collective-permute-start(f32[6,1,16,128]{3,2,1,0:T(8,128)S(1)} %broadcast.81), channel_id=1, source_target_pairs={{1,0},{2,1},{3,2},{4,3},{5,4},{6,5},{7,6},{8,7},{9,8},{10,9},{11,1... | collective-permute-start | bytes 147464 | tf_op jit(solution)/shard_map/ppermute | solution.py:22
  11.0 12.6 %all-to-all-start.2 = ((s32[64,1,1]{2,1,0:T(1,128)}), s32[64,1,1]{2,1,0:T(1,128)S(1)}, u32[]{:S(2)}, u32[]{:S(2)}) async-start(s32[64,1,1]{2,1,0:T(1,128)} %copy.78), calls=%async_computation.2 | async-start | bytes 65536 | tf_op jit(solution)/shard_map/all_to_all | solution.py:64
  23.6 14.8 %all-to-all-start = ((s32[64,8,1]{1,2,0:T(1,128)}), s32[64,8,1]{1,2,0:T(1,128)S(1)}, u32[]{:S(2)}, u32[]{:S(2)}) async-start(s32[64,8,1]{1,2,0:T(1,128)} %bitcast.9), calls=%async_computation | async-start | bytes 65536 | tf_op jit(solution)/shard_map/all_to_all | solution.py:63
  38.5 18.6 %all-to-all-start.1 = ((f32[6,64,8]{2,0,1:T(8,128)}), f32[6,64,8]{2,0,1:T(8,128)S(1)}, u32[]{:S(2)}, u32[]{:S(2)}) async-start(f32[6,64,8]{2,0,1:T(8,128)} %copy.76), calls=%async_computation.1 | async-start | bytes 524288 | tf_op jit(solution)/shard_map/all_to_all | solution.py:61
  58.8 6.5 %collective-permute-start.2 = (f32[6,1,16,128]{3,2,1,0:T(8,128)S(1)}, f32[6,1,16,128]{3,2,1,0:T(8,128)S(1)}, u32[]{:S(2)}, u32[]{:S(2)}) collective-permute-start(f32[6,1,16,128]{3,2,1,0:T(8,128)S(1)} %get-tuple-element.32), channel_id=1, source_target_pairs={{1,0},{2,1},{3,2},{4,3},{5,4},{6,5},{7,6},{8,7},{9,8},{10,9},{11,1... | collective-permute-start | bytes 147464 | tf_op jit(solution)/shard_map/ppermute | solution.py:22
  63.2 8.7 %collective-permute-start.3 = (f32[6,1,16,128]{3,2,1,0:T(8,128)S(1)}, f32[6,1,16,128]{3,2,1,0:T(8,128)S(1)}, u32[]{:S(2)}, u32[]{:S(2)}) collective-permute-start(f32[6,1,16,128]{3,2,1,0:T(8,128)S(1)} %get-tuple-element.33), channel_id=1, source_target_pairs={{0,1},{1,2},{2,3},{3,4},{4,5},{5,6},{6,7},{7,8},{8,9},{9,10},{10,1... | collective-permute-start | bytes 147464 | tf_op jit(solution)/shard_map/ppermute | solution.py:20
  72.2 4.5 %collective-permute-start.4 = (f32[6,1,16,128]{3,2,1,0:T(8,128)S(1)}, f32[6,1,16,128]{3,2,1,0:T(8,128)S(1)}, u32[]{:S(2)}, u32[]{:S(2)}) collective-permute-start(f32[6,1,16,128]{3,2,1,0:T(8,128)S(1)} %get-tuple-element.30), channel_id=1, source_target_pairs={{1,0},{2,1},{3,2},{4,3},{5,4},{6,5},{7,6},{8,7},{9,8},{10,9},{11,1... | collective-permute-start | bytes 147464 | tf_op jit(solution)/shard_map/ppermute | solution.py:22
  74.1 8.7 %collective-permute-start.5 = (f32[6,1,16,128]{3,2,1,0:T(8,128)S(1)}, f32[6,1,16,128]{3,2,1,0:T(8,128)S(1)}, u32[]{:S(2)}, u32[]{:S(2)}) collective-permute-start(f32[6,1,16,128]{3,2,1,0:T(8,128)S(1)} %get-tuple-element.31), channel_id=1, source_target_pairs={{0,1},{1,2},{2,3},{3,4},{4,5},{5,6},{6,7},{7,8},{8,9},{9,10},{10,1... | collective-permute-start | bytes 147464 | tf_op jit(solution)/shard_map/ppermute | solution.py:20
  83.2 4.5 %collective-permute-start.6 = (f32[6,1,16,128]{3,2,1,0:T(8,128)S(1)}, f32[6,1,16,128]{3,2,1,0:T(8,128)S(1)}, u32[]{:S(2)}, u32[]{:S(2)}) collective-permute-start(f32[6,1,16,128]{3,2,1,0:T(8,128)S(1)} %get-tuple-element.28), channel_id=1, source_target_pairs={{1,0},{2,1},{3,2},{4,3},{5,4},{6,5},{7,6},{8,7},{9,8},{10,9},{11,1... | collective-permute-start | bytes 147464 | tf_op jit(solution)/shard_map/ppermute | solution.py:22
  85.1 8.7 %collective-permute-start.7 = (f32[6,1,16,128]{3,2,1,0:T(8,128)S(1)}, f32[6,1,16,128]{3,2,1,0:T(8,128)S(1)}, u32[]{:S(2)}, u32[]{:S(2)}) collective-permute-start(f32[6,1,16,128]{3,2,1,0:T(8,128)S(1)} %get-tuple-element.29), channel_id=1, source_target_pairs={{0,1},{1,2},{2,3},{3,4},{4,5},{5,6},{6,7},{7,8},{8,9},{9,10},{10,1... | collective-permute-start | bytes 147464 | tf_op jit(solution)/shard_map/ppermute | solution.py:20
  118.2 4.4 %collective-permute-start.8 = (f32[6,1,16,128]{3,2,1,0:T(8,128)S(1)}, f32[6,1,16,128]{3,2,1,0:T(8,128)S(1)}, u32[]{:S(2)}, u32[]{:S(2)}) collective-permute-start(f32[6,1,16,128]{3,2,1,0:T(8,128)S(1)} %get-tuple-element.26), channel_id=1, source_target_pairs={{1,0},{2,1},{3,2},{4,3},{5,4},{6,5},{7,6},{8,7},{9,8},{10,9},{11,1... | collective-permute-start | bytes 147464 | tf_op jit(solution)/shard_map/ppermute | solution.py:22
  120.1 8.7 %collective-permute-start.9 = (f32[6,1,16,128]{3,2,1,0:T(8,128)S(1)}, f32[6,1,16,128]{3,2,1,0:T(8,128)S(1)}, u32[]{:S(2)}, u32[]{:S(2)}) collective-permute-start(f32[6,1,16,128]{3,2,1,0:T(8,128)S(1)} %get-tuple-element.27), channel_id=1, source_target_pairs={{0,1},{1,2},{2,3},{3,4},{4,5},{5,6},{6,7},{7,8},{8,9},{9,10},{10,1... | collective-permute-start | bytes 147464 | tf_op jit(solution)/shard_map/ppermute | solution.py:20
  129.2 4.4 %collective-permute-start.10 = (f32[6,1,16,128]{3,2,1,0:T(8,128)S(1)}, f32[6,1,16,128]{3,2,1,0:T(8,128)S(1)}, u32[]{:S(2)}, u32[]{:S(2)}) collective-permute-start(f32[6,1,16,128]{3,2,1,0:T(8,128)S(1)} %get-tuple-element.24), channel_id=1, source_target_pairs={{1,0},{2,1},{3,2},{4,3},{5,4},{6,5},{7,6},{8,7},{9,8},{10,9},{11,1... | collective-permute-start | bytes 147464 | tf_op jit(solution)/shard_map/ppermute | solution.py:22
  131.1 8.7 %collective-permute-start.11 = (f32[6,1,16,128]{3,2,1,0:T(8,128)S(1)}, f32[6,1,16,128]{3,2,1,0:T(8,128)S(1)}, u32[]{:S(2)}, u32[]{:S(2)}) collective-permute-start(f32[6,1,16,128]{3,2,1,0:T(8,128)S(1)} %get-tuple-element.25), channel_id=1, source_target_pairs={{0,1},{1,2},{2,3},{3,4},{4,5},{5,6},{6,7},{7,8},{8,9},{9,10},{10,1... | collective-permute-start | bytes 147464 | tf_op jit(solution)/shard_map/ppermute | solution.py:20
  140.1 5.1 %collective-permute-start.12 = (f32[6,1,16,128]{3,2,1,0:T(8,128)S(1)}, f32[6,1,16,128]{3,2,1,0:T(8,128)S(1)}, u32[]{:S(2)}, u32[]{:S(2)}) collective-permute-start(f32[6,1,16,128]{3,2,1,0:T(8,128)S(1)} %get-tuple-element.22), channel_id=1, source_target_pairs={{1,0},{2,1},{3,2},{4,3},{5,4},{6,5},{7,6},{8,7},{9,8},{10,9},{11,1... | collective-permute-start | bytes 147464 | tf_op jit(solution)/shard_map/ppermute | solution.py:22
  142.0 8.7 %collective-permute-start.13 = (f32[6,1,16,128]{3,2,1,0:T(8,128)S(1)}, f32[6,1,16,128]{3,2,1,0:T(8,128)S(1)}, u32[]{:S(2)}, u32[]{:S(2)}) collective-permute-start(f32[6,1,16,128]{3,2,1,0:T(8,128)S(1)} %get-tuple-element.23), channel_id=1, source_target_pairs={{0,1},{1,2},{2,3},{3,4},{4,5},{5,6},{6,7},{7,8},{8,9},{9,10},{10,1... | collective-permute-start | bytes 147464 | tf_op jit(solution)/shard_map/ppermute | solution.py:20
where the time goes:
time: 183 us; the launch traced here: 182 us
  starting transfers between devices  64.3 us (35%)
  waiting for transfers between devices  48.5 us (27%)
  blocking collectives  31 us (17%)
  local copies, waits for them, and re-layouts  21.7 us (12%)
  other arithmetic  14.8 us (8%)
    ppermute x7, waiting for transfers between devices, extended(): lax.ppermute(tail, axis, [(i, (i + 1) % count) for i in range(ends)])  37.1 us
    psum x1, blocking collectives, body(): gradient = lax.psum(term, 'freq')  31 us
    ppermute x7, starting transfers between devices, extended(): lax.ppermute(head, axis, [((i + 1) % count, i) for i in range(ends)])  21 us
    ppermute x7, starting transfers between devices, extended(): lax.ppermute(tail, axis, [(i, (i + 1) % count) for i in range(ends)])  16 us
    slice x2, local copies, waits for them, and re-layouts, relax(): resid_im = source[3:] - applied_im  10.7 us
    all_to_all x1, starting transfers between devices, body(): lax.all_to_all(slot_cells, 'tile', split_axis=0, concat_axis=0, tiled=True)  10.1 us
    all_to_all x1, starting transfers between devices, body(): lax.all_to_all(observed[0], 'tile', split_axis=1, concat_axis=1, tiled=True)  9.41 us
    all_to_all x1, waiting for transfers between devices, body(): lax.all_to_all(observed[0], 'tile', split_axis=1, concat_axis=1, tiled=True)  7.87 us
  transfers between devices with their start and end apart: 17, of which 9 were waited for; matrix products, arithmetic and copies ran while one was open for 4% of the time, Pallas kernels for 0%

commit v1 on v0

v1 whole, which is shorter than its diff:
```python
import jax
import jax.numpy as jnp
from jax import lax
from jax.experimental import pallas as pl
from jax.experimental.pallas import tpu as pltpu
from jax.sharding import PartitionSpec as P

SWEEPS = 4
DAMPING = 0.8
HALO = SWEEPS - 1
ROWS = 8
LANES = 128

VMEM = pl.BlockSpec(memory_space=pltpu.VMEM)
SMEM = pl.BlockSpec(memory_space=pltpu.SMEM)


def pack_kernel(source, cond, observed, cells, counts, to_right, to_left, payload, values, columns):
    depth = cond.shape[0]
    for out, first in ((to_right, depth - HALO), (to_left, 0)):
        out[:6] = source[:, first:first + HALO]
        out[6] = cond[first:first + HALO]
    tiles = counts.shape[1]
    slots = cells.shape[1]
    cap = slots // tiles
    values[0:6] = observed[0]
    values[6:7] = cells[...].astype(jnp.float32)
    owner = lax.broadcasted_iota(jnp.int32, (tiles, slots), 1) // cap
    spread = (owner == lax.broadcasted_iota(jnp.int32, (tiles, slots), 0)).astype(jnp.bfloat16)
    count = jnp.broadcast_to(counts[...].astype(jnp.float32), (8, tiles)).astype(jnp.bfloat16)
    repeated = lax.dot_general(count, spread, (((1,), (0,)), ((), ())), preferred_element_type=jnp.float32)
    within = lax.broadcasted_iota(jnp.int32, (8, slots), 1) % cap
    live = (within.astype(jnp.float32) < repeated).astype(jnp.float32)
    values[7:8] = live[7:8]
    columns[...] = jnp.zeros_like(columns)
    for part in range(slots // LANES):
        turned = values[:, part * LANES:(part + 1) * LANES].T
        columns[cap + part * LANES:cap + (part + 1) * LANES, 0:ROWS] = turned
    planes = [jnp.zeros((tiles, LANES), jnp.float32), jnp.zeros((tiles, LANES), jnp.float32)]
    for group in range(3):
        for slot in range(cap):
            piece = columns[pl.ds(group * cap + slot, tiles, stride=cap), :]
            shift = (group % 2) * 64 + slot * ROWS
            planes[group // 2] += pltpu.roll(piece, shift, 1) if shift else piece
    for plane in range(2):
        payload[:, plane, :] = planes[plane]


def spread_kernel(received, out, left, right):
    tiles = received.shape[0]
    turned = []
    for plane in range(2):
        here = received[:, plane, :]
        turned.append(jnp.concatenate([here, pltpu.roll(here, LANES - ROWS, 1)], axis=0).T)
    layer = out.shape[2]
    depth = out.shape[1] - 2 * HALO
    plan = (
        ((depth - HALO) * layer, HALO * layer, 0),
        (0, depth * layer, HALO),
        (0, HALO * layer, HALO + depth),
    )
    for group, (first, rows, where) in enumerate(plan):
        base = (group % 2) * 64
        record = jnp.concatenate(
            [turned[group // 2][base + 16 * j:base + 16 * j + ROWS] for j in range(4)], axis=1
        )
        slots = record.shape[1]
        alive = record[7:8]
        cell = record[6:7].astype(jnp.int32)
        value = jnp.where(alive > 0.0, record, 0.0)
        high = value.astype(jnp.bfloat16).astype(jnp.float32)
        rest = value - high
        middle = rest.astype(jnp.bfloat16).astype(jnp.float32)
        low = rest - middle
        row = lax.broadcasted_iota(jnp.int32, (rows, slots), 0) + first
        hit = row == (cell >> 7)
        place = 0
        for terms, names in ((high, (0, 1, 2, 3, 4, 5, 7)), (middle, range(6)), (low, range(6))):
            for name in names:
                left[place:place + rows] = jnp.where(hit, terms[name:name + 1], 0.0).astype(jnp.bfloat16)
                place += rows
        lane = lax.broadcasted_iota(jnp.int32, (LANES, slots), 0) == (cell & (LANES - 1))
        right[...] = lane.astype(jnp.float32).astype(jnp.bfloat16)
        sums = lax.dot_general(
            left[:place], right[...], (((1,), (1,)), ((), ())), preferred_element_type=jnp.float32
        )
        for name in range(6):
            total = sums[name * rows:(name + 1) * rows]
            total = total + sums[(7 + name) * rows:(8 + name) * rows]
            total = total + sums[(13 + name) * rows:(14 + name) * rows]
            out[name, where:where + rows // layer] = total.reshape(rows // layer, layer, LANES)
        out[6, where:where + rows // layer] = sums[6 * rows:7 * rows].reshape(rows // layer, layer, LANES)


PITCH = 24


def clear(buffer, layers):
    for part in range(6):
        for layer in range(layers + 1):
            buffer[part, layer * PITCH:layer * PITCH + 8] = jnp.zeros((8, LANES), jnp.float32)


def coefficients(factor, cond, hl, hr, pq, depth):
    tile = lax.axis_index("tile")
    last = lax.axis_size("tile") - 1
    layers = depth + 2 * HALO
    for layer in range(layers):
        if layer < HALO:
            sigma, scale = hl[6, layer], jnp.where(tile > 0, DAMPING, 0.0)
        elif layer < HALO + depth:
            sigma, scale = cond[layer - HALO], DAMPING
        else:
            sigma, scale = hr[6, layer - HALO - depth], jnp.where(tile < last, DAMPING, 0.0)
        absorb = factor * sigma
        weight = scale / (36.0 + absorb * absorb)
        pq[0, layer] = 6.0 * weight
        pq[1, layer] = absorb * weight


def first_sweep(src, pq, dst, layers):
    def step(layer, carry):
        at = pl.ds(pl.multiple_of(layer * PITCH + 8, 8), 16)
        p, q = pq[0, layer], pq[1, layer]
        for part in range(3):
            re, im = src[part, layer], src[part + 3, layer]
            dst[part, at] = p * re + q * im
            dst[part + 3, at] = p * im - q * re
        return carry

    lax.fori_loop(0, layers, step, 0, unroll=2)


def sweep(src, pq, old, new, lo, hi, unroll, emit=None):
    lane = lax.broadcasted_iota(jnp.int32, (16, LANES), 1)
    not_first, not_last = lane > 0, lane < LANES - 1

    def neighbours(part, base):
        middle = old[part, pl.ds(base, 16)]
        beside = old[part, pl.ds(base - PITCH, 16)] + old[part, pl.ds(base + PITCH, 16)]
        beside = beside + (old[part, pl.ds(base - 1, 16)] + old[part, pl.ds(base + 1, 16)])
        beside = beside + jnp.where(not_first, pltpu.roll(middle, 1, 1), 0.0)
        beside = beside + jnp.where(not_last, pltpu.roll(middle, LANES - 1, 1), 0.0)
        return middle, beside

    def step(layer, carry):
        base = layer * PITCH + 8
        p, q = pq[0, layer], pq[1, layer]
        results = []
        for part in range(3):
            mid_re, sum_re = neighbours(part, base)
            mid_im, sum_im = neighbours(part + 3, base)
            sum_re = sum_re + src[part, layer]
            sum_im = sum_im + src[part + 3, layer]
            new_re = (1.0 - DAMPING) * mid_re + (p * sum_re + q * sum_im)
            new_im = (1.0 - DAMPING) * mid_im + (p * sum_im - q * sum_re)
            if emit is None:
                at = pl.ds(pl.multiple_of(base, 8), 16)
                new[part, at] = new_re
                new[part + 3, at] = new_im
            results.append((new_re, new_im))
        if emit is not None:
            emit(layer, results)
        return carry

    lax.fori_loop(lo, hi, step, 0, unroll=unroll)


def relax(src, pq, one, two, depth, emit):
    layers = depth + 2 * HALO
    clear(one, layers)
    clear(two, layers)
    first_sweep(src, pq, one, layers)
    old, new = one, two
    for index in range(1, SWEEPS):
        final = index == SWEEPS - 1
        sweep(src, pq, old, new, index, layers - index, 2, emit if final else None)
        old, new = new, old


def forward_kernel(factor, source, cond, hl, hr, field, to_right, to_left, src, pq, one, two):
    depth = cond.shape[0]
    coefficients(factor[0], cond, hl, hr, pq, depth)
    src[:, 0:HALO] = hl[:6]
    src[:, HALO:HALO + depth] = source[...]
    src[:, HALO + depth:] = hr[:6]

    def emit(layer, results):
        for part, (re, im) in enumerate(results):
            field[0, part, layer - HALO] = re
            field[0, part + 3, layer - HALO] = im

    relax(src, pq, one, two, depth, emit)
    to_right[...] = field[0, :, depth - HALO:]
    to_left[...] = field[0, :, 0:HALO]


def adjoint_kernel(factor, sums, cond, hl, hr, field, fl, fr, terms, src, pq, one, two):
    depth = cond.shape[0]
    coefficients(factor[0], cond, hl, hr, pq, depth)
    for part in range(6):
        src[part, 0:HALO] = sums[6, 0:HALO] * fl[part] - sums[part, 0:HALO]
        own = slice(HALO, HALO + depth)
        src[part, own] = sums[6, own] * field[0, part] - sums[part, own]
        src[part, HALO + depth:] = sums[6, HALO + depth:] * fr[part] - sums[part, HALO + depth:]

    def emit(layer, results):
        at = layer - HALO
        total = 0.0
        for part, (re, im) in enumerate(results):
            total = total + (re * field[0, part + 3, at] + im * field[0, part, at])
        total = factor[0] * total
        rows = pl.ds(pl.multiple_of(at * 16, 16), 16)
        for copy in range(terms.shape[0]):
            terms[copy, rows] = total

    relax(src, pq, one, two, depth, emit)


def working(depth):
    layers = depth + 2 * HALO
    buffer = pltpu.VMEM((6, layers * PITCH + 8, LANES), jnp.float32)
    return [
        pltpu.VMEM((6, layers, 16, LANES), jnp.float32),
        pltpu.VMEM((2, layers, 16, LANES), jnp.float32),
        buffer,
        buffer,
    ]


def shape(*dims):
    return jax.ShapeDtypeStruct(dims, jnp.float32)


def cost(flops, size):
    return pl.CostEstimate(flops=flops, bytes_accessed=size, transcendentals=0)


def body(source, conductivity, freq_factor, observed, slot_cells, block_counts):
    tiles, freqs = lax.axis_size("tile"), lax.axis_size("freq")
    depth, ny, nz = conductivity.shape
    slots = slot_cells.shape[0]
    to_right, to_left, payload = pl.pallas_call(
        pack_kernel,
        out_shape=(shape(7, HALO, ny, nz), shape(7, HALO, ny, nz), shape(tiles, 2, LANES)),
        in_specs=[VMEM] * 5,
        out_specs=(VMEM, VMEM, VMEM),
        scratch_shapes=[
            pltpu.VMEM((ROWS, slots), jnp.float32),
            pltpu.VMEM((slots + 2 * (slots // tiles), LANES), jnp.float32),
        ],
        cost_estimate=cost(10**6, 10**6),
        name="pack",
    )(source, conductivity, observed, slot_cells.reshape(1, -1), block_counts.reshape(1, -1))
    rightward = [(i, i + 1) for i in range(tiles - 1)]
    leftward = [(i + 1, i) for i in range(tiles - 1)]
    hl = lax.ppermute(to_right, "tile", rightward)
    hr = lax.ppermute(to_left, "tile", leftward)
    received = lax.all_to_all(payload, "tile", split_axis=0, concat_axis=0, tiled=True)
    field, to_right, to_left = pl.pallas_call(
        forward_kernel,
        out_shape=(shape(1, 6, depth, ny, nz), shape(6, HALO, ny, nz), shape(6, HALO, ny, nz)),
        in_specs=[SMEM] + [VMEM] * 4,
        out_specs=(VMEM, VMEM, VMEM),
        scratch_shapes=working(depth),
        cost_estimate=cost(10**7, 10**6),
        name="forward",
    )(freq_factor, source, conductivity, hl, hr)
    fl = lax.ppermute(to_right, "tile", rightward)
    fr = lax.ppermute(to_left, "tile", leftward)
    layers = depth + 2 * HALO
    sums = pl.pallas_call(
        spread_kernel,
        out_shape=shape(7, layers, ny, nz),
        in_specs=[VMEM],
        out_specs=VMEM,
        scratch_shapes=[
            pltpu.VMEM((19 * depth * ny, slots), jnp.bfloat16),
            pltpu.VMEM((LANES, slots), jnp.bfloat16),
        ],
        cost_estimate=cost(10**7, 10**6),
        name="spread",
    )(received)
    terms = pl.pallas_call(
        adjoint_kernel,
        out_shape=shape(freqs, depth * ny, nz),
        in_specs=[SMEM] + [VMEM] * 7,
        out_specs=VMEM,
        scratch_shapes=working(depth),
        cost_estimate=cost(10**7, 10**6),
        name="adjoint",
    )(freq_factor, sums, conductivity, hl, hr, field, fl, fr)
    terms = lax.all_to_all(terms, "freq", split_axis=0, concat_axis=0, tiled=True)
    gradient = jnp.sum(terms, axis=0).reshape(depth, ny, nz)
    return (field, gradient)


def solution(mesh):
    in_specs = (
        P(None, "tile", None, None),
        P("tile", None, None),
        P("freq"),
        P("freq", None, "tile"),
        P("tile"),
        P("tile"),
    )
    out_specs = (P("freq", None, "tile", None, None), P("tile", None, None))
    return jax.shard_map(body, mesh=mesh, in_specs=in_specs, out_specs=out_specs, check_vma=False)
```

time: 183 us -> 77.2 us (0.42)
  the two profiles are of different devices: /device:TPU:256 before, /device:TPU:1 now
where the time goes in v1:
time: 77.2 us; the launch traced here: 76.8 us
  blocking collectives  45.4 us (59%)
  starting transfers between devices  14.4 us (19%)
  Pallas kernels  11.6 us (15%)
  local copies, waits for them, and re-layouts  2.72 us (4%)
  between operations  1.36 us (2%)
    all_to_all x1, blocking collectives, body(): lax.all_to_all(payload, 'tile', split_axis=0, concat_axis=0, tiled=True)  27.6 us
    all_to_all x1, blocking collectives, body(): lax.all_to_all(terms, 'freq', split_axis=0, concat_axis=0, tiled=True)  17.8 us
    ppermute x1, starting transfers between devices, body(): hr = lax.ppermute(to_left, 'tile', leftward)  5.58 us
    ppermute x1, starting transfers between devices, body(): hl = lax.ppermute(to_right, 'tile', rightward)  4.5 us
    pallas_call x1, Pallas kernels, body(): pl.pallas_call(adjoint_kernel, out_shape=shape(freqs, depth * ny, nz), in...  3.42 us
    pallas_call x1, Pallas kernels, body(): pl.pallas_call(forward_kernel, out_shape=(shape(1, 6, depth, ny, nz), sha...  3.2 us
    pallas_call x1, Pallas kernels, body(): pl.pallas_call(spread_kernel, out_shape=shape(7, layers, ny, nz), in_spec...  2.75 us
    unnamed x11, local copies, waits for them, and re-layouts  2.72 us
  transfers between devices with their start and end apart: 4, of which 1 were waited for; matrix products, arithmetic and copies ran while one was open for 0% of the time, Pallas kernels for 4%

profile of v1, /device:TPU:1, one launch (start us, length us, event | category | flops | bytes accessed | tf_op | source)
XLA Modules:
  0.0 76.8 jit_solution(13753154414986989645)
XLA Ops:
  0.6 1.3 %copy.8.observed = f32[1,6,512]{2,1,0:T(8,128)} copy(f32[1,6,512]{2,0,1:T(1,128)} %param.9) | data formatting | bytes 24576 | tf_op args[3]
  1.9 2.2 %pack.1 = (f32[7,3,16,128]{3,2,1,0:T(8,128)}, f32[7,3,16,128]{3,2,1,0:T(8,128)}, f32[64,2,128]{2,1,0:T(2,128)}) custom-call(f32[6,4,16,128]{3,2,1,0:T(8,128)} %source.3, f32[4,16,128]{2,1,0:T(8,128)} %cond.5, f32[1,6,512]{2,1,0:T(8,128)} %copy.8.observed, s32[1,512]{1,0:T(1,128)} %bitcast.4, s32[1,64]{1,0:T(1,128)} %bitcast.5), custom_call_target="tpu_custom_call" | custom-call | flops 1000000 | bytes 1000000 | tf_op jit(solution)/shard_map/pack/pallas_call | solution.py:243
  4.2 4.5 %collective-permute-start = (f32[7,3,16,128]{3,2,1,0:T(8,128)}, f32[7,3,16,128]{3,2,1,0:T(8,128)S(1)}, u32[]{:S(2)}, u32[]{:S(2)}) collective-permute-start(f32[7,3,16,128]{3,2,1,0:T(8,128)} %get-tuple-element.8), channel_id=1, source_target_pairs={{0,1},{1,2},{2,3},{3,4},{4,5},{5,6},{6,7},{7,8},{8,9},{9,10},{10,1... | collective-permute-start | bytes 516104 | tf_op jit(solution)/shard_map/ppermute | solution.py:257
  8.7 5.6 %collective-permute-start.1 = (f32[7,3,16,128]{3,2,1,0:T(8,128)}, f32[7,3,16,128]{3,2,1,0:T(8,128)S(1)}, u32[]{:S(2)}, u32[]{:S(2)}) collective-permute-start(f32[7,3,16,128]{3,2,1,0:T(8,128)} %get-tuple-element.9), channel_id=1, source_target_pairs={{1,0},{2,1},{3,2},{4,3},{5,4},{6,5},{7,6},{8,7},{9,8},{10,9},{11,1... | collective-permute-start | bytes 516104 | tf_op jit(solution)/shard_map/ppermute | solution.py:258
  14.9 0.0 copy-start.4
  14.9 0.0 collective-permute-done.hl
  14.9 0.0 copy-start
  14.9 0.7 collective-permute-done.1.hr
  15.6 0.0 copy-done
  15.6 0.0 copy-start.1
  15.6 0.7 copy-done.1
  16.3 3.2 %forward.1 = (f32[1,6,4,16,128]{4,3,2,1,0:T(8,128)}, f32[6,3,16,128]{3,2,1,0:T(8,128)}, f32[6,3,16,128]{3,2,1,0:T(8,128)}) custom-call(f32[1]{0:T(128)S(6)} %copy.9.factor, f32[6,4,16,128]{3,2,1,0:T(8,128)} %source.3, f32[4,16,128]{2,1,0:T(8,128)} %cond.5, f32[7,3,16,128]{3,2,1,0:T(8,128)} %copy-done, f32[7,3,16,128]{3,2,1,0:T(8,128)} %copy-done.1), custom_call_target="tpu_custom_call" | custom-call | flops 10000000 | bytes 1000000 | tf_op jit(solution)/shard_map/forward/pallas_call | solution.py:260
  19.5 1.9 %collective-permute-start.2 = (f32[6,3,16,128]{3,2,1,0:T(8,128)}, f32[6,3,16,128]{3,2,1,0:T(8,128)S(1)}, u32[]{:S(2)}, u32[]{:S(2)}) collective-permute-start(f32[6,3,16,128]{3,2,1,0:T(8,128)} %get-tuple-element.12), channel_id=1, source_target_pairs={{0,1},{1,2},{2,3},{3,4},{4,5},{5,6},{6,7},{7,8},{8,9},{9,10},{10,1... | collective-permute-start | bytes 442376 | tf_op jit(solution)/shard_map/ppermute | solution.py:269
  21.4 2.4 %collective-permute-start.3 = (f32[6,3,16,128]{3,2,1,0:T(8,128)}, f32[6,3,16,128]{3,2,1,0:T(8,128)S(1)}, u32[]{:S(2)}, u32[]{:S(2)}) collective-permute-start(f32[6,3,16,128]{3,2,1,0:T(8,128)} %get-tuple-element.13), channel_id=1, source_target_pairs={{1,0},{2,1},{3,2},{4,3},{5,4},{6,5},{7,6},{8,7},{9,8},{10,9},{11,1... | collective-permute-start | bytes 442376 | tf_op jit(solution)/shard_map/ppermute | solution.py:270
  23.8 0.0 copy-done.4
  23.8 27.6 %all_to_all.10.received = f32[64,2,128]{2,1,0:T(2,128)} all-to-all(f32[64,2,128]{2,1,0:T(2,128)S(1)} %copy-done.4), channel_id=1, replica_groups=mesh['freq'=8,'tile'=64] {'tile'}, dimensions={0} | all-to-all | bytes 131072 | tf_op jit(solution)/shard_map/all_to_all | solution.py:259
  51.4 2.8 %spread.1.sums = f32[7,10,16,128]{3,2,1,0:T(8,128)} custom-call(f32[64,2,128]{2,1,0:T(2,128)} %all_to_all.10.received), custom_call_target="tpu_custom_call" | custom-call | flops 10000000 | bytes 1000000 | tf_op jit(solution)/shard_map/spread/pallas_call | solution.py:272
  54.2 0.0 collective-permute-done.2.fl
  54.2 0.0 copy-start.2
  54.2 0.0 collective-permute-done.3.fr
  54.2 0.0 copy-start.3
  54.2 0.7 copy-done.2
  54.9 0.1 copy-done.3
  54.9 3.4 %adjoint.1 = f32[8,64,128]{2,1,0:T(8,128)} custom-call(f32[1]{0:T(128)S(6)} %copy.9.factor, f32[7,10,16,128]{3,2,1,0:T(8,128)} %spread.1.sums, f32[4,16,128]{2,1,0:T(8,128)} %cond.5, f32[7,3,16,128]{3,2,1,0:T(8,128)} %copy-done, f32[7,3,16,128]{3,2,1,0:T(8,128)} %copy-done.1, f32[1,6,4,16,128]{4,3,2,1,0:T(8,128)} %get-tuple-element.6.field, ...), custom_call_target="tpu_custom_call" | custom-call | flops 10000000 | bytes 1000000 | tf_op jit(solution)/shard_map/adjoint/pallas_call | solution.py:284
  58.3 17.8 %all_to_all.11 = f32[8,64,128]{2,1,0:T(8,128)S(1)} all-to-all(f32[8,64,128]{2,1,0:T(8,128)} %adjoint.1), channel_id=1, replica_groups=mesh['freq'=8,'tile'=64] {'freq'}, dimensions={0} | all-to-all | bytes 524288 | tf_op jit(solution)/shard_map/all_to_all | solution.py:293
  76.1 0.6 reduce_sum.9
Async XLA Ops:
  4.2 10.7 %collective-permute-start = (f32[7,3,16,128]{3,2,1,0:T(8,128)}, f32[7,3,16,128]{3,2,1,0:T(8,128)S(1)}, u32[]{:S(2)}, u32[]{:S(2)}) collective-permute-start(f32[7,3,16,128]{3,2,1,0:T(8,128)} %get-tuple-element.8), channel_id=1, source_target_pairs={{0,1},{1,2},{2,3},{3,4},{4,5},{5,6},{6,7},{7,8},{8,9},{9,10},{10,1... | collective-permute-start | bytes 516104 | tf_op jit(solution)/shard_map/ppermute | solution.py:257
  8.7 6.9 %collective-permute-start.1 = (f32[7,3,16,128]{3,2,1,0:T(8,128)}, f32[7,3,16,128]{3,2,1,0:T(8,128)S(1)}, u32[]{:S(2)}, u32[]{:S(2)}) collective-permute-start(f32[7,3,16,128]{3,2,1,0:T(8,128)} %get-tuple-element.9), channel_id=1, source_target_pairs={{1,0},{2,1},{3,2},{4,3},{5,4},{6,5},{7,6},{8,7},{9,8},{10,9},{11,1... | collective-permute-start | bytes 516104 | tf_op jit(solution)/shard_map/ppermute | solution.py:258
  14.9 8.9 %copy-start.4 = (f32[64,2,128]{2,1,0:T(2,128)S(1)}, f32[64,2,128]{2,1,0:T(2,128)}, u32[]{:S(2)}) copy-start(f32[64,2,128]{2,1,0:T(2,128)} %get-tuple-element.11) | copy-start | bytes 196612
  14.9 0.7 copy-start
  15.6 0.7 copy-start.1
  19.5 34.7 %collective-permute-start.2 = (f32[6,3,16,128]{3,2,1,0:T(8,128)}, f32[6,3,16,128]{3,2,1,0:T(8,128)S(1)}, u32[]{:S(2)}, u32[]{:S(2)}) collective-permute-start(f32[6,3,16,128]{3,2,1,0:T(8,128)} %get-tuple-element.12), channel_id=1, source_target_pairs={{0,1},{1,2},{2,3},{3,4},{4,5},{5,6},{6,7},{7,8},{8,9},{9,10},{10,1... | collective-permute-start | bytes 442376 | tf_op jit(solution)/shard_map/ppermute | solution.py:269
  21.4 32.8 %collective-permute-start.3 = (f32[6,3,16,128]{3,2,1,0:T(8,128)}, f32[6,3,16,128]{3,2,1,0:T(8,128)S(1)}, u32[]{:S(2)}, u32[]{:S(2)}) collective-permute-start(f32[6,3,16,128]{3,2,1,0:T(8,128)} %get-tuple-element.13), channel_id=1, source_target_pairs={{1,0},{2,1},{3,2},{4,3},{5,4},{6,5},{7,6},{8,7},{9,8},{10,9},{11,1... | collective-permute-start | bytes 442376 | tf_op jit(solution)/shard_map/ppermute | solution.py:270
  54.2 0.7 copy-start.2
  54.2 0.7 copy-start.3

commit v2 on v1

--- a/solution.py
+++ b/solution.py
@@ -23,7 +23,8 @@
     tiles = counts.shape[1]
     slots = cells.shape[1]
     cap = slots // tiles
-    values[0:6] = observed[0]
+    for part in range(6):
+        values[part:part + 1] = observed[part]
     values[6:7] = cells[...].astype(jnp.float32)
     owner = lax.broadcasted_iota(jnp.int32, (tiles, slots), 1) // cap
     spread = (owner == lax.broadcasted_iota(jnp.int32, (tiles, slots), 0)).astype(jnp.bfloat16)
@@ -232,6 +233,9 @@
     return jax.ShapeDtypeStruct(dims, jnp.float32)
 
 
+LIMIT = pltpu.CompilerParams(vmem_limit_bytes=16 * 2**20)
+
+
 def cost(flops, size):
     return pl.CostEstimate(flops=flops, bytes_accessed=size, transcendentals=0)
 
@@ -251,7 +255,7 @@
         ],
         cost_estimate=cost(10**6, 10**6),
         name="pack",
-    )(source, conductivity, observed, slot_cells.reshape(1, -1), block_counts.reshape(1, -1))
+    )(source, conductivity, observed.transpose(1, 0, 2), slot_cells.reshape(1, -1), block_counts.reshape(1, -1))
     rightward = [(i, i + 1) for i in range(tiles - 1)]
     leftward = [(i + 1, i) for i in range(tiles - 1)]
     hl = lax.ppermute(to_right, "tile", rightward)
@@ -263,7 +267,8 @@
         in_specs=[SMEM] + [VMEM] * 4,
         out_specs=(VMEM, VMEM, VMEM),
         scratch_shapes=working(depth),
-        cost_estimate=cost(10**7, 10**6),
+        cost_estimate=cost(10**10, 10**9),
+        compiler_params=LIMIT,
         name="forward",
     )(freq_factor, source, conductivity, hl, hr)
     fl = lax.ppermute(to_right, "tile", rightward)
@@ -278,7 +283,8 @@
             pltpu.VMEM((19 * depth * ny, slots), jnp.bfloat16),
             pltpu.VMEM((LANES, slots), jnp.bfloat16),
         ],
-        cost_estimate=cost(10**7, 10**6),
+        cost_estimate=cost(10**10, 10**9),
+        compiler_params=LIMIT,
         name="spread",
     )(received)
     terms = pl.pallas_call(
@@ -288,6 +294,7 @@
         out_specs=VMEM,
         scratch_shapes=working(depth),
         cost_estimate=cost(10**7, 10**6),
+        compiler_params=LIMIT,
         name="adjoint",
     )(freq_factor, sums, conductivity, hl, hr, field, fl, fr)
     terms = lax.all_to_all(terms, "freq", split_axis=0, concat_axis=0, tiled=True)

time: 77.2 us -> 57.8 us (0.75)
  blocking collectives: 45.4 us -> 18.5 us
  starting transfers between devices: 14.4 us -> 26.8 us
  Pallas kernels: 11.6 us -> 6.7 us
  waiting for transfers between devices: 0.68 us -> 3.43 us
  local copies, waits for them, and re-layouts: 2.72 us -> 0.02 us
    all_to_all x1 -> x0, blocking collectives: 27.6 us -> none  [body(): lax.all_to_all(payload, 'tile', split_axis=0, concat_axis=0, tiled=True)]
    all_to_all x0 -> x1, starting transfers between devices: none -> 11.2 us  [body(): lax.all_to_all(payload, 'tile', split_axis=0, concat_axis=0, tiled=True)]
    unnamed x11 -> x6, local copies, waits for them, and re-layouts: 2.72 us -> 0.02 us
    pallas_call x1, Pallas kernels: 3.42 us -> 1.36 us  [body(): pl.pallas_call(adjoint_kernel, out_shape=shape(freqs, depth * ny, nz), in...]
    all_to_all x0 -> x1, waiting for transfers between devices: none -> 1.79 us  [body(): lax.all_to_all(payload, 'tile', split_axis=0, concat_axis=0, tiled=True)]
    pallas_call x1, Pallas kernels: 2.75 us -> 1.09 us  [body(): pl.pallas_call(spread_kernel, out_shape=shape(7, layers, ny, nz), in_spec...]
    ppermute x1, waiting for transfers between devices: 0.01 us -> 1.63 us  [body(): fr = lax.ppermute(to_left, 'tile', leftward)]
    ppermute x1, starting transfers between devices: 1.91 us -> 3.53 us  [body(): fl = lax.ppermute(to_right, 'tile', rightward)]
  transfers between devices with their start and end apart: 4 -> 5, of which waited for: 1 -> 2; matrix products, arithmetic and copies ran while one was open for 0% -> 0% of each run, Pallas kernels for 4% -> 5%
where the time goes in v2:
time: 57.8 us; the launch traced here: 57.4 us
  starting transfers between devices  26.8 us (46%)
  blocking collectives  18.5 us (32%)
  Pallas kernels  6.7 us (12%)
  waiting for transfers between devices  3.43 us (6%)
  between operations  1.4 us (2%)
  other arithmetic  0.63 us (1%)
    all_to_all x1, blocking collectives, body(): lax.all_to_all(terms, 'freq', split_axis=0, concat_axis=0, tiled=True)  18.5 us
    all_to_all x1, starting transfers between devices, body(): lax.all_to_all(payload, 'tile', split_axis=0, concat_axis=0, tiled=True)  11.2 us
    ppermute x1, starting transfers between devices, body(): hr = lax.ppermute(to_left, 'tile', leftward)  5.58 us
    ppermute x1, starting transfers between devices, body(): hl = lax.ppermute(to_right, 'tile', rightward)  4.5 us
    ppermute x1, starting transfers between devices, body(): fl = lax.ppermute(to_right, 'tile', rightward)  3.53 us
    pallas_call x1, Pallas kernels, body(): pl.pallas_call(pack_kernel, out_shape=(shape(7, HALO, ny, nz), shape(7, H...  2.25 us
    ppermute x1, starting transfers between devices, body(): fr = lax.ppermute(to_left, 'tile', leftward)  2.05 us
    pallas_call x1, Pallas kernels, body(): pl.pallas_call(forward_kernel, out_shape=(shape(1, 6, depth, ny, nz), sha...  2 us
  transfers between devices with their start and end apart: 5, of which 2 were waited for; matrix products, arithmetic and copies ran while one was open for 0% of the time, Pallas kernels for 5%

profile of v2, /device:TPU:1, one launch (start us, length us, event | category | flops | bytes accessed | tf_op | source)
XLA Modules:
  0.0 57.4 jit_solution(17766988536327060078)
XLA Ops:
  0.6 0.0 copy-start.1
  0.6 2.3 %pack.1 = (f32[7,3,16,128]{3,2,1,0:T(8,128)}, f32[7,3,16,128]{3,2,1,0:T(8,128)}, f32[64,2,128]{2,1,0:T(2,128)}) custom-call(f32[6,4,16,128]{3,2,1,0:T(8,128)} %source.3, f32[4,16,128]{2,1,0:T(8,128)} %cond.5, f32[6,1,512]{2,1,0:T(1,128)} %bitcast.5, s32[1,512]{1,0:T(1,128)} %bitcast.6, s32[1,64]{1,0:T(1,128)} %bitcast.7), custom_call_target="tpu_custom_call" | custom-call | flops 1000000 | bytes 1000000 | tf_op jit(solution)/shard_map/pack/pallas_call | solution.py:247
  2.9 4.5 %collective-permute-start = (f32[7,3,16,128]{3,2,1,0:T(8,128)}, f32[7,3,16,128]{3,2,1,0:T(8,128)S(1)}, u32[]{:S(2)}, u32[]{:S(2)}) collective-permute-start(f32[7,3,16,128]{3,2,1,0:T(8,128)} %get-tuple-element.8), channel_id=1, source_target_pairs={{0,1},{1,2},{2,3},{3,4},{4,5},{5,6},{6,7},{7,8},{8,9},{9,10},{10,1... | collective-permute-start | bytes 516104 | tf_op jit(solution)/shard_map/ppermute | solution.py:261
  7.4 5.6 %collective-permute-start.1 = (f32[7,3,16,128]{3,2,1,0:T(8,128)}, f32[7,3,16,128]{3,2,1,0:T(8,128)S(1)}, u32[]{:S(2)}, u32[]{:S(2)}) collective-permute-start(f32[7,3,16,128]{3,2,1,0:T(8,128)} %get-tuple-element.9), channel_id=1, source_target_pairs={{1,0},{2,1},{3,2},{4,3},{5,4},{6,5},{7,6},{8,7},{9,8},{10,9},{11,1... | collective-permute-start | bytes 516104 | tf_op jit(solution)/shard_map/ppermute | solution.py:262
  13.0 0.0 copy-start.2
  13.0 11.2 %all-to-all-start = ((f32[64,2,128]{2,1,0:T(2,128)}), f32[64,2,128]{2,1,0:T(2,128)S(1)}, u32[]{:S(2)}, u32[]{:S(2)}) async-start(f32[64,2,128]{2,1,0:T(2,128)} %get-tuple-element.11), calls=%async_computation | async-start | bytes 131072 | tf_op jit(solution)/shard_map/all_to_all | solution.py:263
  24.8 0.0 collective-permute-done.hl
  24.8 0.0 collective-permute-done.1.hr
  24.8 0.0 copy-done.1
  24.8 0.0 copy-done.2
  24.8 2.0 %forward.1 = (f32[1,6,4,16,128]{4,3,2,1,0:T(8,128)}, f32[6,3,16,128]{3,2,1,0:T(8,128)S(1)}, f32[6,3,16,128]{3,2,1,0:T(8,128)S(1)}) custom-call(f32[1]{0:T(128)S(6)} %copy.8.factor, f32[6,4,16,128]{3,2,1,0:T(8,128)S(1)} %copy-done.1, f32[4,16,128]{2,1,0:T(8,128)S(1)} %copy-done.2, f32[7,3,16,128]{3,2,1,0:T(8,128)S(1)} %collective-permute-done.hl, ...), custom_call_target="tpu_custom_call" | custom-call | flops 10000000000 | bytes 1000000000 | tf_op jit(solution)/shard_map/forward/pallas_call | solution.py:264
  26.8 3.5 %collective-permute-start.2 = (f32[6,3,16,128]{3,2,1,0:T(8,128)S(1)}, f32[6,3,16,128]{3,2,1,0:T(8,128)S(1)}, u32[]{:S(2)}, u32[]{:S(2)}) collective-permute-start(f32[6,3,16,128]{3,2,1,0:T(8,128)S(1)} %get-tuple-element.12), channel_id=1, source_target_pairs={{0,1},{1,2},{2,3},{3,4},{4,5},{5,6},{6,7},{7,8},{8,9},{9,10},{10,1... | collective-permute-start | bytes 442376 | tf_op jit(solution)/shard_map/ppermute | solution.py:274
  30.4 0.0 copy-start
  30.4 2.1 %collective-permute-start.3 = (f32[6,3,16,128]{3,2,1,0:T(8,128)S(1)}, f32[6,3,16,128]{3,2,1,0:T(8,128)S(1)}, u32[]{:S(2)}, u32[]{:S(2)}) collective-permute-start(f32[6,3,16,128]{3,2,1,0:T(8,128)S(1)} %get-tuple-element.13), channel_id=1, source_target_pairs={{1,0},{2,1},{3,2},{4,3},{5,4},{6,5},{7,6},{8,7},{9,8},{10,9},{11,1... | collective-permute-start | bytes 442376 | tf_op jit(solution)/shard_map/ppermute | solution.py:275
  32.4 1.8 %all-to-all-done.received = f32[64,2,128]{2,1,0:T(2,128)S(1)} async-done(((f32[64,2,128]{2,1,0:T(2,128)}), f32[64,2,128]{2,1,0:T(2,128)S(1)}, u32[]{:S(2)}, u32[]{:S(2)}) %all-to-all-start) | async-done | bytes 65568 | tf_op jit(solution)/shard_map/all_to_all | solution.py:263
  34.2 1.1 %spread.1.sums = f32[7,10,16,128]{3,2,1,0:T(8,128)S(1)} custom-call(f32[64,2,128]{2,1,0:T(2,128)S(1)} %all-to-all-done.received), custom_call_target="tpu_custom_call" | custom-call | flops 10000000000 | bytes 1000000000 | tf_op jit(solution)/shard_map/spread/pallas_call | solution.py:277
  35.3 0.0 collective-permute-done.2.fl
  35.4 1.6 %collective-permute-done.3.fr = f32[6,3,16,128]{3,2,1,0:T(8,128)S(1)} collective-permute-done((f32[6,3,16,128]{3,2,1,0:T(8,128)S(1)}, f32[6,3,16,128]{3,2,1,0:T(8,128)S(1)}, u32[]{:S(2)}, u32[]{:S(2)}) %collective-permute-start.3) | collective-permute-done | bytes 147488 | tf_op jit(solution)/shard_map/ppermute | solution.py:275
  37.0 0.0 copy-done
  37.0 1.4 %adjoint.1 = f32[8,64,128]{2,1,0:T(8,128)S(1)} custom-call(f32[1]{0:T(128)S(6)} %copy.8.factor, f32[7,10,16,128]{3,2,1,0:T(8,128)S(1)} %spread.1.sums, f32[4,16,128]{2,1,0:T(8,128)S(1)} %copy-done.2, f32[7,3,16,128]{3,2,1,0:T(8,128)S(1)} %collective-permute-done.hl, f32[7,3,16,128]{3,2,1,0:T(8,128)S(1)} %collective-permute-done.1.hr, ...), custom_call_target="tpu_custom_call" | custom-call | flops 10000000 | bytes 1000000 | tf_op jit(solution)/shard_map/adjoint/pallas_call | solution.py:290
  38.4 18.5 %all_to_all.10 = f32[8,64,128]{2,1,0:T(8,128)S(1)} all-to-all(f32[8,64,128]{2,1,0:T(8,128)S(1)} %adjoint.1), channel_id=1, replica_groups=mesh['freq'=8,'tile'=64] {'freq'}, dimensions={0} | all-to-all | bytes 524288 | tf_op jit(solution)/shard_map/all_to_all | solution.py:300
  56.8 0.6 %reduce_sum.9 = f32[64,128]{1,0:T(8,128)} reduce(f32[8,64,128]{2,1,0:T(8,128)S(1)} %all_to_all.10, f32[]{:T(128)} %constant.0.clone.1), dimensions={0}, to_apply=%region_0.0 | reduce | flops 57344 | bytes 294916 | tf_op jit(solution)/shard_map/reduce_sum | solution.py:301
Async XLA Ops:
  0.6 24.2 %copy-start.1 = (f32[6,4,16,128]{3,2,1,0:T(8,128)S(1)}, f32[6,4,16,128]{3,2,1,0:T(8,128)}, u32[]{:S(2)}) copy-start(f32[6,4,16,128]{3,2,1,0:T(8,128)} %source.3) | copy-start | bytes 589828
  2.9 21.9 %collective-permute-start = (f32[7,3,16,128]{3,2,1,0:T(8,128)}, f32[7,3,16,128]{3,2,1,0:T(8,128)S(1)}, u32[]{:S(2)}, u32[]{:S(2)}) collective-permute-start(f32[7,3,16,128]{3,2,1,0:T(8,128)} %get-tuple-element.8), channel_id=1, source_target_pairs={{0,1},{1,2},{2,3},{3,4},{4,5},{5,6},{6,7},{7,8},{8,9},{9,10},{10,1... | collective-permute-start | bytes 516104 | tf_op jit(solution)/shard_map/ppermute | solution.py:261
  7.4 17.4 %collective-permute-start.1 = (f32[7,3,16,128]{3,2,1,0:T(8,128)}, f32[7,3,16,128]{3,2,1,0:T(8,128)S(1)}, u32[]{:S(2)}, u32[]{:S(2)}) collective-permute-start(f32[7,3,16,128]{3,2,1,0:T(8,128)} %get-tuple-element.9), channel_id=1, source_target_pairs={{1,0},{2,1},{3,2},{4,3},{5,4},{6,5},{7,6},{8,7},{9,8},{10,9},{11,1... | collective-permute-start | bytes 516104 | tf_op jit(solution)/shard_map/ppermute | solution.py:262
  13.0 11.9 %copy-start.2 = (f32[4,16,128]{2,1,0:T(8,128)S(1)}, f32[4,16,128]{2,1,0:T(8,128)}, u32[]{:S(2)}) copy-start(f32[4,16,128]{2,1,0:T(8,128)} %cond.5) | copy-start | bytes 98308
  13.0 21.2 %all-to-all-start = ((f32[64,2,128]{2,1,0:T(2,128)}), f32[64,2,128]{2,1,0:T(2,128)S(1)}, u32[]{:S(2)}, u32[]{:S(2)}) async-start(f32[64,2,128]{2,1,0:T(2,128)} %get-tuple-element.11), calls=%async_computation | async-start | bytes 131072 | tf_op jit(solution)/shard_map/all_to_all | solution.py:263
  26.8 8.5 %collective-permute-start.2 = (f32[6,3,16,128]{3,2,1,0:T(8,128)S(1)}, f32[6,3,16,128]{3,2,1,0:T(8,128)S(1)}, u32[]{:S(2)}, u32[]{:S(2)}) collective-permute-start(f32[6,3,16,128]{3,2,1,0:T(8,128)S(1)} %get-tuple-element.12), channel_id=1, source_target_pairs={{0,1},{1,2},{2,3},{3,4},{4,5},{5,6},{6,7},{7,8},{8,9},{9,10},{10,1... | collective-permute-start | bytes 442376 | tf_op jit(solution)/shard_map/ppermute | solution.py:274
  30.4 6.6 %copy-start = (f32[1,6,4,16,128]{4,3,2,1,0:T(8,128)S(1)}, f32[1,6,4,16,128]{4,3,2,1,0:T(8,128)}, u32[]{:S(2)}) copy-start(f32[1,6,4,16,128]{4,3,2,1,0:T(8,128)} %get-tuple-element.6.field) | copy-start | bytes 589828
  30.4 6.6 %collective-permute-start.3 = (f32[6,3,16,128]{3,2,1,0:T(8,128)S(1)}, f32[6,3,16,128]{3,2,1,0:T(8,128)S(1)}, u32[]{:S(2)}, u32[]{:S(2)}) collective-permute-start(f32[6,3,16,128]{3,2,1,0:T(8,128)S(1)} %get-tuple-element.13), channel_id=1, source_target_pairs={{1,0},{2,1},{3,2},{4,3},{5,4},{6,5},{7,6},{8,7},{9,8},{10,9},{11,1... | collective-permute-start | bytes 442376 | tf_op jit(solution)/shard_map/ppermute | solution.py:275

commit v3 on v2

--- a/solution.py
+++ b/solution.py
@@ -13,22 +13,42 @@
 
 VMEM = pl.BlockSpec(memory_space=pltpu.VMEM)
 SMEM = pl.BlockSpec(memory_space=pltpu.SMEM)
-
-
-def pack_kernel(source, cond, observed, cells, counts, to_right, to_left, payload, values, columns):
-    depth = cond.shape[0]
-    for out, first in ((to_right, depth - HALO), (to_left, 0)):
-        out[:6] = source[:, first:first + HALO]
-        out[6] = cond[first:first + HALO]
+HBM = pl.BlockSpec(memory_space=pltpu.HBM)
+
+
+def pack_kernel(
+    source, cond, observed, cells, counts, own, near_edge, payload,
+    observed_in, cells_in, counts_in, values, columns, arrived,
+):
+    core = lax.axis_index("tile") % 2
+    edge = pl.ds(2 * core, 2)
+    copies = [
+        pltpu.make_async_copy(start, end, arrived.at[i])
+        for i, (start, end) in enumerate(
+            (
+                (observed, observed_in),
+                (cells, cells_in),
+                (counts, counts_in),
+                (cond, own.at[6]),
+                (cond.at[edge], near_edge.at[6]),
+                (source, own.at[pl.ds(0, 6)]),
+                (source.at[:, edge], near_edge.at[pl.ds(0, 6)]),
+            )
+        )
+    ]
+    for copy in copies:
+        copy.start()
+    for copy in copies[:3]:
+        copy.wait()
     tiles = counts.shape[1]
     slots = cells.shape[1]
     cap = slots // tiles
     for part in range(6):
-        values[part:part + 1] = observed[part]
-    values[6:7] = cells[...].astype(jnp.float32)
+        values[part:part + 1] = observed_in[part]
+    values[6:7] = cells_in[...].astype(jnp.float32)
     owner = lax.broadcasted_iota(jnp.int32, (tiles, slots), 1) // cap
     spread = (owner == lax.broadcasted_iota(jnp.int32, (tiles, slots), 0)).astype(jnp.bfloat16)
-    count = jnp.broadcast_to(counts[...].astype(jnp.float32), (8, tiles)).astype(jnp.bfloat16)
+    count = jnp.broadcast_to(counts_in[...].astype(jnp.float32), (8, tiles)).astype(jnp.bfloat16)
     repeated = lax.dot_general(count, spread, (((1,), (0,)), ((), ())), preferred_element_type=jnp.float32)
     within = lax.broadcasted_iota(jnp.int32, (8, slots), 1) % cap
     live = (within.astype(jnp.float32) < repeated).astype(jnp.float32)
@@ -45,6 +65,8 @@
             planes[group // 2] += pltpu.roll(piece, shift, 1) if shift else piece
     for plane in range(2):
         payload[:, plane, :] = planes[plane]
+    for copy in copies[3:]:
+        copy.wait()
 
 
 def spread_kernel(received, out, left, right):
@@ -102,18 +124,11 @@
             buffer[part, layer * PITCH:layer * PITCH + 8] = jnp.zeros((8, LANES), jnp.float32)
 
 
-def coefficients(factor, cond, hl, hr, pq, depth):
-    tile = lax.axis_index("tile")
-    last = lax.axis_size("tile") - 1
-    layers = depth + 2 * HALO
-    for layer in range(layers):
-        if layer < HALO:
-            sigma, scale = hl[6, layer], jnp.where(tile > 0, DAMPING, 0.0)
-        elif layer < HALO + depth:
-            sigma, scale = cond[layer - HALO], DAMPING
-        else:
-            sigma, scale = hr[6, layer - HALO - depth], jnp.where(tile < last, DAMPING, 0.0)
-        absorb = factor * sigma
+def coefficients(absorbs, pq, tile, tiles):
+    depth = len(absorbs) - 4 * HALO
+    for layer, absorb in enumerate(absorbs):
+        place = tile * depth + layer - 2 * HALO
+        scale = jnp.where((place >= 0) & (place < tiles * depth), DAMPING, 0.0)
         weight = scale / (36.0 + absorb * absorb)
         pq[0, layer] = 6.0 * weight
         pq[1, layer] = absorb * weight
@@ -167,8 +182,8 @@
     lax.fori_loop(lo, hi, step, 0, unroll=unroll)
 
 
-def relax(src, pq, one, two, depth, emit):
-    layers = depth + 2 * HALO
+def relax(src, pq, one, two, emit):
+    layers = src.shape[1]
     clear(one, layers)
     clear(two, layers)
     first_sweep(src, pq, one, layers)
@@ -179,54 +194,64 @@
         old, new = new, old
 
 
-def forward_kernel(factor, source, cond, hl, hr, field, to_right, to_left, src, pq, one, two):
-    depth = cond.shape[0]
-    coefficients(factor[0], cond, hl, hr, pq, depth)
-    src[:, 0:HALO] = hl[:6]
-    src[:, HALO:HALO + depth] = source[...]
-    src[:, HALO + depth:] = hr[:6]
+def choose_kernel(own, other, out):
+    core = lax.axis_index("tile") % 2
+    depth = own.shape[1]
+    out[:, 0:depth] = other[...]
+    out[:, depth:] = own[:, pl.ds(2 * (1 - core), 2)]
+
+
+def forward_kernel(factor, own, other, far, edge, near, near_pq, src, pq, one, two):
+    depth = own.shape[1]
+    tile, tiles = lax.axis_index("tile"), lax.axis_size("tile")
+    even = tile % 2 == 0
+    views = [(far, depth + i, edge, i) for i in range(2)]
+    views += [(far, i, other, i) for i in range(depth)]
+    views += [(own, i, own, i) for i in range(depth)]
+    views += [(other, i, far, i) for i in range(depth)]
+    views += [(edge, i, far, depth + i) for i in range(2)]
+    absorbs = []
+    for layer, (first, at, second, there) in enumerate(views):
+        if first is second:
+            src[:, layer] = first[:6, at]
+            absorbs.append(factor[0] * first[6, at])
+        else:
+            src[:, layer] = jnp.where(even, first[:6, at], second[:6, there])
+            absorbs.append(factor[0] * jnp.where(even, first[6, at], second[6, there]))
+    coefficients(absorbs, pq, tile, tiles)
+    near_pq[...] = pq[:, HALO:-HALO]
 
     def emit(layer, results):
         for part, (re, im) in enumerate(results):
-            field[0, part, layer - HALO] = re
-            field[0, part + 3, layer - HALO] = im
-
-    relax(src, pq, one, two, depth, emit)
-    to_right[...] = field[0, :, depth - HALO:]
-    to_left[...] = field[0, :, 0:HALO]
-
-
-def adjoint_kernel(factor, sums, cond, hl, hr, field, fl, fr, terms, src, pq, one, two):
-    depth = cond.shape[0]
-    coefficients(factor[0], cond, hl, hr, pq, depth)
+            near[part, layer - HALO] = re
+            near[part + 3, layer - HALO] = im
+
+    relax(src, pq, one, two, emit)
+
+
+def adjoint_kernel(factor, sums, near, pq, terms, field, src, one, two, left):
+    depth = near.shape[1] - 2 * HALO
+    copy = pltpu.make_async_copy(near.at[:, pl.ds(HALO, depth)], field.at[0], left)
+    copy.start()
     for part in range(6):
-        src[part, 0:HALO] = sums[6, 0:HALO] * fl[part] - sums[part, 0:HALO]
-        own = slice(HALO, HALO + depth)
-        src[part, own] = sums[6, own] * field[0, part] - sums[part, own]
-        src[part, HALO + depth:] = sums[6, HALO + depth:] * fr[part] - sums[part, HALO + depth:]
+        src[part] = sums[6] * near[part] - sums[part]
 
     def emit(layer, results):
-        at = layer - HALO
         total = 0.0
         for part, (re, im) in enumerate(results):
-            total = total + (re * field[0, part + 3, at] + im * field[0, part, at])
+            total = total + (re * near[part + 3, layer] + im * near[part, layer])
         total = factor[0] * total
-        rows = pl.ds(pl.multiple_of(at * 16, 16), 16)
-        for copy in range(terms.shape[0]):
-            terms[copy, rows] = total
-
-    relax(src, pq, one, two, depth, emit)
-
-
-def working(depth):
-    layers = depth + 2 * HALO
+        rows = pl.ds(pl.multiple_of((layer - HALO) * 16, 16), 16)
+        for index in range(terms.shape[0]):
+            terms[index, rows] = total
+
+    relax(src, pq, one, two, emit)
+    copy.wait()
+
+
+def working(layers):
     buffer = pltpu.VMEM((6, layers * PITCH + 8, LANES), jnp.float32)
-    return [
-        pltpu.VMEM((6, layers, 16, LANES), jnp.float32),
-        pltpu.VMEM((2, layers, 16, LANES), jnp.float32),
-        buffer,
-        buffer,
-    ]
+    return [pltpu.VMEM((6, layers, 16, LANES), jnp.float32), buffer, buffer]
 
 
 def shape(*dims):
@@ -244,36 +269,61 @@
     tiles, freqs = lax.axis_size("tile"), lax.axis_size("freq")
     depth, ny, nz = conductivity.shape
     slots = slot_cells.shape[0]
-    to_right, to_left, payload = pl.pallas_call(
+    own, near_edge, payload = pl.pallas_call(
         pack_kernel,
-        out_shape=(shape(7, HALO, ny, nz), shape(7, HALO, ny, nz), shape(tiles, 2, LANES)),
-        in_specs=[VMEM] * 5,
+        out_shape=(shape(7, depth, ny, nz), shape(7, 2, ny, nz), shape(tiles, 2, LANES)),
+        in_specs=[HBM] * 5,
         out_specs=(VMEM, VMEM, VMEM),
         scratch_shapes=[
+            pltpu.VMEM((6, 1, slots), jnp.float32),
+            pltpu.VMEM((1, slots), jnp.int32),
+            pltpu.VMEM((1, tiles), jnp.int32),
             pltpu.VMEM((ROWS, slots), jnp.float32),
             pltpu.VMEM((slots + 2 * (slots // tiles), LANES), jnp.float32),
+            pltpu.SemaphoreType.DMA((7,)),
         ],
+        compiler_params=LIMIT,
         cost_estimate=cost(10**6, 10**6),
         name="pack",
-    )(source, conductivity, observed.transpose(1, 0, 2), slot_cells.reshape(1, -1), block_counts.reshape(1, -1))
-    rightward = [(i, i + 1) for i in range(tiles - 1)]
-    leftward = [(i + 1, i) for i in range(tiles - 1)]
-    hl = lax.ppermute(to_right, "tile", rightward)
-    hr = lax.ppermute(to_left, "tile", leftward)
+    )(
+        *(
+            pltpu.with_memory_space_constraint(x, pltpu.HBM)
+            for x in (
+                source,
+                conductivity,
+                observed.transpose(1, 0, 2),
+                slot_cells.reshape(1, -1),
+                block_counts.reshape(1, -1),
+            )
+        )
+    )
+    chips = tiles // 2
+    other = lax.ppermute(own, "tile", [(i, i ^ 1) for i in range(tiles)])
     received = lax.all_to_all(payload, "tile", split_axis=0, concat_axis=0, tiled=True)
-    field, to_right, to_left = pl.pallas_call(
+    six = pl.pallas_call(
+        choose_kernel,
+        out_shape=shape(7, depth + 2, ny, nz),
+        in_specs=[VMEM] * 2,
+        out_specs=VMEM,
+        compiler_params=LIMIT,
+        cost_estimate=cost(10**10, 10**9),
+        name="choose",
+    )(own, other)
+    up = [(2 * k, 2 * k + 2) for k in range(chips - 1)]
+    down = [(2 * k + 2, 2 * k) for k in range(chips - 1)]
+    far = lax.ppermute(six, "tile", up + [(i + 1, j + 1) for i, j in down])
+    edge = lax.ppermute(near_edge, "tile", down + [(i + 1, j + 1) for i, j in up])
+    wide, layers = depth + 4 * HALO, depth + 2 * HALO
+    near, near_pq = pl.pallas_call(
         forward_kernel,
-        out_shape=(shape(1, 6, depth, ny, nz), shape(6, HALO, ny, nz), shape(6, HALO, ny, nz)),
+        out_shape=(shape(6, layers, ny, nz), shape(2, layers, ny, nz)),
         in_specs=[SMEM] + [VMEM] * 4,
-        out_specs=(VMEM, VMEM, VMEM),
-        scratch_shapes=working(depth),
-        cost_estimate=cost(10**10, 10**9),
-        compiler_params=LIMIT,
+        out_specs=(VMEM, VMEM),
+        scratch_shapes=[working(wide)[0], pltpu.VMEM((2, wide, ny, nz), jnp.float32)] + working(wide)[1:],
+        compiler_params=LIMIT,
+        cost_estimate=cost(10**6, 10**6),
         name="forward",
-    )(freq_factor, source, conductivity, hl, hr)
-    fl = lax.ppermute(to_right, "tile", rightward)
-    fr = lax.ppermute(to_left, "tile", leftward)
-    layers = depth + 2 * HALO
+    )(freq_factor, own, other, far, edge)
     sums = pl.pallas_call(
         spread_kernel,
         out_shape=shape(7, layers, ny, nz),
@@ -283,20 +333,20 @@
             pltpu.VMEM((19 * depth * ny, slots), jnp.bfloat16),
             pltpu.VMEM((LANES, slots), jnp.bfloat16),
         ],
+        compiler_params=LIMIT,
         cost_estimate=cost(10**10, 10**9),
-        compiler_params=LIMIT,
         name="spread",
     )(received)
-    terms = pl.pallas_call(
+    terms, field = pl.pallas_call(
         adjoint_kernel,
-        out_shape=shape(freqs, depth * ny, nz),
-        in_specs=[SMEM] + [VMEM] * 7,
-        out_specs=VMEM,
-        scratch_shapes=working(depth),
+        out_shape=(shape(freqs, depth * ny, nz), shape(1, 6, depth, ny, nz)),
+        in_specs=[SMEM] + [VMEM] * 3,
+        out_specs=(VMEM, HBM),
+        scratch_shapes=working(layers) + [pltpu.SemaphoreType.DMA],
+        compiler_params=LIMIT,
         cost_estimate=cost(10**7, 10**6),
-        compiler_params=LIMIT,
         name="adjoint",
-    )(freq_factor, sums, conductivity, hl, hr, field, fl, fr)
+    )(freq_factor, sums, near, near_pq)
     terms = lax.all_to_all(terms, "freq", split_axis=0, concat_axis=0, tiled=True)
     gradient = jnp.sum(terms, axis=0).reshape(depth, ny, nz)
     return (field, gradient)

time: 57.8 us -> 56.6 us (0.979)
  the two profiles are of different devices: /device:TPU:1 before, /device:TPU:7 now
where the time goes in v3:
time: 56.6 us; the launch traced here: 56.3 us
  starting transfers between devices  21.4 us (38%)
  blocking collectives  19 us (34%)
  Pallas kernels  7.02 us (12%)
  waiting for transfers between devices  6.8 us (12%)
  between operations  1.37 us (2%)
  other arithmetic  0.63 us (1%)
    all_to_all x1, blocking collectives, body(): lax.all_to_all(terms, 'freq', split_axis=0, concat_axis=0, tiled=True)  19 us
    all_to_all x1, starting transfers between devices, body(): lax.all_to_all(payload, 'tile', split_axis=0, concat_axis=0, tiled=True)  13.6 us
    ppermute x1, waiting for transfers between devices, body(): far = lax.ppermute(six, 'tile', up + [(i + 1, j + 1) for i, j in down])  4.78 us
    ppermute x1, starting transfers between devices, body(): lax.ppermute(near_edge, 'tile', down + [(i + 1, j + 1) for i, j in up])  3.09 us
    pallas_call x1, Pallas kernels, body(): pl.pallas_call(forward_kernel, out_shape=(shape(6, layers, ny, nz), shape...  2.59 us
    ppermute x1, starting transfers between devices, body(): other = lax.ppermute(own, 'tile', [(i, i ^ 1) for i in range(tiles)])  2.58 us
    ppermute x1, starting transfers between devices, body(): far = lax.ppermute(six, 'tile', up + [(i + 1, j + 1) for i, j in down])  2.19 us
    all_to_all x1, waiting for transfers between devices, body(): lax.all_to_all(payload, 'tile', split_axis=0, concat_axis=0, tiled=True)  2.01 us
  transfers between devices with their start and end apart: 4, of which 2 were waited for; matrix products, arithmetic and copies ran while one was open for 0% of the time, Pallas kernels for 2%

profile of v3, /device:TPU:7, one launch (start us, length us, event | category | flops | bytes accessed | tf_op | source)
XLA Modules:
  0.0 56.3 jit_solution(2896061262592574935)
XLA Ops:
  0.6 2.0 %pack.1 = (f32[7,4,16,128]{3,2,1,0:T(8,128)S(1)}, f32[7,2,16,128]{3,2,1,0:T(8,128)S(1)}, f32[64,2,128]{2,1,0:T(2,128)}) custom-call(f32[6,4,16,128]{3,2,1,0:T(8,128)} %source.1, f32[4,16,128]{2,1,0:T(8,128)} %cond.1, f32[6,1,512]{2,1,0:T(1,128)} %bitcast.5, s32[1,512]{1,0:T(1,128)} %bitcast.6, s32[1,64]{1,0:T(1,128)} %bitcast.7), custom_call_target="tpu_custom_call" | custom-call | flops 1000000 | bytes 1000000 | tf_op jit(solution)/shard_map/pack/pallas_call | solution.py:272
  2.6 2.6 %collective-permute-start = (f32[7,4,16,128]{3,2,1,0:T(8,128)S(1)}, f32[7,4,16,128]{3,2,1,0:T(8,128)S(1)}, u32[]{:S(2)}, u32[]{:S(2)}) collective-permute-start(f32[7,4,16,128]{3,2,1,0:T(8,128)S(1)} %get-tuple-element.10.own), channel_id=1, source_target_pairs={{0,1},{1,0},{2,3},{3,2},{4,5},{5,4},{6,7},{7,6},{8,9},{9,8},{10,11... | collective-permute-start | bytes 688136 | tf_op jit(solution)/shard_map/ppermute | solution.py:301
  5.2 13.6 %all-to-all-start = ((f32[64,2,128]{2,1,0:T(2,128)}), f32[64,2,128]{2,1,0:T(2,128)S(1)}, u32[]{:S(2)}, u32[]{:S(2)}) async-start(f32[64,2,128]{2,1,0:T(2,128)} %get-tuple-element.9), calls=%async_computation | async-start | bytes 131072 | tf_op jit(solution)/shard_map/all_to_all | solution.py:302
  18.8 3.1 %collective-permute-start.2 = (f32[7,2,16,128]{3,2,1,0:T(8,128)S(1)}, f32[7,2,16,128]{3,2,1,0:T(8,128)S(1)}, u32[]{:S(2)}, u32[]{:S(2)}) collective-permute-start(f32[7,2,16,128]{3,2,1,0:T(8,128)S(1)} %get-tuple-element.11), channel_id=1, source_target_pairs={{2,0},{4,2},{6,4},{8,6},{10,8},{12,10},{14,12},{16,14},{18,16},{20... | collective-permute-start | bytes 344072 | tf_op jit(solution)/shard_map/ppermute | solution.py:315
  22.5 0.0 collective-permute-done.other
  22.6 2.2 %collective-permute-start.1 = (f32[7,6,16,128]{3,2,1,0:T(8,128)S(1)}, f32[7,6,16,128]{3,2,1,0:T(8,128)S(1)}, u32[]{:S(2)}, u32[]{:S(2)}) collective-permute-start(f32[7,6,16,128]{3,2,1,0:T(8,128)S(1)} %choose.1), channel_id=1, source_target_pairs={{0,2},{2,4},{4,6},{6,8},{8,10},{10,12},{12,14},{14,16},{16,18},{18... | collective-permute-start | bytes 1032200 | tf_op jit(solution)/shard_map/ppermute | solution.py:314
  24.8 2.0 %all-to-all-done.received = f32[64,2,128]{2,1,0:T(2,128)S(1)} async-done(((f32[64,2,128]{2,1,0:T(2,128)}), f32[64,2,128]{2,1,0:T(2,128)S(1)}, u32[]{:S(2)}, u32[]{:S(2)}) %all-to-all-start) | async-done | bytes 65568 | tf_op jit(solution)/shard_map/all_to_all | solution.py:302
  26.8 1.1 %spread.1.sums = f32[7,10,16,128]{3,2,1,0:T(8,128)S(1)} custom-call(f32[64,2,128]{2,1,0:T(2,128)S(1)} %all-to-all-done.received), custom_call_target="tpu_custom_call" | custom-call | flops 10000000000 | bytes 1000000000 | tf_op jit(solution)/shard_map/spread/pallas_call | solution.py:327
  27.9 0.0 collective-permute-done.2.edge
  27.9 4.8 %collective-permute-done.1.far = f32[7,6,16,128]{3,2,1,0:T(8,128)S(1)} collective-permute-done((f32[7,6,16,128]{3,2,1,0:T(8,128)S(1)}, f32[7,6,16,128]{3,2,1,0:T(8,128)S(1)}, u32[]{:S(2)}, u32[]{:S(2)}) %collective-permute-start.1) | collective-permute-done | bytes 344096 | tf_op jit(solution)/shard_map/ppermute | solution.py:314
  32.7 2.6 %forward.1 = (f32[6,10,16,128]{3,2,1,0:T(8,128)S(1)}, f32[2,10,16,128]{3,2,1,0:T(8,128)S(1)}) custom-call(f32[1]{0:T(128)S(6)} %copy.8.factor, f32[7,4,16,128]{3,2,1,0:T(8,128)S(1)} %get-tuple-element.10.own, f32[7,4,16,128]{3,2,1,0:T(8,128)S(1)} %collective-permute-done.other, f32[7,6,16,128]{3,2,1,0:T(8,128)S(1)} %collective-permute-done.1.far, ...), custom_call_target="tpu_custom_call" | custom-call | flops 1000000 | bytes 1000000 | tf_op jit(solution)/shard_map/forward/pallas_call | solution.py:317
  35.3 1.4 %adjoint.1 = (f32[8,64,128]{2,1,0:T(8,128)S(1)}, f32[1,6,4,16,128]{4,3,2,1,0:T(8,128)}) custom-call(f32[1]{0:T(128)S(6)} %copy.8.factor, f32[7,10,16,128]{3,2,1,0:T(8,128)S(1)} %spread.1.sums, f32[6,10,16,128]{3,2,1,0:T(8,128)S(1)} %get-tuple-element.12.near, f32[2,10,16,128]{3,2,1,0:T(8,128)S(1)} %get-tuple-element.13.pq), custom_call_target="tpu_custom_call" | custom-call | flops 10000000 | bytes 1000000 | tf_op jit(solution)/shard_map/adjoint/pallas_call | solution.py:340
  36.6 19.0 %all_to_all.10 = f32[8,64,128]{2,1,0:T(8,128)S(1)} all-to-all(f32[8,64,128]{2,1,0:T(8,128)S(1)} %get-tuple-element.15), channel_id=1, replica_groups=mesh['freq'=8,'tile'=64] {'freq'}, dimensions={0} | all-to-all | bytes 524288 | tf_op jit(solution)/shard_map/all_to_all | solution.py:350
  55.6 0.6 %reduce_sum.9 = f32[64,128]{1,0:T(8,128)} reduce(f32[8,64,128]{2,1,0:T(8,128)S(1)} %all_to_all.10, f32[]{:T(128)} %constant.0.clone.1), dimensions={0}, to_apply=%region_0.0 | reduce | flops 57344 | bytes 294916 | tf_op jit(solution)/shard_map/reduce_sum | solution.py:351
  (1 shorter events, 0.0 us)
Async XLA Ops:
  2.6 19.9 %collective-permute-start = (f32[7,4,16,128]{3,2,1,0:T(8,128)S(1)}, f32[7,4,16,128]{3,2,1,0:T(8,128)S(1)}, u32[]{:S(2)}, u32[]{:S(2)}) collective-permute-start(f32[7,4,16,128]{3,2,1,0:T(8,128)S(1)} %get-tuple-element.10.own), channel_id=1, source_target_pairs={{0,1},{1,0},{2,3},{3,2},{4,5},{5,4},{6,7},{7,6},{8,9},{9,8},{10,11... | collective-permute-start | bytes 688136 | tf_op jit(solution)/shard_map/ppermute | solution.py:301
  5.2 21.6 %all-to-all-start = ((f32[64,2,128]{2,1,0:T(2,128)}), f32[64,2,128]{2,1,0:T(2,128)S(1)}, u32[]{:S(2)}, u32[]{:S(2)}) async-start(f32[64,2,128]{2,1,0:T(2,128)} %get-tuple-element.9), calls=%async_computation | async-start | bytes 131072 | tf_op jit(solution)/shard_map/all_to_all | solution.py:302
  18.8 9.1 %collective-permute-start.2 = (f32[7,2,16,128]{3,2,1,0:T(8,128)S(1)}, f32[7,2,16,128]{3,2,1,0:T(8,128)S(1)}, u32[]{:S(2)}, u32[]{:S(2)}) collective-permute-start(f32[7,2,16,128]{3,2,1,0:T(8,128)S(1)} %get-tuple-element.11), channel_id=1, source_target_pairs={{2,0},{4,2},{6,4},{8,6},{10,8},{12,10},{14,12},{16,14},{18,16},{20... | collective-permute-start | bytes 344072 | tf_op jit(solution)/shard_map/ppermute | solution.py:315
  22.6 10.1 %collective-permute-start.1 = (f32[7,6,16,128]{3,2,1,0:T(8,128)S(1)}, f32[7,6,16,128]{3,2,1,0:T(8,128)S(1)}, u32[]{:S(2)}, u32[]{:S(2)}) collective-permute-start(f32[7,6,16,128]{3,2,1,0:T(8,128)S(1)} %choose.1), channel_id=1, source_target_pairs={{0,2},{2,4},{4,6},{6,8},{8,10},{10,12},{12,14},{14,16},{16,18},{18... | collective-permute-start | bytes 1032200 | tf_op jit(solution)/shard_map/ppermute | solution.py:314

commit v4 on v3

--- a/solution.py
+++ b/solution.py
@@ -21,7 +21,7 @@
     observed_in, cells_in, counts_in, values, columns, arrived,
 ):
     core = lax.axis_index("tile") % 2
-    edge = pl.ds(2 * core, 2)
+    edge = pl.ds(2 * (1 - core), 2)
     copies = [
         pltpu.make_async_copy(start, end, arrived.at[i])
         for i, (start, end) in enumerate(
@@ -194,22 +194,21 @@
         old, new = new, old
 
 
-def choose_kernel(own, other, out):
-    core = lax.axis_index("tile") % 2
-    depth = own.shape[1]
-    out[:, 0:depth] = other[...]
-    out[:, depth:] = own[:, pl.ds(2 * (1 - core), 2)]
-
-
-def forward_kernel(factor, own, other, far, edge, near, near_pq, src, pq, one, two):
+def choose_kernel(own, across, out):
+    out[0] = own[...]
+    out[1] = across[...]
+
+
+def forward_kernel(factor, own, across, edge, other, near, near_pq, src, pq, one, two):
     depth = own.shape[1]
     tile, tiles = lax.axis_index("tile"), lax.axis_size("tile")
     even = tile % 2 == 0
-    views = [(far, depth + i, edge, i) for i in range(2)]
-    views += [(far, i, other, i) for i in range(depth)]
+    mine, theirs = other.at[0], other.at[1]
+    views = [(edge, i, across, depth - 2 + i) for i in range(2)]
+    views += [(theirs, i, mine, i) for i in range(depth)]
     views += [(own, i, own, i) for i in range(depth)]
-    views += [(other, i, far, i) for i in range(depth)]
-    views += [(edge, i, far, depth + i) for i in range(2)]
+    views += [(mine, i, theirs, i) for i in range(depth)]
+    views += [(across, i, edge, i) for i in range(2)]
     absorbs = []
     for layer, (first, at, second, there) in enumerate(views):
         if first is second:
@@ -298,21 +297,21 @@
         )
     )
     chips = tiles // 2
-    other = lax.ppermute(own, "tile", [(i, i ^ 1) for i in range(tiles)])
+    up = [(2 * k, 2 * k + 2) for k in range(chips - 1)]
+    down = [(2 * k + 2, 2 * k) for k in range(chips - 1)]
+    across = lax.ppermute(own, "tile", down + [(i + 1, j + 1) for i, j in up])
+    edge = lax.ppermute(near_edge, "tile", up + [(i + 1, j + 1) for i, j in down])
     received = lax.all_to_all(payload, "tile", split_axis=0, concat_axis=0, tiled=True)
-    six = pl.pallas_call(
+    chosen = pl.pallas_call(
         choose_kernel,
-        out_shape=shape(7, depth + 2, ny, nz),
+        out_shape=shape(2, 7, depth, ny, nz),
         in_specs=[VMEM] * 2,
         out_specs=VMEM,
         compiler_params=LIMIT,
         cost_estimate=cost(10**10, 10**9),
         name="choose",
-    )(own, other)
-    up = [(2 * k, 2 * k + 2) for k in range(chips - 1)]
-    down = [(2 * k + 2, 2 * k) for k in range(chips - 1)]
-    far = lax.ppermute(six, "tile", up + [(i + 1, j + 1) for i, j in down])
-    edge = lax.ppermute(near_edge, "tile", down + [(i + 1, j + 1) for i, j in up])
+    )(own, across)
+    other = lax.ppermute(chosen, "tile", [(i, i ^ 1) for i in range(tiles)])
     wide, layers = depth + 4 * HALO, depth + 2 * HALO
     near, near_pq = pl.pallas_call(
         forward_kernel,
@@ -323,7 +322,7 @@
         compiler_params=LIMIT,
         cost_estimate=cost(10**6, 10**6),
         name="forward",
-    )(freq_factor, own, other, far, edge)
+    )(freq_factor, own, across, edge, other)
     sums = pl.pallas_call(
         spread_kernel,
         out_shape=shape(7, layers, ny, nz),

time: 56.6 us -> 53.7 us (0.949)
  the two profiles are of different devices: /device:TPU:7 before, /device:TPU:1 now
where the time goes in v4:
time: 53.7 us; the launch traced here: 53.3 us
  starting transfers between devices  23.2 us (43%)
  blocking collectives  17.6 us (33%)
  Pallas kernels  7.03 us (13%)
  waiting for transfers between devices  3.54 us (7%)
  between operations  1.37 us (3%)
  other arithmetic  0.63 us (1%)
    all_to_all x1, blocking collectives, body(): lax.all_to_all(terms, 'freq', split_axis=0, concat_axis=0, tiled=True)  17.6 us
    all_to_all x1, starting transfers between devices, body(): lax.all_to_all(payload, 'tile', split_axis=0, concat_axis=0, tiled=True)  13.4 us
    ppermute x1, starting transfers between devices, body(): other = lax.ppermute(chosen, 'tile', [(i, i ^ 1) for i in range(tiles)])  4.55 us
    ppermute x1, starting transfers between devices, body(): across = lax.ppermute(own, 'tile', down + [(i + 1, j + 1) for i, j in up])  3.96 us
    all_to_all x1, waiting for transfers between devices, body(): lax.all_to_all(payload, 'tile', split_axis=0, concat_axis=0, tiled=True)  3.53 us
    pallas_call x1, Pallas kernels, body(): pl.pallas_call(forward_kernel, out_shape=(shape(6, layers, ny, nz), shape...  2.59 us
    pallas_call x1, Pallas kernels, body(): pl.pallas_call(pack_kernel, out_shape=(shape(7, depth, ny, nz), shape(7,...  1.95 us
    pallas_call x1, Pallas kernels, body(): pl.pallas_call(adjoint_kernel, out_shape=(shape(freqs, depth * ny, nz), s...  1.36 us
  transfers between devices with their start and end apart: 4, of which 1 were waited for; matrix products, arithmetic and copies ran while one was open for 0% of the time, Pallas kernels for 2%

profile of v4, /device:TPU:1, one launch (start us, length us, event | category | flops | bytes accessed | tf_op | source)
XLA Modules:
  0.0 53.3 jit_solution(17348282773726337822)
XLA Ops:
  0.6 2.0 %pack.1 = (f32[7,4,16,128]{3,2,1,0:T(8,128)S(1)}, f32[7,2,16,128]{3,2,1,0:T(8,128)S(1)}, f32[64,2,128]{2,1,0:T(2,128)}) custom-call(f32[6,4,16,128]{3,2,1,0:T(8,128)} %source.1, f32[4,16,128]{2,1,0:T(8,128)} %cond.1, f32[6,1,512]{2,1,0:T(1,128)} %bitcast.5, s32[1,512]{1,0:T(1,128)} %bitcast.6, s32[1,64]{1,0:T(1,128)} %bitcast.7), custom_call_target="tpu_custom_call" | custom-call | flops 1000000 | bytes 1000000 | tf_op jit(solution)/shard_map/pack/pallas_call | solution.py:271
  2.6 4.0 %collective-permute-start = (f32[7,4,16,128]{3,2,1,0:T(8,128)S(1)}, f32[7,4,16,128]{3,2,1,0:T(8,128)S(1)}, u32[]{:S(2)}, u32[]{:S(2)}) collective-permute-start(f32[7,4,16,128]{3,2,1,0:T(8,128)S(1)} %get-tuple-element.10.own), channel_id=1, source_target_pairs={{2,0},{4,2},{6,4},{8,6},{10,8},{12,10},{14,12},{16,14},{18,16},{20... | collective-permute-start | bytes 688136 | tf_op jit(solution)/shard_map/ppermute | solution.py:302
  6.6 13.4 %all-to-all-start = ((f32[64,2,128]{2,1,0:T(2,128)}), f32[64,2,128]{2,1,0:T(2,128)S(1)}, u32[]{:S(2)}, u32[]{:S(2)}) async-start(f32[64,2,128]{2,1,0:T(2,128)} %get-tuple-element.9), calls=%async_computation | async-start | bytes 131072 | tf_op jit(solution)/shard_map/all_to_all | solution.py:304
  19.9 1.3 %collective-permute-start.1 = (f32[7,2,16,128]{3,2,1,0:T(8,128)S(1)}, f32[7,2,16,128]{3,2,1,0:T(8,128)S(1)}, u32[]{:S(2)}, u32[]{:S(2)}) collective-permute-start(f32[7,2,16,128]{3,2,1,0:T(8,128)S(1)} %get-tuple-element.11), channel_id=1, source_target_pairs={{0,2},{2,4},{4,6},{6,8},{8,10},{10,12},{12,14},{14,16},{16,18},{18... | collective-permute-start | bytes 344072 | tf_op jit(solution)/shard_map/ppermute | solution.py:303
  21.9 0.0 collective-permute-done.across
  21.9 4.6 %collective-permute-start.2 = (f32[2,7,4,16,128]{4,3,2,1,0:T(8,128)S(1)}, f32[2,7,4,16,128]{4,3,2,1,0:T(8,128)S(1)}, u32[]{:S(2)}, u32[]{:S(2)}) collective-permute-start(f32[2,7,4,16,128]{4,3,2,1,0:T(8,128)S(1)} %choose.1), channel_id=1, source_target_pairs={{0,1},{1,0},{2,3},{3,2},{4,5},{5,4},{6,7},{7,6},{8,9},{9,8},{10,11... | collective-permute-start | bytes 1376264 | tf_op jit(solution)/shard_map/ppermute | solution.py:314
  26.5 3.5 %all-to-all-done.received = f32[64,2,128]{2,1,0:T(2,128)S(1)} async-done(((f32[64,2,128]{2,1,0:T(2,128)}), f32[64,2,128]{2,1,0:T(2,128)S(1)}, u32[]{:S(2)}, u32[]{:S(2)}) %all-to-all-start) | async-done | bytes 65568 | tf_op jit(solution)/shard_map/all_to_all | solution.py:304
  30.0 1.1 %spread.1.sums = f32[7,10,16,128]{3,2,1,0:T(8,128)S(1)} custom-call(f32[64,2,128]{2,1,0:T(2,128)S(1)} %all-to-all-done.received), custom_call_target="tpu_custom_call" | custom-call | flops 10000000000 | bytes 1000000000 | tf_op jit(solution)/shard_map/spread/pallas_call | solution.py:326
  31.1 0.0 collective-permute-done.1.edge
  31.1 0.0 collective-permute-done.2.other
  31.1 2.6 %forward.1 = (f32[6,10,16,128]{3,2,1,0:T(8,128)S(1)}, f32[2,10,16,128]{3,2,1,0:T(8,128)S(1)}) custom-call(f32[1]{0:T(128)S(6)} %copy.8.factor, f32[7,4,16,128]{3,2,1,0:T(8,128)S(1)} %get-tuple-element.10.own, f32[7,4,16,128]{3,2,1,0:T(8,128)S(1)} %collective-permute-done.across, f32[7,2,16,128]{3,2,1,0:T(8,128)S(1)} %collective-permute-done.1.edge, ...), custom_call_target="tpu_custom_call" | custom-call | flops 1000000 | bytes 1000000 | tf_op jit(solution)/shard_map/forward/pallas_call | solution.py:316
  33.7 1.4 %adjoint.1 = (f32[8,64,128]{2,1,0:T(8,128)S(1)}, f32[1,6,4,16,128]{4,3,2,1,0:T(8,128)}) custom-call(f32[1]{0:T(128)S(6)} %copy.8.factor, f32[7,10,16,128]{3,2,1,0:T(8,128)S(1)} %spread.1.sums, f32[6,10,16,128]{3,2,1,0:T(8,128)S(1)} %get-tuple-element.12.near, f32[2,10,16,128]{3,2,1,0:T(8,128)S(1)} %get-tuple-element.13.pq), custom_call_target="tpu_custom_call" | custom-call | flops 10000000 | bytes 1000000 | tf_op jit(solution)/shard_map/adjoint/pallas_call | solution.py:339
  35.1 17.6 %all_to_all.10 = f32[8,64,128]{2,1,0:T(8,128)S(1)} all-to-all(f32[8,64,128]{2,1,0:T(8,128)S(1)} %get-tuple-element.15), channel_id=1, replica_groups=mesh['freq'=8,'tile'=64] {'freq'}, dimensions={0} | all-to-all | bytes 524288 | tf_op jit(solution)/shard_map/all_to_all | solution.py:349
  52.7 0.6 %reduce_sum.9 = f32[64,128]{1,0:T(8,128)} reduce(f32[8,64,128]{2,1,0:T(8,128)S(1)} %all_to_all.10, f32[]{:T(128)} %constant.0.clone.1), dimensions={0}, to_apply=%region_0.0 | reduce | flops 57344 | bytes 294916 | tf_op jit(solution)/shard_map/reduce_sum | solution.py:350
  (1 shorter events, 0.0 us)
Async XLA Ops:
  2.6 19.3 %collective-permute-start = (f32[7,4,16,128]{3,2,1,0:T(8,128)S(1)}, f32[7,4,16,128]{3,2,1,0:T(8,128)S(1)}, u32[]{:S(2)}, u32[]{:S(2)}) collective-permute-start(f32[7,4,16,128]{3,2,1,0:T(8,128)S(1)} %get-tuple-element.10.own), channel_id=1, source_target_pairs={{2,0},{4,2},{6,4},{8,6},{10,8},{12,10},{14,12},{16,14},{18,16},{20... | collective-permute-start | bytes 688136 | tf_op jit(solution)/shard_map/ppermute | solution.py:302
  6.6 23.5 %all-to-all-start = ((f32[64,2,128]{2,1,0:T(2,128)}), f32[64,2,128]{2,1,0:T(2,128)S(1)}, u32[]{:S(2)}, u32[]{:S(2)}) async-start(f32[64,2,128]{2,1,0:T(2,128)} %get-tuple-element.9), calls=%async_computation | async-start | bytes 131072 | tf_op jit(solution)/shard_map/all_to_all | solution.py:304
  19.9 11.2 %collective-permute-start.1 = (f32[7,2,16,128]{3,2,1,0:T(8,128)S(1)}, f32[7,2,16,128]{3,2,1,0:T(8,128)S(1)}, u32[]{:S(2)}, u32[]{:S(2)}) collective-permute-start(f32[7,2,16,128]{3,2,1,0:T(8,128)S(1)} %get-tuple-element.11), channel_id=1, source_target_pairs={{0,2},{2,4},{4,6},{6,8},{8,10},{10,12},{12,14},{14,16},{16,18},{18... | collective-permute-start | bytes 344072 | tf_op jit(solution)/shard_map/ppermute | solution.py:303
  21.9 9.2 %collective-permute-start.2 = (f32[2,7,4,16,128]{4,3,2,1,0:T(8,128)S(1)}, f32[2,7,4,16,128]{4,3,2,1,0:T(8,128)S(1)}, u32[]{:S(2)}, u32[]{:S(2)}) collective-permute-start(f32[2,7,4,16,128]{4,3,2,1,0:T(8,128)S(1)} %choose.1), channel_id=1, source_target_pairs={{0,1},{1,0},{2,3},{3,2},{4,5},{5,4},{6,7},{7,6},{8,9},{9,8},{10,11... | collective-permute-start | bytes 1376264 | tf_op jit(solution)/shard_map/ppermute | solution.py:314

commit v5 on v4

--- a/solution.py
+++ b/solution.py
@@ -77,12 +77,9 @@
         turned.append(jnp.concatenate([here, pltpu.roll(here, LANES - ROWS, 1)], axis=0).T)
     layer = out.shape[2]
     depth = out.shape[1] - 2 * HALO
-    plan = (
-        ((depth - HALO) * layer, HALO * layer, 0),
-        (0, depth * layer, HALO),
-        (0, HALO * layer, HALO + depth),
-    )
-    for group, (first, rows, where) in enumerate(plan):
+    half = depth * layer // 2
+    plan = ((depth - HALO, HALO, 0), (0, depth, HALO), (0, HALO, HALO + depth))
+    for group, (first, layers, where) in enumerate(plan):
         base = (group % 2) * 64
         record = jnp.concatenate(
             [turned[group // 2][base + 16 * j:base + 16 * j + ROWS] for j in range(4)], axis=1
@@ -95,24 +92,27 @@
         rest = value - high
         middle = rest.astype(jnp.bfloat16).astype(jnp.float32)
         low = rest - middle
-        row = lax.broadcasted_iota(jnp.int32, (rows, slots), 0) + first
-        hit = row == (cell >> 7)
+        row = cell // LANES
+        hit = lax.broadcasted_iota(jnp.int32, (half, slots), 0) == row % half
         place = 0
         for terms, names in ((high, (0, 1, 2, 3, 4, 5, 7)), (middle, range(6)), (low, range(6))):
             for name in names:
-                left[place:place + rows] = jnp.where(hit, terms[name:name + 1], 0.0).astype(jnp.bfloat16)
-                place += rows
-        lane = lax.broadcasted_iota(jnp.int32, (LANES, slots), 0) == (cell & (LANES - 1))
-        right[...] = lane.astype(jnp.float32).astype(jnp.bfloat16)
+                left[group, place:place + half] = jnp.where(hit, terms[name:name + 1], 0.0).astype(jnp.bfloat16)
+                place += half
+        column = cell % LANES + LANES * (row // half)
+        lane = lax.broadcasted_iota(jnp.int32, (2 * LANES, slots), 0) == column
+        right[group] = lane.astype(jnp.float32).astype(jnp.bfloat16)
         sums = lax.dot_general(
-            left[:place], right[...], (((1,), (1,)), ((), ())), preferred_element_type=jnp.float32
+            left[group], right[group], (((1,), (1,)), ((), ())), preferred_element_type=jnp.float32
         )
-        for name in range(6):
-            total = sums[name * rows:(name + 1) * rows]
-            total = total + sums[(7 + name) * rows:(8 + name) * rows]
-            total = total + sums[(13 + name) * rows:(14 + name) * rows]
-            out[name, where:where + rows // layer] = total.reshape(rows // layer, layer, LANES)
-        out[6, where:where + rows // layer] = sums[6 * rows:7 * rows].reshape(rows // layer, layer, LANES)
+        for name in range(7):
+            total = sums[name * half:(name + 1) * half]
+            if name < 6:
+                total = total + sums[(7 + name) * half:(8 + name) * half]
+                total = total + sums[(13 + name) * half:(14 + name) * half]
+            for index in range(layers):
+                side, at = divmod((first + index) * layer, half)
+                out[name, where + index] = total[at:at + layer, side * LANES:(side + 1) * LANES]
 
 
 PITCH = 24
@@ -147,7 +147,7 @@
     lax.fori_loop(0, layers, step, 0, unroll=2)
 
 
-def sweep(src, pq, old, new, lo, hi, unroll, emit=None):
+def sweep(src, pq, old, new, lo, hi, emit=None):
     lane = lax.broadcasted_iota(jnp.int32, (16, LANES), 1)
     not_first, not_last = lane > 0, lane < LANES - 1
 
@@ -179,7 +179,7 @@
             emit(layer, results)
         return carry
 
-    lax.fori_loop(lo, hi, step, 0, unroll=unroll)
+    lax.fori_loop(lo, hi, step, 0, unroll=hi - lo)
 
 
 def relax(src, pq, one, two, emit):
@@ -190,7 +190,7 @@
     old, new = one, two
     for index in range(1, SWEEPS):
         final = index == SWEEPS - 1
-        sweep(src, pq, old, new, index, layers - index, 2, emit if final else None)
+        sweep(src, pq, old, new, index, layers - index, emit if final else None)
         old, new = new, old
 
 
@@ -264,11 +264,10 @@
     return pl.CostEstimate(flops=flops, bytes_accessed=size, transcendentals=0)
 
 
-def body(source, conductivity, freq_factor, observed, slot_cells, block_counts):
-    tiles, freqs = lax.axis_size("tile"), lax.axis_size("freq")
+def pack(source, conductivity, observed, slot_cells, block_counts):
     depth, ny, nz = conductivity.shape
-    slots = slot_cells.shape[0]
-    own, near_edge, payload = pl.pallas_call(
+    slots, tiles = slot_cells.shape[0], block_counts.shape[0]
+    return pl.pallas_call(
         pack_kernel,
         out_shape=(shape(7, depth, ny, nz), shape(7, 2, ny, nz), shape(tiles, 2, LANES)),
         in_specs=[HBM] * 5,
@@ -296,56 +295,82 @@
             )
         )
     )
+
+
+def choose(own, across):
+    return pl.pallas_call(
+        choose_kernel,
+        out_shape=shape(2, *own.shape),
+        in_specs=[VMEM] * 2,
+        out_specs=VMEM,
+        compiler_params=LIMIT,
+        cost_estimate=cost(10**10, 10**9),
+        name="choose",
+    )(own, across)
+
+
+def forward(factor, own, across, edge, other):
+    depth, ny, nz = own.shape[1:]
+    wide, layers = depth + 4 * HALO, depth + 2 * HALO
+    return pl.pallas_call(
+        forward_kernel,
+        out_shape=(shape(6, layers, ny, nz), shape(2, layers, ny, nz)),
+        in_specs=[SMEM] + [VMEM] * 4,
+        out_specs=(VMEM, VMEM),
+        scratch_shapes=[working(wide)[0], pltpu.VMEM((2, wide, ny, nz), jnp.float32)] + working(wide)[1:],
+        compiler_params=LIMIT,
+        cost_estimate=cost(10**6, 10**6),
+        name="forward",
+    )(factor, own, across, edge, other)
+
+
+def spread(received, depth, ny, nz):
+    slots = received.shape[0] * received.shape[2] // (2 * ROWS)
+    return pl.pallas_call(
+        spread_kernel,
+        out_shape=shape(7, depth + 2 * HALO, ny, nz),
+        in_specs=[VMEM],
+        out_specs=VMEM,
+        scratch_shapes=[
+            pltpu.VMEM((3, 19 * depth * ny // 2, slots), jnp.bfloat16),
+            pltpu.VMEM((3, 2 * LANES, slots), jnp.bfloat16),
+        ],
+        compiler_params=LIMIT,
+        cost_estimate=cost(10**10, 10**9),
+        name="spread",
+    )(received)
+
+
+def adjoint(factor, sums, near, near_pq, freqs):
+    layers, ny, nz = near.shape[1:]
+    depth = layers - 2 * HALO
+    return pl.pallas_call(
+        adjoint_kernel,
+        out_shape=(shape(freqs, depth * ny, nz), shape(1, 6, depth, ny, nz)),
+        in_specs=[SMEM] + [VMEM] * 3,
+        out_specs=(VMEM, HBM),
+        scratch_shapes=working(layers) + [pltpu.SemaphoreType.DMA],
+        compiler_params=LIMIT,
+        cost_estimate=cost(10**7, 10**6),
+        name="adjoint",
+    )(factor, sums, near, near_pq)
+
+
+def body(source, conductivity, freq_factor, observed, slot_cells, block_counts):
+    tiles, freqs = lax.axis_size("tile"), lax.axis_size("freq")
+    depth, ny, nz = conductivity.shape
+    own, near_edge, payload = pack(source, conductivity, observed, slot_cells, block_counts)
     chips = tiles // 2
     up = [(2 * k, 2 * k + 2) for k in range(chips - 1)]
     down = [(2 * k + 2, 2 * k) for k in range(chips - 1)]
     across = lax.ppermute(own, "tile", down + [(i + 1, j + 1) for i, j in up])
     edge = lax.ppermute(near_edge, "tile", up + [(i + 1, j + 1) for i, j in down])
     received = lax.all_to_all(payload, "tile", split_axis=0, concat_axis=0, tiled=True)
-    chosen = pl.pallas_call(
-        choose_kernel,
-        out_shape=shape(2, 7, depth, ny, nz),
-        in_specs=[VMEM] * 2,
-        out_specs=VMEM,
-        compiler_params=LIMIT,
-        cost_estimate=cost(10**10, 10**9),
-        name="choose",
-    )(own, across)
+    chosen = choose(own, across)
     other = lax.ppermute(chosen, "tile", [(i, i ^ 1) for i in range(tiles)])
-    wide, layers = depth + 4 * HALO, depth + 2 * HALO
-    near, near_pq = pl.pallas_call(
-        forward_kernel,
-        out_shape=(shape(6, layers, ny, nz), shape(2, layers, ny, nz)),
-        in_specs=[SMEM] + [VMEM] * 4,
-        out_specs=(VMEM, VMEM),
-        scratch_shapes=[working(wide)[0], pltpu.VMEM((2, wide, ny, nz), jnp.float32)] + working(wide)[1:],
-        compiler_params=LIMIT,
-        cost_estimate=cost(10**6, 10**6),
-        name="forward",
-    )(freq_factor, own, across, edge, other)
-    sums = pl.pallas_call(
-        spread_kernel,
-        out_shape=shape(7, layers, ny, nz),
-        in_specs=[VMEM],
-        out_specs=VMEM,
-        scratch_shapes=[
-            pltpu.VMEM((19 * depth * ny, slots), jnp.bfloat16),
-            pltpu.VMEM((LANES, slots), jnp.bfloat16),
-        ],
-        compiler_params=LIMIT,
-        cost_estimate=cost(10**10, 10**9),
-        name="spread",
-    )(received)
-    terms, field = pl.pallas_call(
-        adjoint_kernel,
-        out_shape=(shape(freqs, depth * ny, nz), shape(1, 6, depth, ny, nz)),
-        in_specs=[SMEM] + [VMEM] * 3,
-        out_specs=(VMEM, HBM),
-        scratch_shapes=working(layers) + [pltpu.SemaphoreType.DMA],
-        compiler_params=LIMIT,
-        cost_estimate=cost(10**7, 10**6),
-        name="adjoint",
-    )(freq_factor, sums, near, near_pq)
+    near, near_pq = forward(freq_factor, own, across, edge, other)
+    sums = spread(received, depth, ny, nz)
+    terms, field = adjoint(freq_factor, sums, near, near_pq, freqs)
     terms = lax.all_to_all(terms, "freq", split_axis=0, concat_axis=0, tiled=True)
     gradient = jnp.sum(terms, axis=0).reshape(depth, ny, nz)
     return (field, gradient)

time: 53.7 us -> 51.4 us (0.957)
  Pallas kernels: 7.03 us -> 4.79 us
    pallas_call x5, Pallas kernels: 7.03 us -> 4.79 us  [the longest x1 1.95 us: pack(): pl.pallas_call(pack_kernel, out_shape=(shape(7, depth, ny, nz), shape(7,...]
where the time goes in v5:
time: 51.4 us; the launch traced here: 51.1 us
  starting transfers between devices  23.2 us (45%)
  blocking collectives  17.6 us (34%)
  Pallas kernels  4.79 us (9%)
  waiting for transfers between devices  3.54 us (7%)
  between operations  1.37 us (3%)
  other arithmetic  0.63 us (1%)
    all_to_all x1, blocking collectives, body(): lax.all_to_all(terms, 'freq', split_axis=0, concat_axis=0, tiled=True)  17.6 us
    all_to_all x1, starting transfers between devices, body(): lax.all_to_all(payload, 'tile', split_axis=0, concat_axis=0, tiled=True)  13.4 us
    ppermute x1, starting transfers between devices, body(): other = lax.ppermute(chosen, 'tile', [(i, i ^ 1) for i in range(tiles)])  4.55 us
    ppermute x1, starting transfers between devices, body(): across = lax.ppermute(own, 'tile', down + [(i + 1, j + 1) for i, j in up])  3.96 us
    all_to_all x1, waiting for transfers between devices, body(): lax.all_to_all(payload, 'tile', split_axis=0, concat_axis=0, tiled=True)  3.53 us
    pallas_call x1, Pallas kernels, pack(): pl.pallas_call(pack_kernel, out_shape=(shape(7, depth, ny, nz), shape(7,...  1.95 us
    ppermute x1, starting transfers between devices, body(): lax.ppermute(near_edge, 'tile', up + [(i + 1, j + 1) for i, j in down])  1.29 us
    pallas_call x1, Pallas kernels, forward(): pl.pallas_call(forward_kernel, out_shape=(shape(6, layers, ny, nz), shape...  1.26 us
  transfers between devices with their start and end apart: 4, of which 1 were waited for; matrix products, arithmetic and copies ran while one was open for 0% of the time, Pallas kernels for 2%

profile of v5, /device:TPU:1, one launch (start us, length us, event | category | flops | bytes accessed | tf_op | source)
XLA Modules:
  0.0 51.1 jit_solution(4797191059748354313)
XLA Ops:
  0.6 2.0 %pack.1 = (f32[7,4,16,128]{3,2,1,0:T(8,128)S(1)}, f32[7,2,16,128]{3,2,1,0:T(8,128)S(1)}, f32[64,2,128]{2,1,0:T(2,128)}) custom-call(f32[6,4,16,128]{3,2,1,0:T(8,128)} %source.1, f32[4,16,128]{2,1,0:T(8,128)} %cond.1, f32[6,1,512]{2,1,0:T(1,128)} %bitcast.5, s32[1,512]{1,0:T(1,128)} %bitcast.6, s32[1,64]{1,0:T(1,128)} %bitcast.7), custom_call_target="tpu_custom_call" | custom-call | flops 1000000 | bytes 1000000 | tf_op jit(solution)/shard_map/pack/pallas_call | solution.py:270
  2.6 4.0 %collective-permute-start = (f32[7,4,16,128]{3,2,1,0:T(8,128)S(1)}, f32[7,4,16,128]{3,2,1,0:T(8,128)S(1)}, u32[]{:S(2)}, u32[]{:S(2)}) collective-permute-start(f32[7,4,16,128]{3,2,1,0:T(8,128)S(1)} %get-tuple-element.10.own), channel_id=1, source_target_pairs={{2,0},{4,2},{6,4},{8,6},{10,8},{12,10},{14,12},{16,14},{18,16},{20... | collective-permute-start | bytes 688136 | tf_op jit(solution)/shard_map/ppermute | solution.py:366
  6.6 13.4 %all-to-all-start = ((f32[64,2,128]{2,1,0:T(2,128)}), f32[64,2,128]{2,1,0:T(2,128)S(1)}, u32[]{:S(2)}, u32[]{:S(2)}) async-start(f32[64,2,128]{2,1,0:T(2,128)} %get-tuple-element.9), calls=%async_computation | async-start | bytes 131072 | tf_op jit(solution)/shard_map/all_to_all | solution.py:368
  19.9 1.3 %collective-permute-start.1 = (f32[7,2,16,128]{3,2,1,0:T(8,128)S(1)}, f32[7,2,16,128]{3,2,1,0:T(8,128)S(1)}, u32[]{:S(2)}, u32[]{:S(2)}) collective-permute-start(f32[7,2,16,128]{3,2,1,0:T(8,128)S(1)} %get-tuple-element.11), channel_id=1, source_target_pairs={{0,2},{2,4},{4,6},{6,8},{8,10},{10,12},{12,14},{14,16},{16,18},{18... | collective-permute-start | bytes 344072 | tf_op jit(solution)/shard_map/ppermute | solution.py:367
  21.9 0.0 collective-permute-done.across
  21.9 4.6 %collective-permute-start.2 = (f32[2,7,4,16,128]{4,3,2,1,0:T(8,128)S(1)}, f32[2,7,4,16,128]{4,3,2,1,0:T(8,128)S(1)}, u32[]{:S(2)}, u32[]{:S(2)}) collective-permute-start(f32[2,7,4,16,128]{4,3,2,1,0:T(8,128)S(1)} %choose.1), channel_id=1, source_target_pairs={{0,1},{1,0},{2,3},{3,2},{4,5},{5,4},{6,7},{7,6},{8,9},{9,8},{10,11... | collective-permute-start | bytes 1376264 | tf_op jit(solution)/shard_map/ppermute | solution.py:370
  26.5 3.5 %all-to-all-done.received = f32[64,2,128]{2,1,0:T(2,128)S(1)} async-done(((f32[64,2,128]{2,1,0:T(2,128)}), f32[64,2,128]{2,1,0:T(2,128)S(1)}, u32[]{:S(2)}, u32[]{:S(2)}) %all-to-all-start) | async-done | bytes 65568 | tf_op jit(solution)/shard_map/all_to_all | solution.py:368
  30.0 0.8 %spread.1.sums = f32[7,10,16,128]{3,2,1,0:T(8,128)S(1)} custom-call(f32[64,2,128]{2,1,0:T(2,128)S(1)} %all-to-all-done.received), custom_call_target="tpu_custom_call" | custom-call | flops 10000000000 | bytes 1000000000 | tf_op jit(solution)/shard_map/spread/pallas_call | solution.py:329
  30.9 0.0 collective-permute-done.1.edge
  30.9 0.0 collective-permute-done.2.other
  30.9 1.3 %forward.1 = (f32[6,10,16,128]{3,2,1,0:T(8,128)S(1)}, f32[2,10,16,128]{3,2,1,0:T(8,128)S(1)}) custom-call(f32[1]{0:T(128)S(6)} %copy.8.factor, f32[7,4,16,128]{3,2,1,0:T(8,128)S(1)} %get-tuple-element.10.own, f32[7,4,16,128]{3,2,1,0:T(8,128)S(1)} %collective-permute-done.across, f32[7,2,16,128]{3,2,1,0:T(8,128)S(1)} %collective-permute-done.1.edge, ...), custom_call_target="tpu_custom_call" | custom-call | flops 1000000 | bytes 1000000 | tf_op jit(solution)/shard_map/forward/pallas_call | solution.py:315
  32.2 0.7 %adjoint.1 = (f32[8,64,128]{2,1,0:T(8,128)S(1)}, f32[1,6,4,16,128]{4,3,2,1,0:T(8,128)}) custom-call(f32[1]{0:T(128)S(6)} %copy.8.factor, f32[7,10,16,128]{3,2,1,0:T(8,128)S(1)} %spread.1.sums, f32[6,10,16,128]{3,2,1,0:T(8,128)S(1)} %get-tuple-element.12.near, f32[2,10,16,128]{3,2,1,0:T(8,128)S(1)} %get-tuple-element.13.pq), custom_call_target="tpu_custom_call" | custom-call | flops 10000000 | bytes 1000000 | tf_op jit(solution)/shard_map/adjoint/pallas_call | solution.py:347
  32.9 17.6 %all_to_all.10 = f32[8,64,128]{2,1,0:T(8,128)S(1)} all-to-all(f32[8,64,128]{2,1,0:T(8,128)S(1)} %get-tuple-element.15), channel_id=1, replica_groups=mesh['freq'=8,'tile'=64] {'freq'}, dimensions={0} | all-to-all | bytes 524288 | tf_op jit(solution)/shard_map/all_to_all | solution.py:374
  50.4 0.6 %reduce_sum.9 = f32[64,128]{1,0:T(8,128)} reduce(f32[8,64,128]{2,1,0:T(8,128)S(1)} %all_to_all.10, f32[]{:T(128)} %constant.0.clone.1), dimensions={0}, to_apply=%region_0.0 | reduce | flops 57344 | bytes 294916 | tf_op jit(solution)/shard_map/reduce_sum | solution.py:375
  (1 shorter events, 0.0 us)
Async XLA Ops:
  2.6 19.3 %collective-permute-start = (f32[7,4,16,128]{3,2,1,0:T(8,128)S(1)}, f32[7,4,16,128]{3,2,1,0:T(8,128)S(1)}, u32[]{:S(2)}, u32[]{:S(2)}) collective-permute-start(f32[7,4,16,128]{3,2,1,0:T(8,128)S(1)} %get-tuple-element.10.own), channel_id=1, source_target_pairs={{2,0},{4,2},{6,4},{8,6},{10,8},{12,10},{14,12},{16,14},{18,16},{20... | collective-permute-start | bytes 688136 | tf_op jit(solution)/shard_map/ppermute | solution.py:366
  6.6 23.5 %all-to-all-start = ((f32[64,2,128]{2,1,0:T(2,128)}), f32[64,2,128]{2,1,0:T(2,128)S(1)}, u32[]{:S(2)}, u32[]{:S(2)}) async-start(f32[64,2,128]{2,1,0:T(2,128)} %get-tuple-element.9), calls=%async_computation | async-start | bytes 131072 | tf_op jit(solution)/shard_map/all_to_all | solution.py:368
  19.9 10.9 %collective-permute-start.1 = (f32[7,2,16,128]{3,2,1,0:T(8,128)S(1)}, f32[7,2,16,128]{3,2,1,0:T(8,128)S(1)}, u32[]{:S(2)}, u32[]{:S(2)}) collective-permute-start(f32[7,2,16,128]{3,2,1,0:T(8,128)S(1)} %get-tuple-element.11), channel_id=1, source_target_pairs={{0,2},{2,4},{4,6},{6,8},{8,10},{10,12},{12,14},{14,16},{16,18},{18... | collective-permute-start | bytes 344072 | tf_op jit(solution)/shard_map/ppermute | solution.py:367
  21.9 8.9 %collective-permute-start.2 = (f32[2,7,4,16,128]{4,3,2,1,0:T(8,128)S(1)}, f32[2,7,4,16,128]{4,3,2,1,0:T(8,128)S(1)}, u32[]{:S(2)}, u32[]{:S(2)}) collective-permute-start(f32[2,7,4,16,128]{4,3,2,1,0:T(8,128)S(1)} %choose.1), channel_id=1, source_target_pairs={{0,1},{1,0},{2,3},{3,2},{4,5},{5,4},{6,7},{7,6},{8,9},{9,8},{10,11... | collective-permute-start | bytes 1376264 | tf_op jit(solution)/shard_map/ppermute | solution.py:370

commit v6 on v5

--- a/solution.py
+++ b/solution.py
@@ -194,12 +194,16 @@
         old, new = new, old
 
 
-def choose_kernel(own, across, out):
+def choose_kernel(own, across, edge, out):
+    del edge
     out[0] = own[...]
     out[1] = across[...]
 
 
-def forward_kernel(factor, own, across, edge, other, near, near_pq, src, pq, one, two):
+def solve_kernel(
+    factor, sums, own, across, edge, other, terms, field, near, far_src, far_pq, far_one, far_two,
+    src, pq, one, two, written,
+):
     depth = own.shape[1]
     tile, tiles = lax.axis_index("tile"), lax.axis_size("tile")
     even = tile % 2 == 0
@@ -212,25 +216,21 @@
     absorbs = []
     for layer, (first, at, second, there) in enumerate(views):
         if first is second:
-            src[:, layer] = first[:6, at]
+            far_src[:, layer] = first[:6, at]
             absorbs.append(factor[0] * first[6, at])
         else:
-            src[:, layer] = jnp.where(even, first[:6, at], second[:6, there])
+            far_src[:, layer] = jnp.where(even, first[:6, at], second[:6, there])
             absorbs.append(factor[0] * jnp.where(even, first[6, at], second[6, there]))
-    coefficients(absorbs, pq, tile, tiles)
-    near_pq[...] = pq[:, HALO:-HALO]
-
-    def emit(layer, results):
+    coefficients(absorbs, far_pq, tile, tiles)
+    pq[...] = far_pq[:, HALO:-HALO]
+
+    def keep(layer, results):
         for part, (re, im) in enumerate(results):
             near[part, layer - HALO] = re
             near[part + 3, layer - HALO] = im
 
-    relax(src, pq, one, two, emit)
-
-
-def adjoint_kernel(factor, sums, near, pq, terms, field, src, one, two, left):
-    depth = near.shape[1] - 2 * HALO
-    copy = pltpu.make_async_copy(near.at[:, pl.ds(HALO, depth)], field.at[0], left)
+    relax(far_src, far_pq, far_one, far_two, keep)
+    copy = pltpu.make_async_copy(near.at[:, pl.ds(HALO, depth)], field.at[0], written)
     copy.start()
     for part in range(6):
         src[part] = sums[6] * near[part] - sums[part]
@@ -250,7 +250,12 @@
 
 def working(layers):
     buffer = pltpu.VMEM((6, layers * PITCH + 8, LANES), jnp.float32)
-    return [pltpu.VMEM((6, layers, 16, LANES), jnp.float32), buffer, buffer]
+    return [
+        pltpu.VMEM((6, layers, 16, LANES), jnp.float32),
+        pltpu.VMEM((2, layers, 16, LANES), jnp.float32),
+        buffer,
+        buffer,
+    ]
 
 
 def shape(*dims):
@@ -297,31 +302,16 @@
     )
 
 
-def choose(own, across):
+def choose(own, across, edge):
     return pl.pallas_call(
         choose_kernel,
         out_shape=shape(2, *own.shape),
-        in_specs=[VMEM] * 2,
+        in_specs=[VMEM] * 3,
         out_specs=VMEM,
         compiler_params=LIMIT,
         cost_estimate=cost(10**10, 10**9),
         name="choose",
-    )(own, across)
-
-
-def forward(factor, own, across, edge, other):
-    depth, ny, nz = own.shape[1:]
-    wide, layers = depth + 4 * HALO, depth + 2 * HALO
-    return pl.pallas_call(
-        forward_kernel,
-        out_shape=(shape(6, layers, ny, nz), shape(2, layers, ny, nz)),
-        in_specs=[SMEM] + [VMEM] * 4,
-        out_specs=(VMEM, VMEM),
-        scratch_shapes=[working(wide)[0], pltpu.VMEM((2, wide, ny, nz), jnp.float32)] + working(wide)[1:],
-        compiler_params=LIMIT,
-        cost_estimate=cost(10**6, 10**6),
-        name="forward",
-    )(factor, own, across, edge, other)
+    )(own, across, edge)
 
 
 def spread(received, depth, ny, nz):
@@ -341,19 +331,24 @@
     )(received)
 
 
-def adjoint(factor, sums, near, near_pq, freqs):
-    layers, ny, nz = near.shape[1:]
-    depth = layers - 2 * HALO
+def solve(factor, sums, own, across, edge, other, freqs):
+    depth, ny, nz = own.shape[1:]
+    wide, layers = depth + 4 * HALO, depth + 2 * HALO
     return pl.pallas_call(
-        adjoint_kernel,
+        solve_kernel,
         out_shape=(shape(freqs, depth * ny, nz), shape(1, 6, depth, ny, nz)),
-        in_specs=[SMEM] + [VMEM] * 3,
+        in_specs=[SMEM] + [VMEM] * 5,
         out_specs=(VMEM, HBM),
-        scratch_shapes=working(layers) + [pltpu.SemaphoreType.DMA],
+        scratch_shapes=[
+            pltpu.VMEM((6, layers, ny, nz), jnp.float32),
+            *working(wide),
+            *working(layers),
+            pltpu.SemaphoreType.DMA,
+        ],
         compiler_params=LIMIT,
         cost_estimate=cost(10**7, 10**6),
-        name="adjoint",
-    )(factor, sums, near, near_pq)
+        name="solve",
+    )(factor, sums, own, across, edge, other)
 
 
 def body(source, conductivity, freq_factor, observed, slot_cells, block_counts):
@@ -366,11 +361,10 @@
     across = lax.ppermute(own, "tile", down + [(i + 1, j + 1) for i, j in up])
     edge = lax.ppermute(near_edge, "tile", up + [(i + 1, j + 1) for i, j in down])
     received = lax.all_to_all(payload, "tile", split_axis=0, concat_axis=0, tiled=True)
-    chosen = choose(own, across)
+    chosen = choose(own, across, edge)
     other = lax.ppermute(chosen, "tile", [(i, i ^ 1) for i in range(tiles)])
-    near, near_pq = forward(freq_factor, own, across, edge, other)
     sums = spread(received, depth, ny, nz)
-    terms, field = adjoint(freq_factor, sums, near, near_pq, freqs)
+    terms, field = solve(freq_factor, sums, own, across, edge, other, freqs)
     terms = lax.all_to_all(terms, "freq", split_axis=0, concat_axis=0, tiled=True)
     gradient = jnp.sum(terms, axis=0).reshape(depth, ny, nz)
     return (field, gradient)

time: 51.4 us -> 56.6 us (1.10)
  waiting for transfers between devices: 3.54 us -> 7.02 us
  starting transfers between devices: 23.2 us -> 24.9 us
    all_to_all x1, starting transfers between devices: 13.4 us -> 17.3 us  [body(): lax.all_to_all(payload, 'tile', split_axis=0, concat_axis=0, tiled=True)]
    all_to_all x1, waiting for transfers between devices: 3.53 us -> 7.01 us  [body(): lax.all_to_all(payload, 'tile', split_axis=0, concat_axis=0, tiled=True)]
    ppermute x1, starting transfers between devices: 4.55 us -> 2.36 us  [body(): other = lax.ppermute(chosen, 'tile', [(i, i ^ 1) for i in range(tiles)])]
    pallas_call x2 -> x1, Pallas kernels: 1.97 us -> 1.96 us  [solve(): pl.pallas_call(solve_kernel, out_shape=(shape(freqs, depth * ny, nz), sha...]
where the time goes in v6:
time: 56.6 us; the launch traced here: 56.3 us
  starting transfers between devices  24.9 us (44%)
  blocking collectives  17.6 us (31%)
  waiting for transfers between devices  7.02 us (12%)
  Pallas kernels  4.78 us (8%)
  between operations  1.36 us (2%)
  other arithmetic  0.63 us (1%)
    all_to_all x1, blocking collectives, body(): lax.all_to_all(terms, 'freq', split_axis=0, concat_axis=0, tiled=True)  17.6 us
    all_to_all x1, starting transfers between devices, body(): lax.all_to_all(payload, 'tile', split_axis=0, concat_axis=0, tiled=True)  17.3 us
    all_to_all x1, waiting for transfers between devices, body(): lax.all_to_all(payload, 'tile', split_axis=0, concat_axis=0, tiled=True)  7.01 us
    ppermute x1, starting transfers between devices, body(): across = lax.ppermute(own, 'tile', down + [(i + 1, j + 1) for i, j in up])  3.96 us
    ppermute x1, starting transfers between devices, body(): other = lax.ppermute(chosen, 'tile', [(i, i ^ 1) for i in range(tiles)])  2.36 us
    pallas_call x1, Pallas kernels, solve(): pl.pallas_call(solve_kernel, out_shape=(shape(freqs, depth * ny, nz), sha...  1.96 us
    pallas_call x1, Pallas kernels, pack(): pl.pallas_call(pack_kernel, out_shape=(shape(7, depth, ny, nz), shape(7,...  1.95 us
    ppermute x1, starting transfers between devices, body(): lax.ppermute(near_edge, 'tile', up + [(i + 1, j + 1) for i, j in down])  1.29 us
  transfers between devices with their start and end apart: 4, of which 1 were waited for; matrix products, arithmetic and copies ran while one was open for 0% of the time, Pallas kernels for 2%

profile of v6, /device:TPU:1, one launch (start us, length us, event | category | flops | bytes accessed | tf_op | source)
XLA Modules:
  0.0 56.3 jit_solution(3663538956846536617)
XLA Ops:
  0.6 2.0 %pack.1 = (f32[7,4,16,128]{3,2,1,0:T(8,128)S(1)}, f32[7,2,16,128]{3,2,1,0:T(8,128)S(1)}, f32[64,2,128]{2,1,0:T(2,128)}) custom-call(f32[6,4,16,128]{3,2,1,0:T(8,128)} %source.1, f32[4,16,128]{2,1,0:T(8,128)} %cond.1, f32[6,1,512]{2,1,0:T(1,128)} %bitcast.5, s32[1,512]{1,0:T(1,128)} %bitcast.6, s32[1,64]{1,0:T(1,128)} %bitcast.7), custom_call_target="tpu_custom_call" | custom-call | flops 1000000 | bytes 1000000 | tf_op jit(solution)/shard_map/pack/pallas_call | solution.py:275
  2.6 4.0 %collective-permute-start = (f32[7,4,16,128]{3,2,1,0:T(8,128)S(1)}, f32[7,4,16,128]{3,2,1,0:T(8,128)S(1)}, u32[]{:S(2)}, u32[]{:S(2)}) collective-permute-start(f32[7,4,16,128]{3,2,1,0:T(8,128)S(1)} %get-tuple-element.8.own), channel_id=1, source_target_pairs={{2,0},{4,2},{6,4},{8,6},{10,8},{12,10},{14,12},{16,14},{18,16},{20... | collective-permute-start | bytes 688136 | tf_op jit(solution)/shard_map/ppermute | solution.py:361
  6.6 1.3 %collective-permute-start.1 = (f32[7,2,16,128]{3,2,1,0:T(8,128)S(1)}, f32[7,2,16,128]{3,2,1,0:T(8,128)S(1)}, u32[]{:S(2)}, u32[]{:S(2)}) collective-permute-start(f32[7,2,16,128]{3,2,1,0:T(8,128)S(1)} %get-tuple-element.9), channel_id=1, source_target_pairs={{0,2},{2,4},{4,6},{6,8},{8,10},{10,12},{12,14},{14,16},{16,18},{18... | collective-permute-start | bytes 344072 | tf_op jit(solution)/shard_map/ppermute | solution.py:362
  7.9 17.3 %all-to-all-start = ((f32[64,2,128]{2,1,0:T(2,128)}), f32[64,2,128]{2,1,0:T(2,128)S(1)}, u32[]{:S(2)}, u32[]{:S(2)}) async-start(f32[64,2,128]{2,1,0:T(2,128)} %get-tuple-element.7), calls=%async_computation | async-start | bytes 131072 | tf_op jit(solution)/shard_map/all_to_all | solution.py:363
  25.8 0.0 collective-permute-done.1.edge
  25.8 0.0 collective-permute-done.across
  25.8 2.4 %collective-permute-start.2 = (f32[2,7,4,16,128]{4,3,2,1,0:T(8,128)S(1)}, f32[2,7,4,16,128]{4,3,2,1,0:T(8,128)S(1)}, u32[]{:S(2)}, u32[]{:S(2)}) collective-permute-start(f32[2,7,4,16,128]{4,3,2,1,0:T(8,128)S(1)} %choose.1), channel_id=1, source_target_pairs={{0,1},{1,0},{2,3},{3,2},{4,5},{5,4},{6,7},{7,6},{8,9},{9,8},{10,11... | collective-permute-start | bytes 1376264 | tf_op jit(solution)/shard_map/ppermute | solution.py:365
  28.2 7.0 %all-to-all-done.received = f32[64,2,128]{2,1,0:T(2,128)S(1)} async-done(((f32[64,2,128]{2,1,0:T(2,128)}), f32[64,2,128]{2,1,0:T(2,128)S(1)}, u32[]{:S(2)}, u32[]{:S(2)}) %all-to-all-start) | async-done | bytes 65568 | tf_op jit(solution)/shard_map/all_to_all | solution.py:363
  35.2 0.8 %spread.1.sums = f32[7,10,16,128]{3,2,1,0:T(8,128)S(1)} custom-call(f32[64,2,128]{2,1,0:T(2,128)S(1)} %all-to-all-done.received), custom_call_target="tpu_custom_call" | custom-call | flops 10000000000 | bytes 1000000000 | tf_op jit(solution)/shard_map/spread/pallas_call | solution.py:319
  36.1 0.0 collective-permute-done.2.other
  36.1 2.0 %solve.1 = (f32[8,64,128]{2,1,0:T(8,128)S(1)}, f32[1,6,4,16,128]{4,3,2,1,0:T(8,128)}) custom-call(f32[1]{0:T(128)S(6)} %copy.8.factor, f32[7,10,16,128]{3,2,1,0:T(8,128)S(1)} %spread.1.sums, f32[7,4,16,128]{3,2,1,0:T(8,128)S(1)} %get-tuple-element.8.own, f32[7,4,16,128]{3,2,1,0:T(8,128)S(1)} %collective-permute-done.across, ...), custom_call_target="tpu_custom_call" | custom-call | flops 10000000 | bytes 1000000 | tf_op jit(solution)/shard_map/solve/pallas_call | solution.py:337
  38.0 17.6 %all_to_all.10 = f32[8,64,128]{2,1,0:T(8,128)S(1)} all-to-all(f32[8,64,128]{2,1,0:T(8,128)S(1)} %get-tuple-element.11), channel_id=1, replica_groups=mesh['freq'=8,'tile'=64] {'freq'}, dimensions={0} | all-to-all | bytes 524288 | tf_op jit(solution)/shard_map/all_to_all | solution.py:368
  55.7 0.6 %reduce_sum.9 = f32[64,128]{1,0:T(8,128)} reduce(f32[8,64,128]{2,1,0:T(8,128)S(1)} %all_to_all.10, f32[]{:T(128)} %constant.0.clone.1), dimensions={0}, to_apply=%region_0.0 | reduce | flops 57344 | bytes 294916 | tf_op jit(solution)/shard_map/reduce_sum | solution.py:369
  (1 shorter events, 0.0 us)
Async XLA Ops:
  2.6 23.2 %collective-permute-start = (f32[7,4,16,128]{3,2,1,0:T(8,128)S(1)}, f32[7,4,16,128]{3,2,1,0:T(8,128)S(1)}, u32[]{:S(2)}, u32[]{:S(2)}) collective-permute-start(f32[7,4,16,128]{3,2,1,0:T(8,128)S(1)} %get-tuple-element.8.own), channel_id=1, source_target_pairs={{2,0},{4,2},{6,4},{8,6},{10,8},{12,10},{14,12},{16,14},{18,16},{20... | collective-permute-start | bytes 688136 | tf_op jit(solution)/shard_map/ppermute | solution.py:361
  6.6 19.2 %collective-permute-start.1 = (f32[7,2,16,128]{3,2,1,0:T(8,128)S(1)}, f32[7,2,16,128]{3,2,1,0:T(8,128)S(1)}, u32[]{:S(2)}, u32[]{:S(2)}) collective-permute-start(f32[7,2,16,128]{3,2,1,0:T(8,128)S(1)} %get-tuple-element.9), channel_id=1, source_target_pairs={{0,2},{2,4},{4,6},{6,8},{8,10},{10,12},{12,14},{14,16},{16,18},{18... | collective-permute-start | bytes 344072 | tf_op jit(solution)/shard_map/ppermute | solution.py:362
  7.9 27.4 %all-to-all-start = ((f32[64,2,128]{2,1,0:T(2,128)}), f32[64,2,128]{2,1,0:T(2,128)S(1)}, u32[]{:S(2)}, u32[]{:S(2)}) async-start(f32[64,2,128]{2,1,0:T(2,128)} %get-tuple-element.7), calls=%async_computation | async-start | bytes 131072 | tf_op jit(solution)/shard_map/all_to_all | solution.py:363
  25.8 10.2 %collective-permute-start.2 = (f32[2,7,4,16,128]{4,3,2,1,0:T(8,128)S(1)}, f32[2,7,4,16,128]{4,3,2,1,0:T(8,128)S(1)}, u32[]{:S(2)}, u32[]{:S(2)}) collective-permute-start(f32[2,7,4,16,128]{4,3,2,1,0:T(8,128)S(1)} %choose.1), channel_id=1, source_target_pairs={{0,1},{1,0},{2,3},{3,2},{4,5},{5,4},{6,7},{7,6},{8,9},{9,8},{10,11... | collective-permute-start | bytes 1376264 | tf_op jit(solution)/shard_map/ppermute | solution.py:365

commit v7 on v5

--- a/solution.py
+++ b/solution.py
@@ -17,11 +17,9 @@
 
 
 def pack_kernel(
-    source, cond, observed, cells, counts, own, near_edge, payload,
+    source, cond, observed, cells, counts, own, payload,
     observed_in, cells_in, counts_in, values, columns, arrived,
 ):
-    core = lax.axis_index("tile") % 2
-    edge = pl.ds(2 * (1 - core), 2)
     copies = [
         pltpu.make_async_copy(start, end, arrived.at[i])
         for i, (start, end) in enumerate(
@@ -30,9 +28,7 @@
                 (cells, cells_in),
                 (counts, counts_in),
                 (cond, own.at[6]),
-                (cond.at[edge], near_edge.at[6]),
                 (source, own.at[pl.ds(0, 6)]),
-                (source.at[:, edge], near_edge.at[pl.ds(0, 6)]),
             )
         )
     ]
@@ -199,7 +195,13 @@
     out[1] = across[...]
 
 
-def forward_kernel(factor, own, across, edge, other, near, near_pq, src, pq, one, two):
+def edge_kernel(factor, own, near_edge, absorb):
+    core = lax.axis_index("tile") % 2
+    near_edge[...] = own[:, pl.ds(2 * (1 - core), 2)]
+    absorb[...] = factor[0] * own[6]
+
+
+def forward_kernel(factor, absorb, own, across, edge, other, near, near_pq, src, pq, one, two):
     depth = own.shape[1]
     tile, tiles = lax.axis_index("tile"), lax.axis_size("tile")
     even = tile % 2 == 0
@@ -213,7 +215,7 @@
     for layer, (first, at, second, there) in enumerate(views):
         if first is second:
             src[:, layer] = first[:6, at]
-            absorbs.append(factor[0] * first[6, at])
+            absorbs.append(absorb[at])
         else:
             src[:, layer] = jnp.where(even, first[:6, at], second[:6, there])
             absorbs.append(factor[0] * jnp.where(even, first[6, at], second[6, there]))
@@ -269,16 +271,16 @@
     slots, tiles = slot_cells.shape[0], block_counts.shape[0]
     return pl.pallas_call(
         pack_kernel,
-        out_shape=(shape(7, depth, ny, nz), shape(7, 2, ny, nz), shape(tiles, 2, LANES)),
+        out_shape=(shape(7, depth, ny, nz), shape(tiles, 2, LANES)),
         in_specs=[HBM] * 5,
-        out_specs=(VMEM, VMEM, VMEM),
+        out_specs=(VMEM, VMEM),
         scratch_shapes=[
             pltpu.VMEM((6, 1, slots), jnp.float32),
             pltpu.VMEM((1, slots), jnp.int32),
             pltpu.VMEM((1, tiles), jnp.int32),
             pltpu.VMEM((ROWS, slots), jnp.float32),
             pltpu.VMEM((slots + 2 * (slots // tiles), LANES), jnp.float32),
-            pltpu.SemaphoreType.DMA((7,)),
+            pltpu.SemaphoreType.DMA((5,)),
         ],
         compiler_params=LIMIT,
         cost_estimate=cost(10**6, 10**6),
@@ -309,19 +311,32 @@
     )(own, across)
 
 
-def forward(factor, own, across, edge, other):
+def edges(factor, own):
+    parts, depth, ny, nz = own.shape
+    return pl.pallas_call(
+        edge_kernel,
+        out_shape=(shape(parts, 2, ny, nz), shape(depth, ny, nz)),
+        in_specs=[SMEM, VMEM],
+        out_specs=(VMEM, VMEM),
+        compiler_params=LIMIT,
+        cost_estimate=cost(10**10, 10**9),
+        name="edges",
+    )(factor, own)
+
+
+def forward(factor, absorb, own, across, edge, other):
     depth, ny, nz = own.shape[1:]
     wide, layers = depth + 4 * HALO, depth + 2 * HALO
     return pl.pallas_call(
         forward_kernel,
         out_shape=(shape(6, layers, ny, nz), shape(2, layers, ny, nz)),
-        in_specs=[SMEM] + [VMEM] * 4,
+        in_specs=[SMEM] + [VMEM] * 5,
         out_specs=(VMEM, VMEM),
         scratch_shapes=[working(wide)[0], pltpu.VMEM((2, wide, ny, nz), jnp.float32)] + working(wide)[1:],
         compiler_params=LIMIT,
         cost_estimate=cost(10**6, 10**6),
         name="forward",
-    )(factor, own, across, edge, other)
+    )(factor, absorb, own, across, edge, other)
 
 
 def spread(received, depth, ny, nz):
@@ -359,16 +374,17 @@
 def body(source, conductivity, freq_factor, observed, slot_cells, block_counts):
     tiles, freqs = lax.axis_size("tile"), lax.axis_size("freq")
     depth, ny, nz = conductivity.shape
-    own, near_edge, payload = pack(source, conductivity, observed, slot_cells, block_counts)
+    own, payload = pack(source, conductivity, observed, slot_cells, block_counts)
     chips = tiles // 2
     up = [(2 * k, 2 * k + 2) for k in range(chips - 1)]
     down = [(2 * k + 2, 2 * k) for k in range(chips - 1)]
     across = lax.ppermute(own, "tile", down + [(i + 1, j + 1) for i, j in up])
+    near_edge, absorb = edges(freq_factor, own)
     edge = lax.ppermute(near_edge, "tile", up + [(i + 1, j + 1) for i, j in down])
     received = lax.all_to_all(payload, "tile", split_axis=0, concat_axis=0, tiled=True)
     chosen = choose(own, across)
     other = lax.ppermute(chosen, "tile", [(i, i ^ 1) for i in range(tiles)])
-    near, near_pq = forward(freq_factor, own, across, edge, other)
+    near, near_pq = forward(freq_factor, absorb, own, across, edge, other)
     sums = spread(received, depth, ny, nz)
     terms, field = adjoint(freq_factor, sums, near, near_pq, freqs)
     terms = lax.all_to_all(terms, "freq", split_axis=0, concat_axis=0, tiled=True)

time: 51.4 us -> 52.2 us (1.016)
  the two profiles are of different devices: /device:TPU:1 before, /device:TPU:6 now
where the time goes in v7:
time: 52.2 us; the launch traced here: 51.9 us
  starting transfers between devices  23.7 us (45%)
  blocking collectives  19.1 us (37%)
  Pallas kernels  4.78 us (9%)
  waiting for transfers between devices  2.32 us (4%)
  between operations  1.37 us (3%)
  other arithmetic  0.63 us (1%)
    all_to_all x1, blocking collectives, body(): lax.all_to_all(terms, 'freq', split_axis=0, concat_axis=0, tiled=True)  19.1 us
    all_to_all x1, starting transfers between devices, body(): lax.all_to_all(payload, 'tile', split_axis=0, concat_axis=0, tiled=True)  13.8 us
    ppermute x1, starting transfers between devices, body(): lax.ppermute(near_edge, 'tile', up + [(i + 1, j + 1) for i, j in down])  5.19 us
    ppermute x1, starting transfers between devices, body(): across = lax.ppermute(own, 'tile', down + [(i + 1, j + 1) for i, j in up])  2.76 us
    pallas_call x1, Pallas kernels, pack(): pl.pallas_call(pack_kernel, out_shape=(shape(7, depth, ny, nz), shape(til...  1.93 us
    ppermute x1, starting transfers between devices, body(): other = lax.ppermute(chosen, 'tile', [(i, i ^ 1) for i in range(tiles)])  1.92 us
    ppermute x1, waiting for transfers between devices, body(): across = lax.ppermute(own, 'tile', down + [(i + 1, j + 1) for i, j in up])  1.4 us
    pallas_call x1, Pallas kernels, forward(): pl.pallas_call(forward_kernel, out_shape=(shape(6, layers, ny, nz), shape...  1.25 us
  transfers between devices with their start and end apart: 4, of which 2 were waited for; matrix products, arithmetic and copies ran while one was open for 0% of the time, Pallas kernels for 2%

profile of v7, /device:TPU:6, one launch (start us, length us, event | category | flops | bytes accessed | tf_op | source)
XLA Modules:
  0.0 51.9 jit_solution(8671527270762013779)
XLA Ops:
  0.6 1.9 %pack.1 = (f32[7,4,16,128]{3,2,1,0:T(8,128)S(1)}, f32[64,2,128]{2,1,0:T(2,128)}) custom-call(f32[6,4,16,128]{3,2,1,0:T(8,128)} %source.1, f32[4,16,128]{2,1,0:T(8,128)} %cond.1, f32[6,1,512]{2,1,0:T(1,128)} %bitcast.5, s32[1,512]{1,0:T(1,128)} %bitcast.6, s32[1,64]{1,0:T(1,128)} %bitcast.7), custom_call_target="tpu_custom_call" | custom-call | flops 1000000 | bytes 1000000 | tf_op jit(solution)/shard_map/pack/pallas_call | solution.py:272
  2.6 13.8 %all-to-all-start = ((f32[64,2,128]{2,1,0:T(2,128)}), f32[64,2,128]{2,1,0:T(2,128)S(1)}, u32[]{:S(2)}, u32[]{:S(2)}) async-start(f32[64,2,128]{2,1,0:T(2,128)} %get-tuple-element.10), calls=%async_computation | async-start | bytes 131072 | tf_op jit(solution)/shard_map/all_to_all | solution.py:384
  16.4 2.8 %collective-permute-start = (f32[7,4,16,128]{3,2,1,0:T(8,128)S(1)}, f32[7,4,16,128]{3,2,1,0:T(8,128)S(1)}, u32[]{:S(2)}, u32[]{:S(2)}) collective-permute-start(f32[7,4,16,128]{3,2,1,0:T(8,128)S(1)} %get-tuple-element.11.own), channel_id=1, source_target_pairs={{2,0},{4,2},{6,4},{8,6},{10,8},{12,10},{14,12},{16,14},{18,16},{20... | collective-permute-start | bytes 688136 | tf_op jit(solution)/shard_map/ppermute | solution.py:381
  19.9 5.2 %collective-permute-start.1 = (f32[7,2,16,128]{3,2,1,0:T(8,128)S(1)}, f32[7,2,16,128]{3,2,1,0:T(8,128)S(1)}, u32[]{:S(2)}, u32[]{:S(2)}) collective-permute-start(f32[7,2,16,128]{3,2,1,0:T(8,128)S(1)} %get-tuple-element.13), channel_id=1, source_target_pairs={{0,2},{2,4},{4,6},{6,8},{8,10},{10,12},{12,14},{14,16},{16,18},{18... | collective-permute-start | bytes 344072 | tf_op jit(solution)/shard_map/ppermute | solution.py:383
  25.0 1.4 %collective-permute-done.across = f32[7,4,16,128]{3,2,1,0:T(8,128)S(1)} collective-permute-done((f32[7,4,16,128]{3,2,1,0:T(8,128)S(1)}, f32[7,4,16,128]{3,2,1,0:T(8,128)S(1)}, u32[]{:S(2)}, u32[]{:S(2)}) %collective-permute-start) | collective-permute-done | bytes 229408 | tf_op jit(solution)/shard_map/ppermute | solution.py:381
  26.5 1.9 %collective-permute-start.2 = (f32[2,7,4,16,128]{4,3,2,1,0:T(8,128)S(1)}, f32[2,7,4,16,128]{4,3,2,1,0:T(8,128)S(1)}, u32[]{:S(2)}, u32[]{:S(2)}) collective-permute-start(f32[2,7,4,16,128]{4,3,2,1,0:T(8,128)S(1)} %choose.1), channel_id=1, source_target_pairs={{0,1},{1,0},{2,3},{3,2},{4,5},{5,4},{6,7},{7,6},{8,9},{9,8},{10,11... | collective-permute-start | bytes 1376264 | tf_op jit(solution)/shard_map/ppermute | solution.py:386
  28.4 0.0 all-to-all-done.received
  28.4 0.8 %spread.1.sums = f32[7,10,16,128]{3,2,1,0:T(8,128)S(1)} custom-call(f32[64,2,128]{2,1,0:T(2,128)S(1)} %all-to-all-done.received), custom_call_target="tpu_custom_call" | custom-call | flops 10000000000 | bytes 1000000000 | tf_op jit(solution)/shard_map/spread/pallas_call | solution.py:344
  29.3 0.0 collective-permute-done.1.edge
  29.3 0.9 %collective-permute-done.2.other = f32[2,7,4,16,128]{4,3,2,1,0:T(8,128)S(1)} collective-permute-done((f32[2,7,4,16,128]{4,3,2,1,0:T(8,128)S(1)}, f32[2,7,4,16,128]{4,3,2,1,0:T(8,128)S(1)}, u32[]{:S(2)}, u32[]{:S(2)}) %collective-permute-start.2) | collective-permute-done | bytes 458784 | tf_op jit(solution)/shard_map/ppermute | solution.py:386
  30.2 1.2 %forward.1 = (f32[6,10,16,128]{3,2,1,0:T(8,128)S(1)}, f32[2,10,16,128]{3,2,1,0:T(8,128)S(1)}) custom-call(f32[1]{0:T(128)S(6)} %copy.8.factor, f32[4,16,128]{2,1,0:T(8,128)S(1)} %get-tuple-element.12.absorb, f32[7,4,16,128]{3,2,1,0:T(8,128)S(1)} %get-tuple-element.11.own, f32[7,4,16,128]{3,2,1,0:T(8,128)S(1)} %collective-permute-done.across, ...), custom_call_target="tpu_custom_call" | custom-call | flops 1000000 | bytes 1000000 | tf_op jit(solution)/shard_map/forward/pallas_call | solution.py:330
  31.4 0.7 %adjoint.1 = (f32[8,64,128]{2,1,0:T(8,128)S(1)}, f32[1,6,4,16,128]{4,3,2,1,0:T(8,128)}) custom-call(f32[1]{0:T(128)S(6)} %copy.8.factor, f32[7,10,16,128]{3,2,1,0:T(8,128)S(1)} %spread.1.sums, f32[6,10,16,128]{3,2,1,0:T(8,128)S(1)} %get-tuple-element.14.near, f32[2,10,16,128]{3,2,1,0:T(8,128)S(1)} %get-tuple-element.15.pq), custom_call_target="tpu_custom_call" | custom-call | flops 10000000 | bytes 1000000 | tf_op jit(solution)/shard_map/adjoint/pallas_call | solution.py:362
  32.2 19.1 %all_to_all.10 = f32[8,64,128]{2,1,0:T(8,128)S(1)} all-to-all(f32[8,64,128]{2,1,0:T(8,128)S(1)} %get-tuple-element.17), channel_id=1, replica_groups=mesh['freq'=8,'tile'=64] {'freq'}, dimensions={0} | all-to-all | bytes 524288 | tf_op jit(solution)/shard_map/all_to_all | solution.py:390
  51.2 0.6 %reduce_sum.9 = f32[64,128]{1,0:T(8,128)} reduce(f32[8,64,128]{2,1,0:T(8,128)S(1)} %all_to_all.10, f32[]{:T(128)} %constant.0.clone.1), dimensions={0}, to_apply=%region_0.0 | reduce | flops 57344 | bytes 294916 | tf_op jit(solution)/shard_map/reduce_sum | solution.py:391
  (2 shorter events, 0.1 us)
Async XLA Ops:
  2.6 25.8 %all-to-all-start = ((f32[64,2,128]{2,1,0:T(2,128)}), f32[64,2,128]{2,1,0:T(2,128)S(1)}, u32[]{:S(2)}, u32[]{:S(2)}) async-start(f32[64,2,128]{2,1,0:T(2,128)} %get-tuple-element.10), calls=%async_computation | async-start | bytes 131072 | tf_op jit(solution)/shard_map/all_to_all | solution.py:384
  16.4 10.0 %collective-permute-start = (f32[7,4,16,128]{3,2,1,0:T(8,128)S(1)}, f32[7,4,16,128]{3,2,1,0:T(8,128)S(1)}, u32[]{:S(2)}, u32[]{:S(2)}) collective-permute-start(f32[7,4,16,128]{3,2,1,0:T(8,128)S(1)} %get-tuple-element.11.own), channel_id=1, source_target_pairs={{2,0},{4,2},{6,4},{8,6},{10,8},{12,10},{14,12},{16,14},{18,16},{20... | collective-permute-start | bytes 688136 | tf_op jit(solution)/shard_map/ppermute | solution.py:381
  19.9 9.4 %collective-permute-start.1 = (f32[7,2,16,128]{3,2,1,0:T(8,128)S(1)}, f32[7,2,16,128]{3,2,1,0:T(8,128)S(1)}, u32[]{:S(2)}, u32[]{:S(2)}) collective-permute-start(f32[7,2,16,128]{3,2,1,0:T(8,128)S(1)} %get-tuple-element.13), channel_id=1, source_target_pairs={{0,2},{2,4},{4,6},{6,8},{8,10},{10,12},{12,14},{14,16},{16,18},{18... | collective-permute-start | bytes 344072 | tf_op jit(solution)/shard_map/ppermute | solution.py:383
  26.5 3.7 %collective-permute-start.2 = (f32[2,7,4,16,128]{4,3,2,1,0:T(8,128)S(1)}, f32[2,7,4,16,128]{4,3,2,1,0:T(8,128)S(1)}, u32[]{:S(2)}, u32[]{:S(2)}) collective-permute-start(f32[2,7,4,16,128]{4,3,2,1,0:T(8,128)S(1)} %choose.1), channel_id=1, source_target_pairs={{0,1},{1,0},{2,3},{3,2},{4,5},{5,4},{6,7},{7,6},{8,9},{9,8},{10,11... | collective-permute-start | bytes 1376264 | tf_op jit(solution)/shard_map/ppermute | solution.py:386

commit v8 on v5

--- a/solution.py
+++ b/solution.py
@@ -69,7 +69,7 @@
         copy.wait()
 
 
-def spread_kernel(received, out, left, right):
+def spread_kernel(received, near, out, left, right):
     tiles = received.shape[0]
     turned = []
     for plane in range(2):
@@ -105,14 +105,16 @@
         sums = lax.dot_general(
             left[group], right[group], (((1,), (1,)), ((), ())), preferred_element_type=jnp.float32
         )
-        for name in range(7):
-            total = sums[name * half:(name + 1) * half]
-            if name < 6:
-                total = total + sums[(7 + name) * half:(8 + name) * half]
-                total = total + sums[(13 + name) * half:(14 + name) * half]
-            for index in range(layers):
-                side, at = divmod((first + index) * layer, half)
-                out[name, where + index] = total[at:at + layer, side * LANES:(side + 1) * LANES]
+        for index in range(layers):
+            side, at = divmod((first + index) * layer, half)
+            columns = slice(side * LANES, (side + 1) * LANES)
+            count = sums[6 * half + at:6 * half + at + layer, columns]
+            for name in range(6):
+                total = 0.0
+                for part in (0, 7, 13):
+                    row = (part + name) * half + at
+                    total = total + sums[row:row + layer, columns]
+                out[name, where + index] = count * near[name, where + index] - total
 
 
 PITCH = 24
@@ -199,7 +201,11 @@
     out[1] = across[...]
 
 
-def forward_kernel(factor, own, across, edge, other, near, near_pq, src, pq, one, two):
+def absorb_kernel(factor, own, absorb):
+    absorb[...] = factor[0] * own[6]
+
+
+def forward_kernel(factor, absorb, own, across, edge, other, near, near_pq, src, pq, one, two):
     depth = own.shape[1]
     tile, tiles = lax.axis_index("tile"), lax.axis_size("tile")
     even = tile % 2 == 0
@@ -209,14 +215,20 @@
     views += [(own, i, own, i) for i in range(depth)]
     views += [(mine, i, theirs, i) for i in range(depth)]
     views += [(across, i, edge, i) for i in range(2)]
+
+    def absorption(view, at):
+        if view is not own:
+            return factor[0] * view[6, at]
+        return absorb[at]
+
     absorbs = []
     for layer, (first, at, second, there) in enumerate(views):
         if first is second:
             src[:, layer] = first[:6, at]
-            absorbs.append(factor[0] * first[6, at])
+            absorbs.append(absorption(first, at))
         else:
             src[:, layer] = jnp.where(even, first[:6, at], second[:6, there])
-            absorbs.append(factor[0] * jnp.where(even, first[6, at], second[6, there]))
+            absorbs.append(jnp.where(even, absorption(first, at), absorption(second, there)))
     coefficients(absorbs, pq, tile, tiles)
     near_pq[...] = pq[:, HALO:-HALO]
 
@@ -228,12 +240,10 @@
     relax(src, pq, one, two, emit)
 
 
-def adjoint_kernel(factor, sums, near, pq, terms, field, src, one, two, left):
+def adjoint_kernel(factor, src, near, pq, terms, field, one, two, left):
     depth = near.shape[1] - 2 * HALO
     copy = pltpu.make_async_copy(near.at[:, pl.ds(HALO, depth)], field.at[0], left)
     copy.start()
-    for part in range(6):
-        src[part] = sums[6] * near[part] - sums[part]
 
     def emit(layer, results):
         total = 0.0
@@ -309,27 +319,42 @@
     )(own, across)
 
 
-def forward(factor, own, across, edge, other):
+def absorption(factor, own):
+    parts, depth, ny, nz = own.shape
+    return pl.pallas_call(
+        absorb_kernel,
+        out_shape=shape(depth, ny, nz),
+        in_specs=[SMEM, VMEM],
+        out_specs=VMEM,
+        compiler_params=LIMIT,
+        cost_estimate=cost(10**10, 10**9),
+        name="absorb",
+    )(factor, own)
+
+
+def forward(factor, absorb, own, across, edge, other):
     depth, ny, nz = own.shape[1:]
     wide, layers = depth + 4 * HALO, depth + 2 * HALO
     return pl.pallas_call(
         forward_kernel,
         out_shape=(shape(6, layers, ny, nz), shape(2, layers, ny, nz)),
-        in_specs=[SMEM] + [VMEM] * 4,
+        in_specs=[SMEM] + [VMEM] * 5,
         out_specs=(VMEM, VMEM),
         scratch_shapes=[working(wide)[0], pltpu.VMEM((2, wide, ny, nz), jnp.float32)] + working(wide)[1:],
         compiler_params=LIMIT,
         cost_estimate=cost(10**6, 10**6),
         name="forward",
-    )(factor, own, across, edge, other)
-
-
-def spread(received, depth, ny, nz):
+    )(factor, absorb, own, across, edge, other)
+
+
+def spread(received, near):
+    layers, ny, nz = near.shape[1:]
+    depth = layers - 2 * HALO
     slots = received.shape[0] * received.shape[2] // (2 * ROWS)
     return pl.pallas_call(
         spread_kernel,
-        out_shape=shape(7, depth + 2 * HALO, ny, nz),
-        in_specs=[VMEM],
+        out_shape=shape(*near.shape),
+        in_specs=[VMEM] * 2,
         out_specs=VMEM,
         scratch_shapes=[
             pltpu.VMEM((3, 19 * depth * ny // 2, slots), jnp.bfloat16),
@@ -338,10 +363,10 @@
         compiler_params=LIMIT,
         cost_estimate=cost(10**10, 10**9),
         name="spread",
-    )(received)
-
-
-def adjoint(factor, sums, near, near_pq, freqs):
+    )(received, near)
+
+
+def adjoint(factor, adjoint_source, near, near_pq, freqs):
     layers, ny, nz = near.shape[1:]
     depth = layers - 2 * HALO
     return pl.pallas_call(
@@ -349,11 +374,11 @@
         out_shape=(shape(freqs, depth * ny, nz), shape(1, 6, depth, ny, nz)),
         in_specs=[SMEM] + [VMEM] * 3,
         out_specs=(VMEM, HBM),
-        scratch_shapes=working(layers) + [pltpu.SemaphoreType.DMA],
+        scratch_shapes=working(layers)[1:] + [pltpu.SemaphoreType.DMA],
         compiler_params=LIMIT,
         cost_estimate=cost(10**7, 10**6),
         name="adjoint",
-    )(factor, sums, near, near_pq)
+    )(factor, adjoint_source, near, near_pq)
 
 
 def body(source, conductivity, freq_factor, observed, slot_cells, block_counts):
@@ -368,9 +393,10 @@
     received = lax.all_to_all(payload, "tile", split_axis=0, concat_axis=0, tiled=True)
     chosen = choose(own, across)
     other = lax.ppermute(chosen, "tile", [(i, i ^ 1) for i in range(tiles)])
-    near, near_pq = forward(freq_factor, own, across, edge, other)
-    sums = spread(received, depth, ny, nz)
-    terms, field = adjoint(freq_factor, sums, near, near_pq, freqs)
+    absorb = absorption(freq_factor, own)
+    near, near_pq = forward(freq_factor, absorb, own, across, edge, other)
+    adjoint_source = spread(received, near)
+    terms, field = adjoint(freq_factor, adjoint_source, near, near_pq, freqs)
     terms = lax.all_to_all(terms, "freq", split_axis=0, concat_axis=0, tiled=True)
     gradient = jnp.sum(terms, axis=0).reshape(depth, ny, nz)
     return (field, gradient)

time: 51.4 us -> 50.1 us (0.975)
  waiting for transfers between devices: 3.54 us -> 2.25 us
    all_to_all x1, waiting for transfers between devices: 3.53 us -> 0.85 us  [body(): lax.all_to_all(payload, 'tile', split_axis=0, concat_axis=0, tiled=True)]
    ppermute x1, waiting for transfers between devices: 0.01 us -> 1.4 us  [body(): other = lax.ppermute(chosen, 'tile', [(i, i ^ 1) for i in range(tiles)])]
  transfers between devices with their start and end apart: 4 -> 4, of which waited for: 1 -> 2; matrix products, arithmetic and copies ran while one was open for 0% -> 0% of each run, Pallas kernels for 2% -> 3%
where the time goes in v8:
time: 50.1 us; the launch traced here: 49.8 us
  starting transfers between devices  23.2 us (46%)
  blocking collectives  17.6 us (35%)
  Pallas kernels  4.77 us (10%)
  waiting for transfers between devices  2.25 us (4%)
  between operations  1.37 us (3%)
  other arithmetic  0.63 us (1%)
    all_to_all x1, blocking collectives, body(): lax.all_to_all(terms, 'freq', split_axis=0, concat_axis=0, tiled=True)  17.6 us
    all_to_all x1, starting transfers between devices, body(): lax.all_to_all(payload, 'tile', split_axis=0, concat_axis=0, tiled=True)  13.4 us
    ppermute x1, starting transfers between devices, body(): other = lax.ppermute(chosen, 'tile', [(i, i ^ 1) for i in range(tiles)])  4.55 us
    ppermute x1, starting transfers between devices, body(): across = lax.ppermute(own, 'tile', down + [(i + 1, j + 1) for i, j in up])  3.96 us
    pallas_call x1, Pallas kernels, pack(): pl.pallas_call(pack_kernel, out_shape=(shape(7, depth, ny, nz), shape(7,...  1.95 us
    ppermute x1, waiting for transfers between devices, body(): other = lax.ppermute(chosen, 'tile', [(i, i ^ 1) for i in range(tiles)])  1.4 us
    ppermute x1, starting transfers between devices, body(): lax.ppermute(near_edge, 'tile', up + [(i + 1, j + 1) for i, j in down])  1.29 us
    pallas_call x1, Pallas kernels, forward(): pl.pallas_call(forward_kernel, out_shape=(shape(6, layers, ny, nz), shape...  1.25 us
  transfers between devices with their start and end apart: 4, of which 2 were waited for; matrix products, arithmetic and copies ran while one was open for 0% of the time, Pallas kernels for 3%

profile of v8, /device:TPU:1, one launch (start us, length us, event | category | flops | bytes accessed | tf_op | source)
XLA Modules:
  0.0 49.8 jit_solution(10839395633011291255)
XLA Ops:
  0.6 2.0 %pack.1 = (f32[7,4,16,128]{3,2,1,0:T(8,128)S(1)}, f32[7,2,16,128]{3,2,1,0:T(8,128)S(1)}, f32[64,2,128]{2,1,0:T(2,128)}) custom-call(f32[6,4,16,128]{3,2,1,0:T(8,128)} %source.1, f32[4,16,128]{2,1,0:T(8,128)} %cond.1, f32[6,1,512]{2,1,0:T(1,128)} %bitcast.5, s32[1,512]{1,0:T(1,128)} %bitcast.6, s32[1,64]{1,0:T(1,128)} %bitcast.7), custom_call_target="tpu_custom_call" | custom-call | flops 1000000 | bytes 1000000 | tf_op jit(solution)/shard_map/pack/pallas_call | solution.py:280
  2.6 4.0 %collective-permute-start = (f32[7,4,16,128]{3,2,1,0:T(8,128)S(1)}, f32[7,4,16,128]{3,2,1,0:T(8,128)S(1)}, u32[]{:S(2)}, u32[]{:S(2)}) collective-permute-start(f32[7,4,16,128]{3,2,1,0:T(8,128)S(1)} %get-tuple-element.10.own), channel_id=1, source_target_pairs={{2,0},{4,2},{6,4},{8,6},{10,8},{12,10},{14,12},{16,14},{18,16},{20... | collective-permute-start | bytes 688136 | tf_op jit(solution)/shard_map/ppermute | solution.py:391
  6.6 13.4 %all-to-all-start = ((f32[64,2,128]{2,1,0:T(2,128)}), f32[64,2,128]{2,1,0:T(2,128)S(1)}, u32[]{:S(2)}, u32[]{:S(2)}) async-start(f32[64,2,128]{2,1,0:T(2,128)} %get-tuple-element.9), calls=%async_computation | async-start | bytes 131072 | tf_op jit(solution)/shard_map/all_to_all | solution.py:393
  19.9 1.3 %collective-permute-start.1 = (f32[7,2,16,128]{3,2,1,0:T(8,128)S(1)}, f32[7,2,16,128]{3,2,1,0:T(8,128)S(1)}, u32[]{:S(2)}, u32[]{:S(2)}) collective-permute-start(f32[7,2,16,128]{3,2,1,0:T(8,128)S(1)} %get-tuple-element.11), channel_id=1, source_target_pairs={{0,2},{2,4},{4,6},{6,8},{8,10},{10,12},{12,14},{14,16},{16,18},{18... | collective-permute-start | bytes 344072 | tf_op jit(solution)/shard_map/ppermute | solution.py:392
  21.9 0.0 collective-permute-done.across
  21.9 4.6 %collective-permute-start.2 = (f32[2,7,4,16,128]{4,3,2,1,0:T(8,128)S(1)}, f32[2,7,4,16,128]{4,3,2,1,0:T(8,128)S(1)}, u32[]{:S(2)}, u32[]{:S(2)}) collective-permute-start(f32[2,7,4,16,128]{4,3,2,1,0:T(8,128)S(1)} %choose.1), channel_id=1, source_target_pairs={{0,1},{1,0},{2,3},{3,2},{4,5},{5,4},{6,7},{7,6},{8,9},{9,8},{10,11... | collective-permute-start | bytes 1376264 | tf_op jit(solution)/shard_map/ppermute | solution.py:395
  26.5 0.0 collective-permute-done.1.edge
  26.5 1.4 %collective-permute-done.2.other = f32[2,7,4,16,128]{4,3,2,1,0:T(8,128)S(1)} collective-permute-done((f32[2,7,4,16,128]{4,3,2,1,0:T(8,128)S(1)}, f32[2,7,4,16,128]{4,3,2,1,0:T(8,128)S(1)}, u32[]{:S(2)}, u32[]{:S(2)}) %collective-permute-start.2) | collective-permute-done | bytes 458784 | tf_op jit(solution)/shard_map/ppermute | solution.py:395
  27.9 1.2 %forward.1 = (f32[6,10,16,128]{3,2,1,0:T(8,128)S(1)}, f32[2,10,16,128]{3,2,1,0:T(8,128)S(1)}) custom-call(f32[1]{0:T(128)S(6)} %copy.8.factor, f32[4,16,128]{2,1,0:T(8,128)S(1)} %absorb.1, f32[7,4,16,128]{3,2,1,0:T(8,128)S(1)} %get-tuple-element.10.own, f32[7,4,16,128]{3,2,1,0:T(8,128)S(1)} %collective-permute-done.across, ...), custom_call_target="tpu_custom_call" | custom-call | flops 1000000 | bytes 1000000 | tf_op jit(solution)/shard_map/forward/pallas_call | solution.py:338
  29.2 0.9 %all-to-all-done.received = f32[64,2,128]{2,1,0:T(2,128)S(1)} async-done(((f32[64,2,128]{2,1,0:T(2,128)}), f32[64,2,128]{2,1,0:T(2,128)S(1)}, u32[]{:S(2)}, u32[]{:S(2)}) %all-to-all-start) | async-done | bytes 65568 | tf_op jit(solution)/shard_map/all_to_all | solution.py:393
  30.0 0.8 %spread.1.src = f32[6,10,16,128]{3,2,1,0:T(8,128)S(1)} custom-call(f32[64,2,128]{2,1,0:T(2,128)S(1)} %all-to-all-done.received, f32[6,10,16,128]{3,2,1,0:T(8,128)S(1)} %get-tuple-element.12.near), custom_call_target="tpu_custom_call" | custom-call | flops 10000000000 | bytes 1000000000 | tf_op jit(solution)/shard_map/spread/pallas_call | solution.py:354
  30.9 0.7 %adjoint.1 = (f32[8,64,128]{2,1,0:T(8,128)S(1)}, f32[1,6,4,16,128]{4,3,2,1,0:T(8,128)}) custom-call(f32[1]{0:T(128)S(6)} %copy.8.factor, f32[6,10,16,128]{3,2,1,0:T(8,128)S(1)} %spread.1.src, f32[6,10,16,128]{3,2,1,0:T(8,128)S(1)} %get-tuple-element.12.near, f32[2,10,16,128]{3,2,1,0:T(8,128)S(1)} %get-tuple-element.13.pq), custom_call_target="tpu_custom_call" | custom-call | flops 10000000 | bytes 1000000 | tf_op jit(solution)/shard_map/adjoint/pallas_call | solution.py:372
  31.6 17.6 %all_to_all.10 = f32[8,64,128]{2,1,0:T(8,128)S(1)} all-to-all(f32[8,64,128]{2,1,0:T(8,128)S(1)} %get-tuple-element.15), channel_id=1, replica_groups=mesh['freq'=8,'tile'=64] {'freq'}, dimensions={0} | all-to-all | bytes 524288 | tf_op jit(solution)/shard_map/all_to_all | solution.py:400
  49.1 0.6 %reduce_sum.9 = f32[64,128]{1,0:T(8,128)} reduce(f32[8,64,128]{2,1,0:T(8,128)S(1)} %all_to_all.10, f32[]{:T(128)} %constant.0.clone.1), dimensions={0}, to_apply=%region_0.0 | reduce | flops 57344 | bytes 294916 | tf_op jit(solution)/shard_map/reduce_sum | solution.py:401
  (2 shorter events, 0.0 us)
Async XLA Ops:
  2.6 19.3 %collective-permute-start = (f32[7,4,16,128]{3,2,1,0:T(8,128)S(1)}, f32[7,4,16,128]{3,2,1,0:T(8,128)S(1)}, u32[]{:S(2)}, u32[]{:S(2)}) collective-permute-start(f32[7,4,16,128]{3,2,1,0:T(8,128)S(1)} %get-tuple-element.10.own), channel_id=1, source_target_pairs={{2,0},{4,2},{6,4},{8,6},{10,8},{12,10},{14,12},{16,14},{18,16},{20... | collective-permute-start | bytes 688136 | tf_op jit(solution)/shard_map/ppermute | solution.py:391
  6.6 23.5 %all-to-all-start = ((f32[64,2,128]{2,1,0:T(2,128)}), f32[64,2,128]{2,1,0:T(2,128)S(1)}, u32[]{:S(2)}, u32[]{:S(2)}) async-start(f32[64,2,128]{2,1,0:T(2,128)} %get-tuple-element.9), calls=%async_computation | async-start | bytes 131072 | tf_op jit(solution)/shard_map/all_to_all | solution.py:393
  19.9 6.6 %collective-permute-start.1 = (f32[7,2,16,128]{3,2,1,0:T(8,128)S(1)}, f32[7,2,16,128]{3,2,1,0:T(8,128)S(1)}, u32[]{:S(2)}, u32[]{:S(2)}) collective-permute-start(f32[7,2,16,128]{3,2,1,0:T(8,128)S(1)} %get-tuple-element.11), channel_id=1, source_target_pairs={{0,2},{2,4},{4,6},{6,8},{8,10},{10,12},{12,14},{14,16},{16,18},{18... | collective-permute-start | bytes 344072 | tf_op jit(solution)/shard_map/ppermute | solution.py:392
  21.9 6.0 %collective-permute-start.2 = (f32[2,7,4,16,128]{4,3,2,1,0:T(8,128)S(1)}, f32[2,7,4,16,128]{4,3,2,1,0:T(8,128)S(1)}, u32[]{:S(2)}, u32[]{:S(2)}) collective-permute-start(f32[2,7,4,16,128]{4,3,2,1,0:T(8,128)S(1)} %choose.1), channel_id=1, source_target_pairs={{0,1},{1,0},{2,3},{3,2},{4,5},{5,4},{6,7},{7,6},{8,9},{9,8},{10,11... | collective-permute-start | bytes 1376264 | tf_op jit(solution)/shard_map/ppermute | solution.py:395

commit v9 on v8

--- a/solution.py
+++ b/solution.py
@@ -69,7 +69,7 @@
         copy.wait()
 
 
-def spread_kernel(received, near, out, left, right):
+def adjoint_source(received, near, out, left, right):
     tiles = received.shape[0]
     turned = []
     for plane in range(2):
@@ -197,8 +197,10 @@
 
 
 def choose_kernel(own, across, out):
-    out[0] = own[...]
-    out[1] = across[...]
+    core = lax.axis_index("tile") % 2
+    depth = own.shape[1]
+    out[:, 0:depth] = own[...]
+    out[:, depth:] = across[:, pl.ds(2 * (1 - core), 2)]
 
 
 def absorb_kernel(factor, own, absorb):
@@ -209,17 +211,16 @@
     depth = own.shape[1]
     tile, tiles = lax.axis_index("tile"), lax.axis_size("tile")
     even = tile % 2 == 0
-    mine, theirs = other.at[0], other.at[1]
-    views = [(edge, i, across, depth - 2 + i) for i in range(2)]
-    views += [(theirs, i, mine, i) for i in range(depth)]
+    views = [(edge, i, other, depth + i) for i in range(2)]
+    views += [(across, i, other, i) for i in range(depth)]
     views += [(own, i, own, i) for i in range(depth)]
-    views += [(mine, i, theirs, i) for i in range(depth)]
-    views += [(across, i, edge, i) for i in range(2)]
+    views += [(other, i, across, i) for i in range(depth)]
+    views += [(other, depth + i, edge, i) for i in range(2)]
 
     def absorption(view, at):
-        if view is not own:
-            return factor[0] * view[6, at]
-        return absorb[at]
+        if view is own:
+            return absorb[at]
+        return factor[0] * view[6, at]
 
     absorbs = []
     for layer, (first, at, second, there) in enumerate(views):
@@ -240,10 +241,11 @@
     relax(src, pq, one, two, emit)
 
 
-def adjoint_kernel(factor, src, near, pq, terms, field, one, two, left):
+def finish_kernel(factor, received, near, pq, terms, field, src, one, two, left, right, written):
     depth = near.shape[1] - 2 * HALO
-    copy = pltpu.make_async_copy(near.at[:, pl.ds(HALO, depth)], field.at[0], left)
+    copy = pltpu.make_async_copy(near.at[:, pl.ds(HALO, depth)], field.at[0], written)
     copy.start()
+    adjoint_source(received, near, src, left, right)
 
     def emit(layer, results):
         total = 0.0
@@ -310,7 +312,7 @@
 def choose(own, across):
     return pl.pallas_call(
         choose_kernel,
-        out_shape=shape(2, *own.shape),
+        out_shape=shape(own.shape[0], own.shape[1] + 2, *own.shape[2:]),
         in_specs=[VMEM] * 2,
         out_specs=VMEM,
         compiler_params=LIMIT,
@@ -347,38 +349,24 @@
     )(factor, absorb, own, across, edge, other)
 
 
-def spread(received, near):
+def finish(factor, received, near, near_pq, freqs):
     layers, ny, nz = near.shape[1:]
     depth = layers - 2 * HALO
     slots = received.shape[0] * received.shape[2] // (2 * ROWS)
     return pl.pallas_call(
-        spread_kernel,
-        out_shape=shape(*near.shape),
-        in_specs=[VMEM] * 2,
-        out_specs=VMEM,
-        scratch_shapes=[
+        finish_kernel,
+        out_shape=(shape(freqs, depth * ny, nz), shape(1, 6, depth, ny, nz)),
+        in_specs=[SMEM] + [VMEM] * 3,
+        out_specs=(VMEM, HBM),
+        scratch_shapes=working(layers) + [
             pltpu.VMEM((3, 19 * depth * ny // 2, slots), jnp.bfloat16),
             pltpu.VMEM((3, 2 * LANES, slots), jnp.bfloat16),
+            pltpu.SemaphoreType.DMA,
         ],
         compiler_params=LIMIT,
         cost_estimate=cost(10**10, 10**9),
-        name="spread",
-    )(received, near)
-
-
-def adjoint(factor, adjoint_source, near, near_pq, freqs):
-    layers, ny, nz = near.shape[1:]
-    depth = layers - 2 * HALO
-    return pl.pallas_call(
-        adjoint_kernel,
-        out_shape=(shape(freqs, depth * ny, nz), shape(1, 6, depth, ny, nz)),
-        in_specs=[SMEM] + [VMEM] * 3,
-        out_specs=(VMEM, HBM),
-        scratch_shapes=working(layers)[1:] + [pltpu.SemaphoreType.DMA],
-        compiler_params=LIMIT,
-        cost_estimate=cost(10**7, 10**6),
-        name="adjoint",
-    )(factor, adjoint_source, near, near_pq)
+        name="finish",
+    )(factor, received, near, near_pq)
 
 
 def body(source, conductivity, freq_factor, observed, slot_cells, block_counts):
@@ -388,15 +376,15 @@
     chips = tiles // 2
     up = [(2 * k, 2 * k + 2) for k in range(chips - 1)]
     down = [(2 * k + 2, 2 * k) for k in range(chips - 1)]
-    across = lax.ppermute(own, "tile", down + [(i + 1, j + 1) for i, j in up])
+    meet = [(2 * k + 1, 2 * k + 2) for k in range(chips - 1)]
+    across = lax.ppermute(own, "tile", meet + [(j, i) for i, j in meet])
     edge = lax.ppermute(near_edge, "tile", up + [(i + 1, j + 1) for i, j in down])
     received = lax.all_to_all(payload, "tile", split_axis=0, concat_axis=0, tiled=True)
     chosen = choose(own, across)
     other = lax.ppermute(chosen, "tile", [(i, i ^ 1) for i in range(tiles)])
     absorb = absorption(freq_factor, own)
     near, near_pq = forward(freq_factor, absorb, own, across, edge, other)
-    adjoint_source = spread(received, near)
-    terms, field = adjoint(freq_factor, adjoint_source, near, near_pq, freqs)
+    terms, field = finish(freq_factor, received, near, near_pq, freqs)
     terms = lax.all_to_all(terms, "freq", split_axis=0, concat_axis=0, tiled=True)
     gradient = jnp.sum(terms, axis=0).reshape(depth, ny, nz)
     return (field, gradient)

time: 50.1 us -> 50.4 us (level)
    ppermute x1, starting transfers between devices: 3.96 us -> 4.51 us  [body(): across = lax.ppermute(own, 'tile', meet + [(j, i) for i, j in meet])]
    pallas_call x3 -> x2, Pallas kernels: 1.56 us -> 1.5 us  [the longest x1 1.47 us: finish(): pl.pallas_call(finish_kernel, out_shape=(shape(freqs, depth * ny, nz), sh...]
where the time goes in v9:
time: 50.4 us; the launch traced here: 50.1 us
  starting transfers between devices  23.5 us (47%)
  blocking collectives  17.6 us (35%)
  Pallas kernels  4.71 us (9%)
  waiting for transfers between devices  2.26 us (4%)
  between operations  1.36 us (3%)
  other arithmetic  0.63 us (1%)
    all_to_all x1, blocking collectives, body(): lax.all_to_all(terms, 'freq', split_axis=0, concat_axis=0, tiled=True)  17.6 us
    all_to_all x1, starting transfers between devices, body(): lax.all_to_all(payload, 'tile', split_axis=0, concat_axis=0, tiled=True)  13.2 us
    ppermute x1, starting transfers between devices, body(): other = lax.ppermute(chosen, 'tile', [(i, i ^ 1) for i in range(tiles)])  4.55 us
    ppermute x1, starting transfers between devices, body(): across = lax.ppermute(own, 'tile', meet + [(j, i) for i, j in meet])  4.51 us
    pallas_call x1, Pallas kernels, pack(): pl.pallas_call(pack_kernel, out_shape=(shape(7, depth, ny, nz), shape(7,...  1.95 us
    pallas_call x1, Pallas kernels, finish(): pl.pallas_call(finish_kernel, out_shape=(shape(freqs, depth * ny, nz), sh...  1.47 us
    ppermute x1, starting transfers between devices, body(): lax.ppermute(near_edge, 'tile', up + [(i + 1, j + 1) for i, j in down])  1.29 us
    pallas_call x1, Pallas kernels, forward(): pl.pallas_call(forward_kernel, out_shape=(shape(6, layers, ny, nz), shape...  1.25 us
  transfers between devices with their start and end apart: 4, of which 2 were waited for; matrix products, arithmetic and copies ran while one was open for 0% of the time, Pallas kernels for 3%

profile of v9, /device:TPU:1, one launch (start us, length us, event | category | flops | bytes accessed | tf_op | source)
XLA Modules:
  0.0 50.1 jit_solution(9076934609989751079)
XLA Ops:
  0.6 2.0 %pack.1 = (f32[7,4,16,128]{3,2,1,0:T(8,128)S(1)}, f32[7,2,16,128]{3,2,1,0:T(8,128)S(1)}, f32[64,2,128]{2,1,0:T(2,128)}) custom-call(f32[6,4,16,128]{3,2,1,0:T(8,128)} %source.1, f32[4,16,128]{2,1,0:T(8,128)} %cond.1, f32[6,1,512]{2,1,0:T(1,128)} %bitcast.5, s32[1,512]{1,0:T(1,128)} %bitcast.6, s32[1,64]{1,0:T(1,128)} %bitcast.7), custom_call_target="tpu_custom_call" | custom-call | flops 1000000 | bytes 1000000 | tf_op jit(solution)/shard_map/pack/pallas_call | solution.py:282
  2.6 4.5 %collective-permute-start = (f32[7,4,16,128]{3,2,1,0:T(8,128)S(1)}, f32[7,4,16,128]{3,2,1,0:T(8,128)S(1)}, u32[]{:S(2)}, u32[]{:S(2)}) collective-permute-start(f32[7,4,16,128]{3,2,1,0:T(8,128)S(1)} %get-tuple-element.10.own), channel_id=1, source_target_pairs={{1,2},{3,4},{5,6},{7,8},{9,10},{11,12},{13,14},{15,16},{17,18},{19... | collective-permute-start | bytes 688136 | tf_op jit(solution)/shard_map/ppermute | solution.py:380
  7.1 13.2 %all-to-all-start = ((f32[64,2,128]{2,1,0:T(2,128)}), f32[64,2,128]{2,1,0:T(2,128)S(1)}, u32[]{:S(2)}, u32[]{:S(2)}) async-start(f32[64,2,128]{2,1,0:T(2,128)} %get-tuple-element.9), calls=%async_computation | async-start | bytes 131072 | tf_op jit(solution)/shard_map/all_to_all | solution.py:382
  20.3 1.3 %collective-permute-start.1 = (f32[7,2,16,128]{3,2,1,0:T(8,128)S(1)}, f32[7,2,16,128]{3,2,1,0:T(8,128)S(1)}, u32[]{:S(2)}, u32[]{:S(2)}) collective-permute-start(f32[7,2,16,128]{3,2,1,0:T(8,128)S(1)} %get-tuple-element.11), channel_id=1, source_target_pairs={{0,2},{2,4},{4,6},{6,8},{8,10},{10,12},{12,14},{14,16},{16,18},{18... | collective-permute-start | bytes 344072 | tf_op jit(solution)/shard_map/ppermute | solution.py:381
  22.2 0.0 collective-permute-done.across
  22.3 4.6 %collective-permute-start.2 = (f32[7,6,16,128]{3,2,1,0:T(8,128)S(1)}, f32[7,6,16,128]{3,2,1,0:T(8,128)S(1)}, u32[]{:S(2)}, u32[]{:S(2)}) collective-permute-start(f32[7,6,16,128]{3,2,1,0:T(8,128)S(1)} %choose.1), channel_id=1, source_target_pairs={{0,1},{1,0},{2,3},{3,2},{4,5},{5,4},{6,7},{7,6},{8,9},{9,8},{10,11... | collective-permute-start | bytes 1032200 | tf_op jit(solution)/shard_map/ppermute | solution.py:384
  26.8 0.0 collective-permute-done.1.edge
  26.9 1.2 %collective-permute-done.2.other = f32[7,6,16,128]{3,2,1,0:T(8,128)S(1)} collective-permute-done((f32[7,6,16,128]{3,2,1,0:T(8,128)S(1)}, f32[7,6,16,128]{3,2,1,0:T(8,128)S(1)}, u32[]{:S(2)}, u32[]{:S(2)}) %collective-permute-start.2) | collective-permute-done | bytes 344096 | tf_op jit(solution)/shard_map/ppermute | solution.py:384
  28.1 1.3 %forward.1 = (f32[6,10,16,128]{3,2,1,0:T(8,128)S(1)}, f32[2,10,16,128]{3,2,1,0:T(8,128)S(1)}) custom-call(f32[1]{0:T(128)S(6)} %copy.8.factor, f32[4,16,128]{2,1,0:T(8,128)S(1)} %absorb.1, f32[7,4,16,128]{3,2,1,0:T(8,128)S(1)} %get-tuple-element.10.own, f32[7,4,16,128]{3,2,1,0:T(8,128)S(1)} %collective-permute-done.across, ...), custom_call_target="tpu_custom_call" | custom-call | flops 1000000 | bytes 1000000 | tf_op jit(solution)/shard_map/forward/pallas_call | solution.py:340
  29.3 1.0 %all-to-all-done.received = f32[64,2,128]{2,1,0:T(2,128)S(1)} async-done(((f32[64,2,128]{2,1,0:T(2,128)}), f32[64,2,128]{2,1,0:T(2,128)S(1)}, u32[]{:S(2)}, u32[]{:S(2)}) %all-to-all-start) | async-done | bytes 65568 | tf_op jit(solution)/shard_map/all_to_all | solution.py:382
  30.4 1.5 %finish.1 = (f32[8,64,128]{2,1,0:T(8,128)S(1)}, f32[1,6,4,16,128]{4,3,2,1,0:T(8,128)}) custom-call(f32[1]{0:T(128)S(6)} %copy.8.factor, f32[64,2,128]{2,1,0:T(2,128)S(1)} %all-to-all-done.received, f32[6,10,16,128]{3,2,1,0:T(8,128)S(1)} %get-tuple-element.12.near, f32[2,10,16,128]{3,2,1,0:T(8,128)S(1)} %get-tuple-element.13.pq), custom_call_target="tpu_custom_call" | custom-call | flops 10000000000 | bytes 1000000000 | tf_op jit(solution)/shard_map/finish/pallas_call | solution.py:356
  31.8 17.6 %all_to_all.10 = f32[8,64,128]{2,1,0:T(8,128)S(1)} all-to-all(f32[8,64,128]{2,1,0:T(8,128)S(1)} %get-tuple-element.15), channel_id=1, replica_groups=mesh['freq'=8,'tile'=64] {'freq'}, dimensions={0} | all-to-all | bytes 524288 | tf_op jit(solution)/shard_map/all_to_all | solution.py:388
  49.5 0.6 %reduce_sum.9 = f32[64,128]{1,0:T(8,128)} reduce(f32[8,64,128]{2,1,0:T(8,128)S(1)} %all_to_all.10, f32[]{:T(128)} %constant.0.clone.1), dimensions={0}, to_apply=%region_0.0 | reduce | flops 57344 | bytes 294916 | tf_op jit(solution)/shard_map/reduce_sum | solution.py:389
  (2 shorter events, 0.0 us)
Async XLA Ops:
  2.6 19.6 %collective-permute-start = (f32[7,4,16,128]{3,2,1,0:T(8,128)S(1)}, f32[7,4,16,128]{3,2,1,0:T(8,128)S(1)}, u32[]{:S(2)}, u32[]{:S(2)}) collective-permute-start(f32[7,4,16,128]{3,2,1,0:T(8,128)S(1)} %get-tuple-element.10.own), channel_id=1, source_target_pairs={{1,2},{3,4},{5,6},{7,8},{9,10},{11,12},{13,14},{15,16},{17,18},{19... | collective-permute-start | bytes 688136 | tf_op jit(solution)/shard_map/ppermute | solution.py:380
  7.1 23.3 %all-to-all-start = ((f32[64,2,128]{2,1,0:T(2,128)}), f32[64,2,128]{2,1,0:T(2,128)S(1)}, u32[]{:S(2)}, u32[]{:S(2)}) async-start(f32[64,2,128]{2,1,0:T(2,128)} %get-tuple-element.9), calls=%async_computation | async-start | bytes 131072 | tf_op jit(solution)/shard_map/all_to_all | solution.py:382
  20.3 6.6 %collective-permute-start.1 = (f32[7,2,16,128]{3,2,1,0:T(8,128)S(1)}, f32[7,2,16,128]{3,2,1,0:T(8,128)S(1)}, u32[]{:S(2)}, u32[]{:S(2)}) collective-permute-start(f32[7,2,16,128]{3,2,1,0:T(8,128)S(1)} %get-tuple-element.11), channel_id=1, source_target_pairs={{0,2},{2,4},{4,6},{6,8},{8,10},{10,12},{12,14},{14,16},{16,18},{18... | collective-permute-start | bytes 344072 | tf_op jit(solution)/shard_map/ppermute | solution.py:381
  22.3 5.8 %collective-permute-start.2 = (f32[7,6,16,128]{3,2,1,0:T(8,128)S(1)}, f32[7,6,16,128]{3,2,1,0:T(8,128)S(1)}, u32[]{:S(2)}, u32[]{:S(2)}) collective-permute-start(f32[7,6,16,128]{3,2,1,0:T(8,128)S(1)} %choose.1), channel_id=1, source_target_pairs={{0,1},{1,0},{2,3},{3,2},{4,5},{5,4},{6,7},{7,6},{8,9},{9,8},{10,11... | collective-permute-start | bytes 1032200 | tf_op jit(solution)/shard_map/ppermute | solution.py:384

commit v10 on v9

--- a/solution.py
+++ b/solution.py
@@ -1,3 +1,5 @@
+import functools
+
 import jax
 import jax.numpy as jnp
 from jax import lax
@@ -17,11 +19,9 @@
 
 
 def pack_kernel(
-    source, cond, observed, cells, counts, own, near_edge, payload,
+    source, cond, observed, cells, counts, own, payload,
     observed_in, cells_in, counts_in, values, columns, arrived,
 ):
-    core = lax.axis_index("tile") % 2
-    edge = pl.ds(2 * (1 - core), 2)
     copies = [
         pltpu.make_async_copy(start, end, arrived.at[i])
         for i, (start, end) in enumerate(
@@ -30,9 +30,7 @@
                 (cells, cells_in),
                 (counts, counts_in),
                 (cond, own.at[6]),
-                (cond.at[edge], near_edge.at[6]),
                 (source, own.at[pl.ds(0, 6)]),
-                (source.at[:, edge], near_edge.at[pl.ds(0, 6)]),
             )
         )
     ]
@@ -117,6 +115,7 @@
                 out[name, where + index] = count * near[name, where + index] - total
 
 
+CUT = 3
 PITCH = 24
 
 
@@ -126,12 +125,17 @@
             buffer[part, layer * PITCH:layer * PITCH + 8] = jnp.zeros((8, LANES), jnp.float32)
 
 
-def coefficients(absorbs, pq, tile, tiles):
-    depth = len(absorbs) - 4 * HALO
-    for layer, absorb in enumerate(absorbs):
+def damping_kernel(out, depth, tiles):
+    tile = lax.axis_index("tile")
+    for layer in range(out.shape[0]):
         place = tile * depth + layer - 2 * HALO
         scale = jnp.where((place >= 0) & (place < tiles * depth), DAMPING, 0.0)
-        weight = scale / (36.0 + absorb * absorb)
+        out[layer] = jnp.full(out.shape[1:], scale, jnp.float32)
+
+
+def coefficients(absorbs, damping, pq):
+    for layer, absorb in enumerate(absorbs):
+        weight = damping[layer] / (36.0 + absorb * absorb)
         pq[0, layer] = 6.0 * weight
         pq[1, layer] = absorb * weight
 
@@ -196,41 +200,41 @@
         old, new = new, old
 
 
-def choose_kernel(own, across, out):
+def parity_kernel(out):
+    out[...] = jnp.full(out.shape, (1 - lax.axis_index("tile") % 2).astype(jnp.float32))
+
+
+def edge_kernel(own, parity, out):
+    even = jnp.concatenate([parity[...], parity[...]], axis=0) > 0.0
+    out[...] = jnp.where(even, own[:, 2:4], own[:, 0:2])
+
+
+def choose_kernel(own, early, late, out, across):
     core = lax.axis_index("tile") % 2
     depth = own.shape[1]
+    across[...] = early[...] + late[...]
     out[:, 0:depth] = own[...]
     out[:, depth:] = across[:, pl.ds(2 * (1 - core), 2)]
 
 
-def absorb_kernel(factor, own, absorb):
-    absorb[...] = factor[0] * own[6]
-
-
-def forward_kernel(factor, absorb, own, across, edge, other, near, near_pq, src, pq, one, two):
+def forward_kernel(factor, damping, own, across, edge, other, near, near_pq, src, pq, one, two):
     depth = own.shape[1]
-    tile, tiles = lax.axis_index("tile"), lax.axis_size("tile")
-    even = tile % 2 == 0
+    even = lax.axis_index("tile") % 2 == 0
     views = [(edge, i, other, depth + i) for i in range(2)]
     views += [(across, i, other, i) for i in range(depth)]
     views += [(own, i, own, i) for i in range(depth)]
     views += [(other, i, across, i) for i in range(depth)]
     views += [(other, depth + i, edge, i) for i in range(2)]
 
-    def absorption(view, at):
-        if view is own:
-            return absorb[at]
-        return factor[0] * view[6, at]
-
     absorbs = []
     for layer, (first, at, second, there) in enumerate(views):
         if first is second:
             src[:, layer] = first[:6, at]
-            absorbs.append(absorption(first, at))
+            absorbs.append(factor[0] * first[6, at])
         else:
             src[:, layer] = jnp.where(even, first[:6, at], second[:6, there])
-            absorbs.append(jnp.where(even, absorption(first, at), absorption(second, there)))
-    coefficients(absorbs, pq, tile, tiles)
+            absorbs.append(factor[0] * jnp.where(even, first[6, at], second[6, there]))
+    coefficients(absorbs, damping, pq)
     near_pq[...] = pq[:, HALO:-HALO]
 
     def emit(layer, results):
@@ -281,16 +285,16 @@
     slots, tiles = slot_cells.shape[0], block_counts.shape[0]
     return pl.pallas_call(
         pack_kernel,
-        out_shape=(shape(7, depth, ny, nz), shape(7, 2, ny, nz), shape(tiles, 2, LANES)),
+        out_shape=(shape(7, depth, ny, nz), shape(tiles, 2, LANES)),
         in_specs=[HBM] * 5,
-        out_specs=(VMEM, VMEM, VMEM),
+        out_specs=(VMEM, VMEM),
         scratch_shapes=[
             pltpu.VMEM((6, 1, slots), jnp.float32),
             pltpu.VMEM((1, slots), jnp.int32),
             pltpu.VMEM((1, tiles), jnp.int32),
             pltpu.VMEM((ROWS, slots), jnp.float32),
             pltpu.VMEM((slots + 2 * (slots // tiles), LANES), jnp.float32),
-            pltpu.SemaphoreType.DMA((7,)),
+            pltpu.SemaphoreType.DMA((5,)),
         ],
         compiler_params=LIMIT,
         cost_estimate=cost(10**6, 10**6),
@@ -309,32 +313,52 @@
     )
 
 
-def choose(own, across):
-    return pl.pallas_call(
-        choose_kernel,
-        out_shape=shape(own.shape[0], own.shape[1] + 2, *own.shape[2:]),
+def edges(own):
+    parts, depth, ny, nz = own.shape
+    parity = pl.pallas_call(
+        parity_kernel,
+        out_shape=shape(8, LANES),
+        out_specs=VMEM,
+        compiler_params=LIMIT,
+        cost_estimate=cost(10**3, 10**3),
+        name="parity",
+    )()
+    return pl.pallas_call(
+        edge_kernel,
+        out_shape=shape(parts, 2, ny, nz),
         in_specs=[VMEM] * 2,
         out_specs=VMEM,
         compiler_params=LIMIT,
         cost_estimate=cost(10**10, 10**9),
+        name="edges",
+    )(own, parity)
+
+
+def choose(own, early, late):
+    parts, depth, ny, nz = own.shape
+    return pl.pallas_call(
+        choose_kernel,
+        out_shape=(shape(parts, depth + 2, ny, nz), shape(*own.shape)),
+        in_specs=[VMEM] * 3,
+        out_specs=(VMEM, VMEM),
+        compiler_params=LIMIT,
+        cost_estimate=cost(10**10, 10**9),
         name="choose",
-    )(own, across)
-
-
-def absorption(factor, own):
-    parts, depth, ny, nz = own.shape
-    return pl.pallas_call(
-        absorb_kernel,
-        out_shape=shape(depth, ny, nz),
-        in_specs=[SMEM, VMEM],
+    )(own, early, late)
+
+
+def layer_damping(depth, ny, nz, tiles):
+    return pl.pallas_call(
+        functools.partial(damping_kernel, depth=depth, tiles=tiles),
+        out_shape=shape(depth + 4 * HALO, ny, nz),
         out_specs=VMEM,
         compiler_params=LIMIT,
         cost_estimate=cost(10**10, 10**9),
-        name="absorb",
-    )(factor, own)
-
-
-def forward(factor, absorb, own, across, edge, other):
+        name="damping",
+    )()
+
+
+def forward(factor, damping, own, across, edge, other):
     depth, ny, nz = own.shape[1:]
     wide, layers = depth + 4 * HALO, depth + 2 * HALO
     return pl.pallas_call(
@@ -346,7 +370,7 @@
         compiler_params=LIMIT,
         cost_estimate=cost(10**6, 10**6),
         name="forward",
-    )(factor, absorb, own, across, edge, other)
+    )(factor, damping, own, across, edge, other)
 
 
 def finish(factor, received, near, near_pq, freqs):
@@ -372,18 +396,23 @@
 def body(source, conductivity, freq_factor, observed, slot_cells, block_counts):
     tiles, freqs = lax.axis_size("tile"), lax.axis_size("freq")
     depth, ny, nz = conductivity.shape
-    own, near_edge, payload = pack(source, conductivity, observed, slot_cells, block_counts)
+    own, payload = pack(source, conductivity, observed, slot_cells, block_counts)
     chips = tiles // 2
     up = [(2 * k, 2 * k + 2) for k in range(chips - 1)]
     down = [(2 * k + 2, 2 * k) for k in range(chips - 1)]
     meet = [(2 * k + 1, 2 * k + 2) for k in range(chips - 1)]
-    across = lax.ppermute(own, "tile", meet + [(j, i) for i, j in meet])
-    edge = lax.ppermute(near_edge, "tile", up + [(i + 1, j + 1) for i, j in down])
+    cut = CUT * tiles // 8
+    early = [(i, j) for i, j in meet if j < cut]
+    late = [(i, j) for i, j in meet if j >= cut]
+    across_early = lax.ppermute(own, "tile", early + [(j, i) for i, j in early])
+    payload, across_early, own = lax.optimization_barrier((payload, across_early, own))
     received = lax.all_to_all(payload, "tile", split_axis=0, concat_axis=0, tiled=True)
-    chosen = choose(own, across)
+    across_late = lax.ppermute(own, "tile", late + [(j, i) for i, j in late])
+    edge = lax.ppermute(edges(own), "tile", up + [(i + 1, j + 1) for i, j in down])
+    chosen, across = choose(own, across_early, across_late)
     other = lax.ppermute(chosen, "tile", [(i, i ^ 1) for i in range(tiles)])
-    absorb = absorption(freq_factor, own)
-    near, near_pq = forward(freq_factor, absorb, own, across, edge, other)
+    damping = layer_damping(depth, ny, nz, tiles)
+    near, near_pq = forward(freq_factor, damping, own, across, edge, other)
     terms, field = finish(freq_factor, received, near, near_pq, freqs)
     terms = lax.all_to_all(terms, "freq", split_axis=0, concat_axis=0, tiled=True)
     gradient = jnp.sum(terms, axis=0).reshape(depth, ny, nz)

time: 50.4 us -> 53.4 us (1.060)
  the two profiles are of different devices: /device:TPU:1 before, /device:TPU:199 now
where the time goes in v10:
time: 53.4 us; the launch traced here: 53.1 us
  starting transfers between devices  22.3 us (42%)
  blocking collectives  18.9 us (35%)
  waiting for transfers between devices  5.07 us (9%)
  Pallas kernels  4.77 us (9%)
  between operations  1.38 us (3%)
  other arithmetic  0.63 us (1%)
    all_to_all x1, blocking collectives, body(): lax.all_to_all(terms, 'freq', split_axis=0, concat_axis=0, tiled=True)  18.9 us
    all_to_all x1, starting transfers between devices, body(): lax.all_to_all(payload, 'tile', split_axis=0, concat_axis=0, tiled=True)  13.2 us
    ppermute x1, starting transfers between devices, body(): across_late = lax.ppermute(own, 'tile', late + [(j, i) for i, j in late])  4.56 us
    ppermute x1, waiting for transfers between devices, body(): across_late = lax.ppermute(own, 'tile', late + [(j, i) for i, j in late])  4.14 us
    pallas_call x1, Pallas kernels, pack(): pl.pallas_call(pack_kernel, out_shape=(shape(7, depth, ny, nz), shape(til...  1.93 us
    ppermute x1, starting transfers between devices, body(): lax.ppermute(edges(own), 'tile', up + [(i + 1, j + 1) for i, j in down])  1.92 us
    ppermute x1, starting transfers between devices, body(): other = lax.ppermute(chosen, 'tile', [(i, i ^ 1) for i in range(tiles)])  1.92 us
    pallas_call x1, Pallas kernels, finish(): pl.pallas_call(finish_kernel, out_shape=(shape(freqs, depth * ny, nz), sh...  1.47 us
  transfers between devices with their start and end apart: 5, of which 3 were waited for; matrix products, arithmetic and copies ran while one was open for 0% of the time, Pallas kernels for 3%

profile of v10, /device:TPU:199, one launch (start us, length us, event | category | flops | bytes accessed | tf_op | source)
XLA Modules:
  0.0 53.1 jit_solution(2492012852790201721)
XLA Ops:
  0.6 1.9 %pack.1 = (f32[7,4,16,128]{3,2,1,0:T(8,128)S(1)}, f32[64,2,128]{2,1,0:T(2,128)}) custom-call(f32[6,4,16,128]{3,2,1,0:T(8,128)} %source.1, f32[4,16,128]{2,1,0:T(8,128)} %cond.1, f32[6,1,512]{2,1,0:T(1,128)} %bitcast.5, s32[1,512]{1,0:T(1,128)} %bitcast.6, s32[1,64]{1,0:T(1,128)} %bitcast.7), custom_call_target="tpu_custom_call" | custom-call | flops 1000000 | bytes 1000000 | tf_op jit(solution)/shard_map/pack/pallas_call | solution.py:286
  2.6 0.7 %collective-permute-start = (f32[7,4,16,128]{3,2,1,0:T(8,128)S(1)}, f32[7,4,16,128]{3,2,1,0:T(8,128)S(1)}, u32[]{:S(2)}, u32[]{:S(2)}) collective-permute-start(f32[7,4,16,128]{3,2,1,0:T(8,128)S(1)} %get-tuple-element.16.own), channel_id=1, source_target_pairs={{1,2},{3,4},{5,6},{7,8},{9,10},{11,12},{13,14},{15,16},{17,18},{19... | collective-permute-start | bytes 688136 | tf_op jit(solution)/shard_map/ppermute | solution.py:407
  3.3 0.0 collective-permute-done.early
  3.3 13.2 %all-to-all-start = ((f32[64,2,128]{2,1,0:T(2,128)}), f32[64,2,128]{2,1,0:T(2,128)S(1)}, u32[]{:S(2)}, u32[]{:S(2)}) async-start(f32[64,2,128]{2,1,0:T(2,128)} %get-tuple-element.15), calls=%async_computation | async-start | bytes 131072 | tf_op jit(solution)/shard_map/all_to_all | solution.py:409
  16.5 4.6 %collective-permute-start.1 = (f32[7,4,16,128]{3,2,1,0:T(8,128)S(1)}, f32[7,4,16,128]{3,2,1,0:T(8,128)S(1)}, u32[]{:S(2)}, u32[]{:S(2)}) collective-permute-start(f32[7,4,16,128]{3,2,1,0:T(8,128)S(1)} %get-tuple-element.16.own), channel_id=1, source_target_pairs={{23,24},{25,26},{27,28},{29,30},{31,32},{33,34},{35,36},{37,38},{3... | collective-permute-start | bytes 688136 | tf_op jit(solution)/shard_map/ppermute | solution.py:410
  21.1 1.9 %collective-permute-start.2 = (f32[7,2,16,128]{3,2,1,0:T(8,128)S(1)}, f32[7,2,16,128]{3,2,1,0:T(8,128)S(1)}, u32[]{:S(2)}, u32[]{:S(2)}) collective-permute-start(f32[7,2,16,128]{3,2,1,0:T(8,128)S(1)} %edges.1), channel_id=1, source_target_pairs={{0,2},{2,4},{4,6},{6,8},{8,10},{10,12},{12,14},{14,16},{16,18},{18... | collective-permute-start | bytes 344072 | tf_op jit(solution)/shard_map/ppermute | solution.py:411
  23.1 4.1 %collective-permute-done.1.late = f32[7,4,16,128]{3,2,1,0:T(8,128)S(1)} collective-permute-done((f32[7,4,16,128]{3,2,1,0:T(8,128)S(1)}, f32[7,4,16,128]{3,2,1,0:T(8,128)S(1)}, u32[]{:S(2)}, u32[]{:S(2)}) %collective-permute-start.1) | collective-permute-done | bytes 229408 | tf_op jit(solution)/shard_map/ppermute | solution.py:410
  27.3 1.9 %collective-permute-start.3 = (f32[7,6,16,128]{3,2,1,0:T(8,128)S(1)}, f32[7,6,16,128]{3,2,1,0:T(8,128)S(1)}, u32[]{:S(2)}, u32[]{:S(2)}) collective-permute-start(f32[7,6,16,128]{3,2,1,0:T(8,128)S(1)} %get-tuple-element.19), channel_id=1, source_target_pairs={{0,1},{1,0},{2,3},{3,2},{4,5},{5,4},{6,7},{7,6},{8,9},{9,8},{10,11... | collective-permute-start | bytes 1032200 | tf_op jit(solution)/shard_map/ppermute | solution.py:413
  29.9 0.1 collective-permute-done.2.edge
  30.0 0.8 %collective-permute-done.3.other = f32[7,6,16,128]{3,2,1,0:T(8,128)S(1)} collective-permute-done((f32[7,6,16,128]{3,2,1,0:T(8,128)S(1)}, f32[7,6,16,128]{3,2,1,0:T(8,128)S(1)}, u32[]{:S(2)}, u32[]{:S(2)}) %collective-permute-start.3) | collective-permute-done | bytes 344096 | tf_op jit(solution)/shard_map/ppermute | solution.py:413
  30.8 1.3 %forward.1 = (f32[6,10,16,128]{3,2,1,0:T(8,128)S(1)}, f32[2,10,16,128]{3,2,1,0:T(8,128)S(1)}) custom-call(f32[1]{0:T(128)S(6)} %copy.8.factor, f32[16,16,128]{2,1,0:T(8,128)S(1)} %damping.1, f32[7,4,16,128]{3,2,1,0:T(8,128)S(1)} %get-tuple-element.16.own, f32[7,4,16,128]{3,2,1,0:T(8,128)S(1)} %get-tuple-element.18.across, ...), custom_call_target="tpu_custom_call" | custom-call | flops 1000000 | bytes 1000000 | tf_op jit(solution)/shard_map/forward/pallas_call | solution.py:364
  32.1 0.0 all-to-all-done.received
  32.1 1.5 %finish.1 = (f32[8,64,128]{2,1,0:T(8,128)S(1)}, f32[1,6,4,16,128]{4,3,2,1,0:T(8,128)}) custom-call(f32[1]{0:T(128)S(6)} %copy.8.factor, f32[64,2,128]{2,1,0:T(2,128)S(1)} %all-to-all-done.received, f32[6,10,16,128]{3,2,1,0:T(8,128)S(1)} %get-tuple-element.20.near, f32[2,10,16,128]{3,2,1,0:T(8,128)S(1)} %get-tuple-element.21.pq), custom_call_target="tpu_custom_call" | custom-call | flops 10000000000 | bytes 1000000000 | tf_op jit(solution)/shard_map/finish/pallas_call | solution.py:380
  33.6 18.9 %all_to_all.10 = f32[8,64,128]{2,1,0:T(8,128)S(1)} all-to-all(f32[8,64,128]{2,1,0:T(8,128)S(1)} %get-tuple-element.23), channel_id=1, replica_groups=mesh['freq'=8,'tile'=64] {'freq'}, dimensions={0} | all-to-all | bytes 524288 | tf_op jit(solution)/shard_map/all_to_all | solution.py:417
  52.5 0.6 %reduce_sum.9 = f32[64,128]{1,0:T(8,128)} reduce(f32[8,64,128]{2,1,0:T(8,128)S(1)} %all_to_all.10, f32[]{:T(128)} %constant.0.clone.1), dimensions={0}, to_apply=%region_0.0 | reduce | flops 57344 | bytes 294916 | tf_op jit(solution)/shard_map/reduce_sum | solution.py:418
  (4 shorter events, 0.1 us)
Async XLA Ops:
  2.6 0.7 %collective-permute-start = (f32[7,4,16,128]{3,2,1,0:T(8,128)S(1)}, f32[7,4,16,128]{3,2,1,0:T(8,128)S(1)}, u32[]{:S(2)}, u32[]{:S(2)}) collective-permute-start(f32[7,4,16,128]{3,2,1,0:T(8,128)S(1)} %get-tuple-element.16.own), channel_id=1, source_target_pairs={{1,2},{3,4},{5,6},{7,8},{9,10},{11,12},{13,14},{15,16},{17,18},{19... | collective-permute-start | bytes 688136 | tf_op jit(solution)/shard_map/ppermute | solution.py:407
  3.3 28.8 %all-to-all-start = ((f32[64,2,128]{2,1,0:T(2,128)}), f32[64,2,128]{2,1,0:T(2,128)S(1)}, u32[]{:S(2)}, u32[]{:S(2)}) async-start(f32[64,2,128]{2,1,0:T(2,128)} %get-tuple-element.15), calls=%async_computation | async-start | bytes 131072 | tf_op jit(solution)/shard_map/all_to_all | solution.py:409
  16.5 10.7 %collective-permute-start.1 = (f32[7,4,16,128]{3,2,1,0:T(8,128)S(1)}, f32[7,4,16,128]{3,2,1,0:T(8,128)S(1)}, u32[]{:S(2)}, u32[]{:S(2)}) collective-permute-start(f32[7,4,16,128]{3,2,1,0:T(8,128)S(1)} %get-tuple-element.16.own), channel_id=1, source_target_pairs={{23,24},{25,26},{27,28},{29,30},{31,32},{33,34},{35,36},{37,38},{3... | collective-permute-start | bytes 688136 | tf_op jit(solution)/shard_map/ppermute | solution.py:410
  21.1 8.9 %collective-permute-start.2 = (f32[7,2,16,128]{3,2,1,0:T(8,128)S(1)}, f32[7,2,16,128]{3,2,1,0:T(8,128)S(1)}, u32[]{:S(2)}, u32[]{:S(2)}) collective-permute-start(f32[7,2,16,128]{3,2,1,0:T(8,128)S(1)} %edges.1), channel_id=1, source_target_pairs={{0,2},{2,4},{4,6},{6,8},{8,10},{10,12},{12,14},{14,16},{16,18},{18... | collective-permute-start | bytes 344072 | tf_op jit(solution)/shard_map/ppermute | solution.py:411
  27.3 3.5 %collective-permute-start.3 = (f32[7,6,16,128]{3,2,1,0:T(8,128)S(1)}, f32[7,6,16,128]{3,2,1,0:T(8,128)S(1)}, u32[]{:S(2)}, u32[]{:S(2)}) collective-permute-start(f32[7,6,16,128]{3,2,1,0:T(8,128)S(1)} %get-tuple-element.19), channel_id=1, source_target_pairs={{0,1},{1,0},{2,3},{3,2},{4,5},{5,4},{6,7},{7,6},{8,9},{9,8},{10,11... | collective-permute-start | bytes 1032200 | tf_op jit(solution)/shard_map/ppermute | solution.py:413

commit v11 on v9

--- a/solution.py
+++ b/solution.py
@@ -1,3 +1,5 @@
+import functools
+
 import jax
 import jax.numpy as jnp
 from jax import lax
@@ -126,12 +128,17 @@
             buffer[part, layer * PITCH:layer * PITCH + 8] = jnp.zeros((8, LANES), jnp.float32)
 
 
-def coefficients(absorbs, pq, tile, tiles):
-    depth = len(absorbs) - 4 * HALO
-    for layer, absorb in enumerate(absorbs):
+def damping_kernel(out, depth, tiles):
+    tile = lax.axis_index("tile")
+    for layer in range(out.shape[0]):
         place = tile * depth + layer - 2 * HALO
         scale = jnp.where((place >= 0) & (place < tiles * depth), DAMPING, 0.0)
-        weight = scale / (36.0 + absorb * absorb)
+        out[layer] = jnp.full(out.shape[1:], scale, jnp.float32)
+
+
+def coefficients(absorbs, damping, pq):
+    for layer, absorb in enumerate(absorbs):
+        weight = damping[layer] / (36.0 + absorb * absorb)
         pq[0, layer] = 6.0 * weight
         pq[1, layer] = absorb * weight
 
@@ -203,34 +210,24 @@
     out[:, depth:] = across[:, pl.ds(2 * (1 - core), 2)]
 
 
-def absorb_kernel(factor, own, absorb):
-    absorb[...] = factor[0] * own[6]
-
-
-def forward_kernel(factor, absorb, own, across, edge, other, near, near_pq, src, pq, one, two):
+def forward_kernel(factor, damping, own, across, edge, other, near, near_pq, src, pq, one, two):
     depth = own.shape[1]
-    tile, tiles = lax.axis_index("tile"), lax.axis_size("tile")
-    even = tile % 2 == 0
+    even = lax.axis_index("tile") % 2 == 0
     views = [(edge, i, other, depth + i) for i in range(2)]
     views += [(across, i, other, i) for i in range(depth)]
     views += [(own, i, own, i) for i in range(depth)]
     views += [(other, i, across, i) for i in range(depth)]
     views += [(other, depth + i, edge, i) for i in range(2)]
 
-    def absorption(view, at):
-        if view is own:
-            return absorb[at]
-        return factor[0] * view[6, at]
-
     absorbs = []
     for layer, (first, at, second, there) in enumerate(views):
         if first is second:
             src[:, layer] = first[:6, at]
-            absorbs.append(absorption(first, at))
+            absorbs.append(factor[0] * first[6, at])
         else:
             src[:, layer] = jnp.where(even, first[:6, at], second[:6, there])
-            absorbs.append(jnp.where(even, absorption(first, at), absorption(second, there)))
-    coefficients(absorbs, pq, tile, tiles)
+            absorbs.append(factor[0] * jnp.where(even, first[6, at], second[6, there]))
+    coefficients(absorbs, damping, pq)
     near_pq[...] = pq[:, HALO:-HALO]
 
     def emit(layer, results):
@@ -321,20 +318,18 @@
     )(own, across)
 
 
-def absorption(factor, own):
-    parts, depth, ny, nz = own.shape
-    return pl.pallas_call(
-        absorb_kernel,
-        out_shape=shape(depth, ny, nz),
-        in_specs=[SMEM, VMEM],
+def layer_damping(depth, ny, nz, tiles):
+    return pl.pallas_call(
+        functools.partial(damping_kernel, depth=depth, tiles=tiles),
+        out_shape=shape(depth + 4 * HALO, ny, nz),
         out_specs=VMEM,
         compiler_params=LIMIT,
         cost_estimate=cost(10**10, 10**9),
-        name="absorb",
-    )(factor, own)
-
-
-def forward(factor, absorb, own, across, edge, other):
+        name="damping",
+    )()
+
+
+def forward(factor, damping, own, across, edge, other):
     depth, ny, nz = own.shape[1:]
     wide, layers = depth + 4 * HALO, depth + 2 * HALO
     return pl.pallas_call(
@@ -346,7 +341,7 @@
         compiler_params=LIMIT,
         cost_estimate=cost(10**6, 10**6),
         name="forward",
-    )(factor, absorb, own, across, edge, other)
+    )(factor, damping, own, across, edge, other)
 
 
 def finish(factor, received, near, near_pq, freqs):
@@ -382,8 +377,8 @@
     received = lax.all_to_all(payload, "tile", split_axis=0, concat_axis=0, tiled=True)
     chosen = choose(own, across)
     other = lax.ppermute(chosen, "tile", [(i, i ^ 1) for i in range(tiles)])
-    absorb = absorption(freq_factor, own)
-    near, near_pq = forward(freq_factor, absorb, own, across, edge, other)
+    damping = layer_damping(depth, ny, nz, tiles)
+    near, near_pq = forward(freq_factor, damping, own, across, edge, other)
     terms, field = finish(freq_factor, received, near, near_pq, freqs)
     terms = lax.all_to_all(terms, "freq", split_axis=0, concat_axis=0, tiled=True)
     gradient = jnp.sum(terms, axis=0).reshape(depth, ny, nz)

time: 50.4 us -> 50.4 us (level)
    ppermute x1, waiting for transfers between devices: 1.23 us -> 0.56 us  [body(): other = lax.ppermute(chosen, 'tile', [(i, i ^ 1) for i in range(tiles)])]
    all_to_all x1, waiting for transfers between devices: 1.02 us -> 1.67 us  [body(): lax.all_to_all(payload, 'tile', split_axis=0, concat_axis=0, tiled=True)]
where the time goes in v11:
time: 50.4 us; the launch traced here: 50.1 us
  starting transfers between devices  23.5 us (47%)
  blocking collectives  17.6 us (35%)
  Pallas kernels  4.74 us (9%)
  waiting for transfers between devices  2.23 us (4%)
  between operations  1.36 us (3%)
  other arithmetic  0.63 us (1%)
    all_to_all x1, blocking collectives, body(): lax.all_to_all(terms, 'freq', split_axis=0, concat_axis=0, tiled=True)  17.6 us
    all_to_all x1, starting transfers between devices, body(): lax.all_to_all(payload, 'tile', split_axis=0, concat_axis=0, tiled=True)  13.2 us
    ppermute x1, starting transfers between devices, body(): other = lax.ppermute(chosen, 'tile', [(i, i ^ 1) for i in range(tiles)])  4.55 us
    ppermute x1, starting transfers between devices, body(): across = lax.ppermute(own, 'tile', meet + [(j, i) for i, j in meet])  4.51 us
    pallas_call x1, Pallas kernels, pack(): pl.pallas_call(pack_kernel, out_shape=(shape(7, depth, ny, nz), shape(7,...  1.95 us
    all_to_all x1, waiting for transfers between devices, body(): lax.all_to_all(payload, 'tile', split_axis=0, concat_axis=0, tiled=True)  1.67 us
    pallas_call x1, Pallas kernels, finish(): pl.pallas_call(finish_kernel, out_shape=(shape(freqs, depth * ny, nz), sh...  1.47 us
    ppermute x1, starting transfers between devices, body(): lax.ppermute(near_edge, 'tile', up + [(i + 1, j + 1) for i, j in down])  1.29 us
  transfers between devices with their start and end apart: 4, of which 2 were waited for; matrix products, arithmetic and copies ran while one was open for 0% of the time, Pallas kernels for 3%

profile of v11, /device:TPU:1, one launch (start us, length us, event | category | flops | bytes accessed | tf_op | source)
XLA Modules:
  0.0 50.1 jit_solution(1125390191104924970)
XLA Ops:
  0.6 2.0 %pack.1 = (f32[7,4,16,128]{3,2,1,0:T(8,128)S(1)}, f32[7,2,16,128]{3,2,1,0:T(8,128)S(1)}, f32[64,2,128]{2,1,0:T(2,128)}) custom-call(f32[6,4,16,128]{3,2,1,0:T(8,128)} %source.1, f32[4,16,128]{2,1,0:T(8,128)} %cond.1, f32[6,1,512]{2,1,0:T(1,128)} %bitcast.5, s32[1,512]{1,0:T(1,128)} %bitcast.6, s32[1,64]{1,0:T(1,128)} %bitcast.7), custom_call_target="tpu_custom_call" | custom-call | flops 1000000 | bytes 1000000 | tf_op jit(solution)/shard_map/pack/pallas_call | solution.py:279
  2.6 4.5 %collective-permute-start = (f32[7,4,16,128]{3,2,1,0:T(8,128)S(1)}, f32[7,4,16,128]{3,2,1,0:T(8,128)S(1)}, u32[]{:S(2)}, u32[]{:S(2)}) collective-permute-start(f32[7,4,16,128]{3,2,1,0:T(8,128)S(1)} %get-tuple-element.10.own), channel_id=1, source_target_pairs={{1,2},{3,4},{5,6},{7,8},{9,10},{11,12},{13,14},{15,16},{17,18},{19... | collective-permute-start | bytes 688136 | tf_op jit(solution)/shard_map/ppermute | solution.py:375
  7.1 13.2 %all-to-all-start = ((f32[64,2,128]{2,1,0:T(2,128)}), f32[64,2,128]{2,1,0:T(2,128)S(1)}, u32[]{:S(2)}, u32[]{:S(2)}) async-start(f32[64,2,128]{2,1,0:T(2,128)} %get-tuple-element.9), calls=%async_computation | async-start | bytes 131072 | tf_op jit(solution)/shard_map/all_to_all | solution.py:377
  20.3 1.3 %collective-permute-start.1 = (f32[7,2,16,128]{3,2,1,0:T(8,128)S(1)}, f32[7,2,16,128]{3,2,1,0:T(8,128)S(1)}, u32[]{:S(2)}, u32[]{:S(2)}) collective-permute-start(f32[7,2,16,128]{3,2,1,0:T(8,128)S(1)} %get-tuple-element.11), channel_id=1, source_target_pairs={{0,2},{2,4},{4,6},{6,8},{8,10},{10,12},{12,14},{14,16},{16,18},{18... | collective-permute-start | bytes 344072 | tf_op jit(solution)/shard_map/ppermute | solution.py:376
  21.6 0.0 collective-permute-done.across
  21.6 4.6 %collective-permute-start.2 = (f32[7,6,16,128]{3,2,1,0:T(8,128)S(1)}, f32[7,6,16,128]{3,2,1,0:T(8,128)S(1)}, u32[]{:S(2)}, u32[]{:S(2)}) collective-permute-start(f32[7,6,16,128]{3,2,1,0:T(8,128)S(1)} %choose.1), channel_id=1, source_target_pairs={{0,1},{1,0},{2,3},{3,2},{4,5},{5,4},{6,7},{7,6},{8,9},{9,8},{10,11... | collective-permute-start | bytes 1032200 | tf_op jit(solution)/shard_map/ppermute | solution.py:379
  26.9 0.0 collective-permute-done.1.edge
  26.9 0.6 %collective-permute-done.2.other = f32[7,6,16,128]{3,2,1,0:T(8,128)S(1)} collective-permute-done((f32[7,6,16,128]{3,2,1,0:T(8,128)S(1)}, f32[7,6,16,128]{3,2,1,0:T(8,128)S(1)}, u32[]{:S(2)}, u32[]{:S(2)}) %collective-permute-start.2) | collective-permute-done | bytes 344096 | tf_op jit(solution)/shard_map/ppermute | solution.py:379
  27.4 1.3 %forward.1 = (f32[6,10,16,128]{3,2,1,0:T(8,128)S(1)}, f32[2,10,16,128]{3,2,1,0:T(8,128)S(1)}) custom-call(f32[1]{0:T(128)S(6)} %copy.8.factor, f32[16,16,128]{2,1,0:T(8,128)S(1)} %damping.1, f32[7,4,16,128]{3,2,1,0:T(8,128)S(1)} %get-tuple-element.10.own, f32[7,4,16,128]{3,2,1,0:T(8,128)S(1)} %collective-permute-done.across, ...), custom_call_target="tpu_custom_call" | custom-call | flops 1000000 | bytes 1000000 | tf_op jit(solution)/shard_map/forward/pallas_call | solution.py:335
  28.7 1.7 %all-to-all-done.received = f32[64,2,128]{2,1,0:T(2,128)S(1)} async-done(((f32[64,2,128]{2,1,0:T(2,128)}), f32[64,2,128]{2,1,0:T(2,128)S(1)}, u32[]{:S(2)}, u32[]{:S(2)}) %all-to-all-start) | async-done | bytes 65568 | tf_op jit(solution)/shard_map/all_to_all | solution.py:377
  30.4 1.5 %finish.1 = (f32[8,64,128]{2,1,0:T(8,128)S(1)}, f32[1,6,4,16,128]{4,3,2,1,0:T(8,128)}) custom-call(f32[1]{0:T(128)S(6)} %copy.8.factor, f32[64,2,128]{2,1,0:T(2,128)S(1)} %all-to-all-done.received, f32[6,10,16,128]{3,2,1,0:T(8,128)S(1)} %get-tuple-element.12.near, f32[2,10,16,128]{3,2,1,0:T(8,128)S(1)} %get-tuple-element.13.pq), custom_call_target="tpu_custom_call" | custom-call | flops 10000000000 | bytes 1000000000 | tf_op jit(solution)/shard_map/finish/pallas_call | solution.py:351
  31.8 17.6 %all_to_all.10 = f32[8,64,128]{2,1,0:T(8,128)S(1)} all-to-all(f32[8,64,128]{2,1,0:T(8,128)S(1)} %get-tuple-element.15), channel_id=1, replica_groups=mesh['freq'=8,'tile'=64] {'freq'}, dimensions={0} | all-to-all | bytes 524288 | tf_op jit(solution)/shard_map/all_to_all | solution.py:383
  49.5 0.6 %reduce_sum.9 = f32[64,128]{1,0:T(8,128)} reduce(f32[8,64,128]{2,1,0:T(8,128)S(1)} %all_to_all.10, f32[]{:T(128)} %constant.0.clone.1), dimensions={0}, to_apply=%region_0.0 | reduce | flops 57344 | bytes 294916 | tf_op jit(solution)/shard_map/reduce_sum | solution.py:384
  (2 shorter events, 0.1 us)
Async XLA Ops:
  2.6 19.0 %collective-permute-start = (f32[7,4,16,128]{3,2,1,0:T(8,128)S(1)}, f32[7,4,16,128]{3,2,1,0:T(8,128)S(1)}, u32[]{:S(2)}, u32[]{:S(2)}) collective-permute-start(f32[7,4,16,128]{3,2,1,0:T(8,128)S(1)} %get-tuple-element.10.own), channel_id=1, source_target_pairs={{1,2},{3,4},{5,6},{7,8},{9,10},{11,12},{13,14},{15,16},{17,18},{19... | collective-permute-start | bytes 688136 | tf_op jit(solution)/shard_map/ppermute | solution.py:375
  7.1 23.3 %all-to-all-start = ((f32[64,2,128]{2,1,0:T(2,128)}), f32[64,2,128]{2,1,0:T(2,128)S(1)}, u32[]{:S(2)}, u32[]{:S(2)}) async-start(f32[64,2,128]{2,1,0:T(2,128)} %get-tuple-element.9), calls=%async_computation | async-start | bytes 131072 | tf_op jit(solution)/shard_map/all_to_all | solution.py:377
  20.3 6.6 %collective-permute-start.1 = (f32[7,2,16,128]{3,2,1,0:T(8,128)S(1)}, f32[7,2,16,128]{3,2,1,0:T(8,128)S(1)}, u32[]{:S(2)}, u32[]{:S(2)}) collective-permute-start(f32[7,2,16,128]{3,2,1,0:T(8,128)S(1)} %get-tuple-element.11), channel_id=1, source_target_pairs={{0,2},{2,4},{4,6},{6,8},{8,10},{10,12},{12,14},{14,16},{16,18},{18... | collective-permute-start | bytes 344072 | tf_op jit(solution)/shard_map/ppermute | solution.py:376
  21.6 5.8 %collective-permute-start.2 = (f32[7,6,16,128]{3,2,1,0:T(8,128)S(1)}, f32[7,6,16,128]{3,2,1,0:T(8,128)S(1)}, u32[]{:S(2)}, u32[]{:S(2)}) collective-permute-start(f32[7,6,16,128]{3,2,1,0:T(8,128)S(1)} %choose.1), channel_id=1, source_target_pairs={{0,1},{1,0},{2,3},{3,2},{4,5},{5,4},{6,7},{7,6},{8,9},{9,8},{10,11... | collective-permute-start | bytes 1032200 | tf_op jit(solution)/shard_map/ppermute | solution.py:379

commit v12 on v11

--- a/solution.py
+++ b/solution.py
@@ -204,21 +204,19 @@
 
 
 def choose_kernel(own, across, out):
-    core = lax.axis_index("tile") % 2
-    depth = own.shape[1]
-    out[:, 0:depth] = own[...]
-    out[:, depth:] = across[:, pl.ds(2 * (1 - core), 2)]
+    out[0] = own[...]
+    out[1] = across[...]
 
 
 def forward_kernel(factor, damping, own, across, edge, other, near, near_pq, src, pq, one, two):
     depth = own.shape[1]
     even = lax.axis_index("tile") % 2 == 0
-    views = [(edge, i, other, depth + i) for i in range(2)]
-    views += [(across, i, other, i) for i in range(depth)]
+    mine, theirs = other.at[0], other.at[1]
+    views = [(edge, i, across, depth - 2 + i) for i in range(2)]
+    views += [(theirs, i, mine, i) for i in range(depth)]
     views += [(own, i, own, i) for i in range(depth)]
-    views += [(other, i, across, i) for i in range(depth)]
-    views += [(other, depth + i, edge, i) for i in range(2)]
-
+    views += [(mine, i, theirs, i) for i in range(depth)]
+    views += [(across, i, edge, i) for i in range(2)]
     absorbs = []
     for layer, (first, at, second, there) in enumerate(views):
         if first is second:
@@ -309,7 +307,7 @@
 def choose(own, across):
     return pl.pallas_call(
         choose_kernel,
-        out_shape=shape(own.shape[0], own.shape[1] + 2, *own.shape[2:]),
+        out_shape=shape(2, *own.shape),
         in_specs=[VMEM] * 2,
         out_specs=VMEM,
         compiler_params=LIMIT,
@@ -371,8 +369,7 @@
     chips = tiles // 2
     up = [(2 * k, 2 * k + 2) for k in range(chips - 1)]
     down = [(2 * k + 2, 2 * k) for k in range(chips - 1)]
-    meet = [(2 * k + 1, 2 * k + 2) for k in range(chips - 1)]
-    across = lax.ppermute(own, "tile", meet + [(j, i) for i, j in meet])
+    across = lax.ppermute(own, "tile", down + [(i + 1, j + 1) for i, j in up])
     edge = lax.ppermute(near_edge, "tile", up + [(i + 1, j + 1) for i, j in down])
     received = lax.all_to_all(payload, "tile", split_axis=0, concat_axis=0, tiled=True)
     chosen = choose(own, across)

time: 50.4 us -> 50.1 us (level)
    ppermute x1, starting transfers between devices: 4.51 us -> 3.96 us  [body(): across = lax.ppermute(own, 'tile', down + [(i + 1, j + 1) for i, j in up])]
where the time goes in v12:
time: 50.1 us; the launch traced here: 49.7 us
  starting transfers between devices  23.2 us (46%)
  blocking collectives  17.6 us (35%)
  Pallas kernels  4.75 us (9%)
  waiting for transfers between devices  2.22 us (4%)
  between operations  1.36 us (3%)
  other arithmetic  0.63 us (1%)
    all_to_all x1, blocking collectives, body(): lax.all_to_all(terms, 'freq', split_axis=0, concat_axis=0, tiled=True)  17.6 us
    all_to_all x1, starting transfers between devices, body(): lax.all_to_all(payload, 'tile', split_axis=0, concat_axis=0, tiled=True)  13.4 us
    ppermute x1, starting transfers between devices, body(): other = lax.ppermute(chosen, 'tile', [(i, i ^ 1) for i in range(tiles)])  4.55 us
    ppermute x1, starting transfers between devices, body(): across = lax.ppermute(own, 'tile', down + [(i + 1, j + 1) for i, j in up])  3.96 us
    pallas_call x1, Pallas kernels, pack(): pl.pallas_call(pack_kernel, out_shape=(shape(7, depth, ny, nz), shape(7,...  1.95 us
    all_to_all x1, waiting for transfers between devices, body(): lax.all_to_all(payload, 'tile', split_axis=0, concat_axis=0, tiled=True)  1.49 us
    pallas_call x1, Pallas kernels, finish(): pl.pallas_call(finish_kernel, out_shape=(shape(freqs, depth * ny, nz), sh...  1.47 us
    ppermute x1, starting transfers between devices, body(): lax.ppermute(near_edge, 'tile', up + [(i + 1, j + 1) for i, j in down])  1.29 us
  transfers between devices with their start and end apart: 4, of which 2 were waited for; matrix products, arithmetic and copies ran while one was open for 0% of the time, Pallas kernels for 3%

profile of v12, /device:TPU:1, one launch (start us, length us, event | category | flops | bytes accessed | tf_op | source)
XLA Modules:
  0.0 49.7 jit_solution(15604176070249764586)
XLA Ops:
  0.6 2.0 %pack.1 = (f32[7,4,16,128]{3,2,1,0:T(8,128)S(1)}, f32[7,2,16,128]{3,2,1,0:T(8,128)S(1)}, f32[64,2,128]{2,1,0:T(2,128)}) custom-call(f32[6,4,16,128]{3,2,1,0:T(8,128)} %source.1, f32[4,16,128]{2,1,0:T(8,128)} %cond.1, f32[6,1,512]{2,1,0:T(1,128)} %bitcast.5, s32[1,512]{1,0:T(1,128)} %bitcast.6, s32[1,64]{1,0:T(1,128)} %bitcast.7), custom_call_target="tpu_custom_call" | custom-call | flops 1000000 | bytes 1000000 | tf_op jit(solution)/shard_map/pack/pallas_call | solution.py:277
  2.6 4.0 %collective-permute-start = (f32[7,4,16,128]{3,2,1,0:T(8,128)S(1)}, f32[7,4,16,128]{3,2,1,0:T(8,128)S(1)}, u32[]{:S(2)}, u32[]{:S(2)}) collective-permute-start(f32[7,4,16,128]{3,2,1,0:T(8,128)S(1)} %get-tuple-element.10.own), channel_id=1, source_target_pairs={{2,0},{4,2},{6,4},{8,6},{10,8},{12,10},{14,12},{16,14},{18,16},{20... | collective-permute-start | bytes 688136 | tf_op jit(solution)/shard_map/ppermute | solution.py:372
  6.6 13.4 %all-to-all-start = ((f32[64,2,128]{2,1,0:T(2,128)}), f32[64,2,128]{2,1,0:T(2,128)S(1)}, u32[]{:S(2)}, u32[]{:S(2)}) async-start(f32[64,2,128]{2,1,0:T(2,128)} %get-tuple-element.9), calls=%async_computation | async-start | bytes 131072 | tf_op jit(solution)/shard_map/all_to_all | solution.py:374
  19.9 1.3 %collective-permute-start.1 = (f32[7,2,16,128]{3,2,1,0:T(8,128)S(1)}, f32[7,2,16,128]{3,2,1,0:T(8,128)S(1)}, u32[]{:S(2)}, u32[]{:S(2)}) collective-permute-start(f32[7,2,16,128]{3,2,1,0:T(8,128)S(1)} %get-tuple-element.11), channel_id=1, source_target_pairs={{0,2},{2,4},{4,6},{6,8},{8,10},{10,12},{12,14},{14,16},{16,18},{18... | collective-permute-start | bytes 344072 | tf_op jit(solution)/shard_map/ppermute | solution.py:373
  21.2 0.0 collective-permute-done.across
  21.3 4.6 %collective-permute-start.2 = (f32[2,7,4,16,128]{4,3,2,1,0:T(8,128)S(1)}, f32[2,7,4,16,128]{4,3,2,1,0:T(8,128)S(1)}, u32[]{:S(2)}, u32[]{:S(2)}) collective-permute-start(f32[2,7,4,16,128]{4,3,2,1,0:T(8,128)S(1)} %choose.1), channel_id=1, source_target_pairs={{0,1},{1,0},{2,3},{3,2},{4,5},{5,4},{6,7},{7,6},{8,9},{9,8},{10,11... | collective-permute-start | bytes 1376264 | tf_op jit(solution)/shard_map/ppermute | solution.py:376
  26.5 0.0 collective-permute-done.1.edge
  26.5 0.7 %collective-permute-done.2.other = f32[2,7,4,16,128]{4,3,2,1,0:T(8,128)S(1)} collective-permute-done((f32[2,7,4,16,128]{4,3,2,1,0:T(8,128)S(1)}, f32[2,7,4,16,128]{4,3,2,1,0:T(8,128)S(1)}, u32[]{:S(2)}, u32[]{:S(2)}) %collective-permute-start.2) | collective-permute-done | bytes 458784 | tf_op jit(solution)/shard_map/ppermute | solution.py:376
  27.3 1.3 %forward.1 = (f32[6,10,16,128]{3,2,1,0:T(8,128)S(1)}, f32[2,10,16,128]{3,2,1,0:T(8,128)S(1)}) custom-call(f32[1]{0:T(128)S(6)} %copy.8.factor, f32[16,16,128]{2,1,0:T(8,128)S(1)} %damping.1, f32[7,4,16,128]{3,2,1,0:T(8,128)S(1)} %get-tuple-element.10.own, f32[7,4,16,128]{3,2,1,0:T(8,128)S(1)} %collective-permute-done.across, ...), custom_call_target="tpu_custom_call" | custom-call | flops 1000000 | bytes 1000000 | tf_op jit(solution)/shard_map/forward/pallas_call | solution.py:333
  28.5 1.5 %all-to-all-done.received = f32[64,2,128]{2,1,0:T(2,128)S(1)} async-done(((f32[64,2,128]{2,1,0:T(2,128)}), f32[64,2,128]{2,1,0:T(2,128)S(1)}, u32[]{:S(2)}, u32[]{:S(2)}) %all-to-all-start) | async-done | bytes 65568 | tf_op jit(solution)/shard_map/all_to_all | solution.py:374
  30.0 1.5 %finish.1 = (f32[8,64,128]{2,1,0:T(8,128)S(1)}, f32[1,6,4,16,128]{4,3,2,1,0:T(8,128)}) custom-call(f32[1]{0:T(128)S(6)} %copy.8.factor, f32[64,2,128]{2,1,0:T(2,128)S(1)} %all-to-all-done.received, f32[6,10,16,128]{3,2,1,0:T(8,128)S(1)} %get-tuple-element.12.near, f32[2,10,16,128]{3,2,1,0:T(8,128)S(1)} %get-tuple-element.13.pq), custom_call_target="tpu_custom_call" | custom-call | flops 10000000000 | bytes 1000000000 | tf_op jit(solution)/shard_map/finish/pallas_call | solution.py:349
  31.5 17.6 %all_to_all.10 = f32[8,64,128]{2,1,0:T(8,128)S(1)} all-to-all(f32[8,64,128]{2,1,0:T(8,128)S(1)} %get-tuple-element.15), channel_id=1, replica_groups=mesh['freq'=8,'tile'=64] {'freq'}, dimensions={0} | all-to-all | bytes 524288 | tf_op jit(solution)/shard_map/all_to_all | solution.py:380
  49.1 0.6 %reduce_sum.9 = f32[64,128]{1,0:T(8,128)} reduce(f32[8,64,128]{2,1,0:T(8,128)S(1)} %all_to_all.10, f32[]{:T(128)} %constant.0.clone.1), dimensions={0}, to_apply=%region_0.0 | reduce | flops 57344 | bytes 294916 | tf_op jit(solution)/shard_map/reduce_sum | solution.py:381
  (2 shorter events, 0.1 us)
Async XLA Ops:
  2.6 18.6 %collective-permute-start = (f32[7,4,16,128]{3,2,1,0:T(8,128)S(1)}, f32[7,4,16,128]{3,2,1,0:T(8,128)S(1)}, u32[]{:S(2)}, u32[]{:S(2)}) collective-permute-start(f32[7,4,16,128]{3,2,1,0:T(8,128)S(1)} %get-tuple-element.10.own), channel_id=1, source_target_pairs={{2,0},{4,2},{6,4},{8,6},{10,8},{12,10},{14,12},{16,14},{18,16},{20... | collective-permute-start | bytes 688136 | tf_op jit(solution)/shard_map/ppermute | solution.py:372
  6.6 23.5 %all-to-all-start = ((f32[64,2,128]{2,1,0:T(2,128)}), f32[64,2,128]{2,1,0:T(2,128)S(1)}, u32[]{:S(2)}, u32[]{:S(2)}) async-start(f32[64,2,128]{2,1,0:T(2,128)} %get-tuple-element.9), calls=%async_computation | async-start | bytes 131072 | tf_op jit(solution)/shard_map/all_to_all | solution.py:374
  19.9 6.6 %collective-permute-start.1 = (f32[7,2,16,128]{3,2,1,0:T(8,128)S(1)}, f32[7,2,16,128]{3,2,1,0:T(8,128)S(1)}, u32[]{:S(2)}, u32[]{:S(2)}) collective-permute-start(f32[7,2,16,128]{3,2,1,0:T(8,128)S(1)} %get-tuple-element.11), channel_id=1, source_target_pairs={{0,2},{2,4},{4,6},{6,8},{8,10},{10,12},{12,14},{14,16},{16,18},{18... | collective-permute-start | bytes 344072 | tf_op jit(solution)/shard_map/ppermute | solution.py:373
  21.3 6.0 %collective-permute-start.2 = (f32[2,7,4,16,128]{4,3,2,1,0:T(8,128)S(1)}, f32[2,7,4,16,128]{4,3,2,1,0:T(8,128)S(1)}, u32[]{:S(2)}, u32[]{:S(2)}) collective-permute-start(f32[2,7,4,16,128]{4,3,2,1,0:T(8,128)S(1)} %choose.1), channel_id=1, source_target_pairs={{0,1},{1,0},{2,3},{3,2},{4,5},{5,4},{6,7},{7,6},{8,9},{9,8},{10,11... | collective-permute-start | bytes 1376264 | tf_op jit(solution)/shard_map/ppermute | solution.py:376

commit v13 on v12

--- a/solution.py
+++ b/solution.py
@@ -79,7 +79,6 @@
         turned.append(jnp.concatenate([here, pltpu.roll(here, LANES - ROWS, 1)], axis=0).T)
     layer = out.shape[2]
     depth = out.shape[1] - 2 * HALO
-    half = depth * layer // 2
     plan = ((depth - HALO, HALO, 0), (0, depth, HALO), (0, HALO, HALO + depth))
     for group, (first, layers, where) in enumerate(plan):
         base = (group % 2) * 64
@@ -94,29 +93,39 @@
         rest = value - high
         middle = rest.astype(jnp.bfloat16).astype(jnp.float32)
         low = rest - middle
-        row = cell // LANES
-        hit = lax.broadcasted_iota(jnp.int32, (half, slots), 0) == row % half
-        place = 0
-        for terms, names in ((high, (0, 1, 2, 3, 4, 5, 7)), (middle, range(6)), (low, range(6))):
-            for name in names:
-                left[group, place:place + half] = jnp.where(hit, terms[name:name + 1], 0.0).astype(jnp.bfloat16)
-                place += half
-        column = cell % LANES + LANES * (row // half)
+        half = layers * layer // 2
+        row = (cell >> 7) - first * layer
+        upper = (row >= half).astype(jnp.int32)
+        hit = lax.broadcasted_iota(jnp.int32, (half, slots), 0) == row - half * upper
+        blocks = [
+            jnp.where(hit, terms[name:name + 1], 0.0)
+            for terms, names in ((high, (0, 1, 2, 3, 4, 5, 7)), (middle, range(6)), (low, range(6)))
+            for name in names
+        ]
+        if len(blocks) * half % 16:
+            blocks.append(jnp.zeros((half, slots), jnp.float32))
+        stacked = jnp.concatenate(blocks, axis=0).astype(jnp.bfloat16)
+        left[group, :stacked.shape[0]] = stacked
+        column = (cell & (LANES - 1)) + LANES * upper
         lane = lax.broadcasted_iota(jnp.int32, (2 * LANES, slots), 0) == column
         right[group] = lane.astype(jnp.float32).astype(jnp.bfloat16)
         sums = lax.dot_general(
-            left[group], right[group], (((1,), (1,)), ((), ())), preferred_element_type=jnp.float32
+            left[group, :stacked.shape[0]], right[group], (((1,), (1,)), ((), ())),
+            preferred_element_type=jnp.float32,
         )
+
+        def part(block, at, size):
+            side, at = divmod(at, half)
+            return sums[block * half + at:block * half + at + size, side * LANES:(side + 1) * LANES]
+
         for index in range(layers):
-            side, at = divmod((first + index) * layer, half)
-            columns = slice(side * LANES, (side + 1) * LANES)
-            count = sums[6 * half + at:6 * half + at + layer, columns]
-            for name in range(6):
-                total = 0.0
-                for part in (0, 7, 13):
-                    row = (part + name) * half + at
-                    total = total + sums[row:row + layer, columns]
-                out[name, where + index] = count * near[name, where + index] - total
+            for piece in range(0, layer, 8):
+                at = index * layer + piece
+                rows = slice(piece, piece + 8)
+                count = part(6, at, 8)
+                for name in range(6):
+                    total = part(name, at, 8) + part(7 + name, at, 8) + part(13 + name, at, 8)
+                    out[name, where + index, rows] = count * near[name, where + index, rows] - total
 
 
 PITCH = 24
@@ -153,7 +162,7 @@
             dst[part + 3, at] = p * im - q * re
         return carry
 
-    lax.fori_loop(0, layers, step, 0, unroll=2)
+    lax.fori_loop(0, layers, step, 0, unroll=16 if layers == 16 else 2)
 
 
 def sweep(src, pq, old, new, lo, hi, emit=None):

time: 50.1 us -> 50 us (level)
  transfers between devices with their start and end apart: 4 -> 4, of which waited for: 2 -> 2; matrix products, arithmetic and copies ran while one was open for 0% -> 0% of each run, Pallas kernels for 3% -> 2%
where the time goes in v13:
time: 50 us; the launch traced here: 49.6 us
  starting transfers between devices  23.2 us (46%)
  blocking collectives  17.6 us (35%)
  Pallas kernels  4.51 us (9%)
  waiting for transfers between devices  2.38 us (5%)
  between operations  1.36 us (3%)
  other arithmetic  0.63 us (1%)
    all_to_all x1, blocking collectives, body(): lax.all_to_all(terms, 'freq', split_axis=0, concat_axis=0, tiled=True)  17.6 us
    all_to_all x1, starting transfers between devices, body(): lax.all_to_all(payload, 'tile', split_axis=0, concat_axis=0, tiled=True)  13.4 us
    ppermute x1, starting transfers between devices, body(): other = lax.ppermute(chosen, 'tile', [(i, i ^ 1) for i in range(tiles)])  4.55 us
    ppermute x1, starting transfers between devices, body(): across = lax.ppermute(own, 'tile', down + [(i + 1, j + 1) for i, j in up])  3.96 us
    pallas_call x1, Pallas kernels, pack(): pl.pallas_call(pack_kernel, out_shape=(shape(7, depth, ny, nz), shape(7,...  1.95 us
    all_to_all x1, waiting for transfers between devices, body(): lax.all_to_all(payload, 'tile', split_axis=0, concat_axis=0, tiled=True)  1.65 us
    pallas_call x1, Pallas kernels, finish(): pl.pallas_call(finish_kernel, out_shape=(shape(freqs, depth * ny, nz), sh...  1.39 us
    ppermute x1, starting transfers between devices, body(): lax.ppermute(near_edge, 'tile', up + [(i + 1, j + 1) for i, j in down])  1.29 us
  transfers between devices with their start and end apart: 4, of which 2 were waited for; matrix products, arithmetic and copies ran while one was open for 0% of the time, Pallas kernels for 2%

profile of v13, /device:TPU:1, one launch (start us, length us, event | category | flops | bytes accessed | tf_op | source)
XLA Modules:
  0.0 49.6 jit_solution(11190095991700989784)
XLA Ops:
  0.6 2.0 %pack.1 = (f32[7,4,16,128]{3,2,1,0:T(8,128)S(1)}, f32[7,2,16,128]{3,2,1,0:T(8,128)S(1)}, f32[64,2,128]{2,1,0:T(2,128)}) custom-call(f32[6,4,16,128]{3,2,1,0:T(8,128)} %source.1, f32[4,16,128]{2,1,0:T(8,128)} %cond.1, f32[6,1,512]{2,1,0:T(1,128)} %bitcast.5, s32[1,512]{1,0:T(1,128)} %bitcast.6, s32[1,64]{1,0:T(1,128)} %bitcast.7), custom_call_target="tpu_custom_call" | custom-call | flops 1000000 | bytes 1000000 | tf_op jit(solution)/shard_map/pack/pallas_call | solution.py:286
  2.6 4.0 %collective-permute-start = (f32[7,4,16,128]{3,2,1,0:T(8,128)S(1)}, f32[7,4,16,128]{3,2,1,0:T(8,128)S(1)}, u32[]{:S(2)}, u32[]{:S(2)}) collective-permute-start(f32[7,4,16,128]{3,2,1,0:T(8,128)S(1)} %get-tuple-element.10.own), channel_id=1, source_target_pairs={{2,0},{4,2},{6,4},{8,6},{10,8},{12,10},{14,12},{16,14},{18,16},{20... | collective-permute-start | bytes 688136 | tf_op jit(solution)/shard_map/ppermute | solution.py:381
  6.6 13.4 %all-to-all-start = ((f32[64,2,128]{2,1,0:T(2,128)}), f32[64,2,128]{2,1,0:T(2,128)S(1)}, u32[]{:S(2)}, u32[]{:S(2)}) async-start(f32[64,2,128]{2,1,0:T(2,128)} %get-tuple-element.9), calls=%async_computation | async-start | bytes 131072 | tf_op jit(solution)/shard_map/all_to_all | solution.py:383
  19.9 1.3 %collective-permute-start.1 = (f32[7,2,16,128]{3,2,1,0:T(8,128)S(1)}, f32[7,2,16,128]{3,2,1,0:T(8,128)S(1)}, u32[]{:S(2)}, u32[]{:S(2)}) collective-permute-start(f32[7,2,16,128]{3,2,1,0:T(8,128)S(1)} %get-tuple-element.11), channel_id=1, source_target_pairs={{0,2},{2,4},{4,6},{6,8},{8,10},{10,12},{12,14},{14,16},{16,18},{18... | collective-permute-start | bytes 344072 | tf_op jit(solution)/shard_map/ppermute | solution.py:382
  21.2 0.0 collective-permute-done.across
  21.3 4.6 %collective-permute-start.2 = (f32[2,7,4,16,128]{4,3,2,1,0:T(8,128)S(1)}, f32[2,7,4,16,128]{4,3,2,1,0:T(8,128)S(1)}, u32[]{:S(2)}, u32[]{:S(2)}) collective-permute-start(f32[2,7,4,16,128]{4,3,2,1,0:T(8,128)S(1)} %choose.1), channel_id=1, source_target_pairs={{0,1},{1,0},{2,3},{3,2},{4,5},{5,4},{6,7},{7,6},{8,9},{9,8},{10,11... | collective-permute-start | bytes 1376264 | tf_op jit(solution)/shard_map/ppermute | solution.py:385
  26.5 0.0 collective-permute-done.1.edge
  26.5 0.7 %collective-permute-done.2.other = f32[2,7,4,16,128]{4,3,2,1,0:T(8,128)S(1)} collective-permute-done((f32[2,7,4,16,128]{4,3,2,1,0:T(8,128)S(1)}, f32[2,7,4,16,128]{4,3,2,1,0:T(8,128)S(1)}, u32[]{:S(2)}, u32[]{:S(2)}) %collective-permute-start.2) | collective-permute-done | bytes 458784 | tf_op jit(solution)/shard_map/ppermute | solution.py:385
  27.3 1.1 %forward.1 = (f32[6,10,16,128]{3,2,1,0:T(8,128)S(1)}, f32[2,10,16,128]{3,2,1,0:T(8,128)S(1)}) custom-call(f32[1]{0:T(128)S(6)} %copy.8.factor, f32[16,16,128]{2,1,0:T(8,128)S(1)} %damping.1, f32[7,4,16,128]{3,2,1,0:T(8,128)S(1)} %get-tuple-element.10.own, f32[7,4,16,128]{3,2,1,0:T(8,128)S(1)} %collective-permute-done.across, ...), custom_call_target="tpu_custom_call" | custom-call | flops 1000000 | bytes 1000000 | tf_op jit(solution)/shard_map/forward/pallas_call | solution.py:342
  28.4 1.7 %all-to-all-done.received = f32[64,2,128]{2,1,0:T(2,128)S(1)} async-done(((f32[64,2,128]{2,1,0:T(2,128)}), f32[64,2,128]{2,1,0:T(2,128)S(1)}, u32[]{:S(2)}, u32[]{:S(2)}) %all-to-all-start) | async-done | bytes 65568 | tf_op jit(solution)/shard_map/all_to_all | solution.py:383
  30.0 1.4 %finish.1 = (f32[8,64,128]{2,1,0:T(8,128)S(1)}, f32[1,6,4,16,128]{4,3,2,1,0:T(8,128)}) custom-call(f32[1]{0:T(128)S(6)} %copy.8.factor, f32[64,2,128]{2,1,0:T(2,128)S(1)} %all-to-all-done.received, f32[6,10,16,128]{3,2,1,0:T(8,128)S(1)} %get-tuple-element.12.near, f32[2,10,16,128]{3,2,1,0:T(8,128)S(1)} %get-tuple-element.13.pq), custom_call_target="tpu_custom_call" | custom-call | flops 10000000000 | bytes 1000000000 | tf_op jit(solution)/shard_map/finish/pallas_call | solution.py:358
  31.4 17.6 %all_to_all.10 = f32[8,64,128]{2,1,0:T(8,128)S(1)} all-to-all(f32[8,64,128]{2,1,0:T(8,128)S(1)} %get-tuple-element.15), channel_id=1, replica_groups=mesh['freq'=8,'tile'=64] {'freq'}, dimensions={0} | all-to-all | bytes 524288 | tf_op jit(solution)/shard_map/all_to_all | solution.py:389
  49.0 0.6 %reduce_sum.9 = f32[64,128]{1,0:T(8,128)} reduce(f32[8,64,128]{2,1,0:T(8,128)S(1)} %all_to_all.10, f32[]{:T(128)} %constant.0.clone.1), dimensions={0}, to_apply=%region_0.0 | reduce | flops 57344 | bytes 294916 | tf_op jit(solution)/shard_map/reduce_sum | solution.py:390
  (2 shorter events, 0.1 us)
Async XLA Ops:
  2.6 18.6 %collective-permute-start = (f32[7,4,16,128]{3,2,1,0:T(8,128)S(1)}, f32[7,4,16,128]{3,2,1,0:T(8,128)S(1)}, u32[]{:S(2)}, u32[]{:S(2)}) collective-permute-start(f32[7,4,16,128]{3,2,1,0:T(8,128)S(1)} %get-tuple-element.10.own), channel_id=1, source_target_pairs={{2,0},{4,2},{6,4},{8,6},{10,8},{12,10},{14,12},{16,14},{18,16},{20... | collective-permute-start | bytes 688136 | tf_op jit(solution)/shard_map/ppermute | solution.py:381
  6.6 23.5 %all-to-all-start = ((f32[64,2,128]{2,1,0:T(2,128)}), f32[64,2,128]{2,1,0:T(2,128)S(1)}, u32[]{:S(2)}, u32[]{:S(2)}) async-start(f32[64,2,128]{2,1,0:T(2,128)} %get-tuple-element.9), calls=%async_computation | async-start | bytes 131072 | tf_op jit(solution)/shard_map/all_to_all | solution.py:383
  19.9 6.6 %collective-permute-start.1 = (f32[7,2,16,128]{3,2,1,0:T(8,128)S(1)}, f32[7,2,16,128]{3,2,1,0:T(8,128)S(1)}, u32[]{:S(2)}, u32[]{:S(2)}) collective-permute-start(f32[7,2,16,128]{3,2,1,0:T(8,128)S(1)} %get-tuple-element.11), channel_id=1, source_target_pairs={{0,2},{2,4},{4,6},{6,8},{8,10},{10,12},{12,14},{14,16},{16,18},{18... | collective-permute-start | bytes 344072 | tf_op jit(solution)/shard_map/ppermute | solution.py:382
  21.3 6.0 %collective-permute-start.2 = (f32[2,7,4,16,128]{4,3,2,1,0:T(8,128)S(1)}, f32[2,7,4,16,128]{4,3,2,1,0:T(8,128)S(1)}, u32[]{:S(2)}, u32[]{:S(2)}) collective-permute-start(f32[2,7,4,16,128]{4,3,2,1,0:T(8,128)S(1)} %choose.1), channel_id=1, source_target_pairs={{0,1},{1,0},{2,3},{3,2},{4,5},{5,4},{6,7},{7,6},{8,9},{9,8},{10,11... | collective-permute-start | bytes 1376264 | tf_op jit(solution)/shard_map/ppermute | solution.py:385

commit v14 on v13

--- a/solution.py
+++ b/solution.py
@@ -20,7 +20,7 @@
 
 def pack_kernel(
     source, cond, observed, cells, counts, own, near_edge, payload,
-    observed_in, cells_in, counts_in, values, columns, arrived,
+    observed_in, cells_in, counts_in, values, columns, staged, arrived, left,
 ):
     core = lax.axis_index("tile") % 2
     edge = pl.ds(2 * (1 - core), 2)
@@ -66,9 +66,12 @@
             shift = (group % 2) * 64 + slot * ROWS
             planes[group // 2] += pltpu.roll(piece, shift, 1) if shift else piece
     for plane in range(2):
-        payload[:, plane, :] = planes[plane]
+        staged[:, plane, :] = planes[plane]
+    sent = pltpu.make_async_copy(staged, payload, left)
+    sent.start()
     for copy in copies[3:]:
         copy.wait()
+    sent.wait()
 
 
 def adjoint_source(received, near, out, left, right):
@@ -287,14 +290,16 @@
         pack_kernel,
         out_shape=(shape(7, depth, ny, nz), shape(7, 2, ny, nz), shape(tiles, 2, LANES)),
         in_specs=[HBM] * 5,
-        out_specs=(VMEM, VMEM, VMEM),
+        out_specs=(VMEM, VMEM, HBM),
         scratch_shapes=[
             pltpu.VMEM((6, 1, slots), jnp.float32),
             pltpu.VMEM((1, slots), jnp.int32),
             pltpu.VMEM((1, tiles), jnp.int32),
             pltpu.VMEM((ROWS, slots), jnp.float32),
             pltpu.VMEM((slots + 2 * (slots // tiles), LANES), jnp.float32),
+            pltpu.VMEM((tiles, 2, LANES), jnp.float32),
             pltpu.SemaphoreType.DMA((7,)),
+            pltpu.SemaphoreType.DMA,
         ],
         compiler_params=LIMIT,
         cost_estimate=cost(10**6, 10**6),

time: 50 us -> 50 us (level)
  no operation moved by 1% of the time
where the time goes in v14:
time: 50 us; the launch traced here: 49.6 us
  starting transfers between devices  23.2 us (46%)
  blocking collectives  17.6 us (35%)
  Pallas kernels  4.51 us (9%)
  waiting for transfers between devices  2.38 us (5%)
  between operations  1.36 us (3%)
  other arithmetic  0.63 us (1%)
    all_to_all x1, blocking collectives, body(): lax.all_to_all(terms, 'freq', split_axis=0, concat_axis=0, tiled=True)  17.6 us
    all_to_all x1, starting transfers between devices, body(): lax.all_to_all(payload, 'tile', split_axis=0, concat_axis=0, tiled=True)  13.4 us
    ppermute x1, starting transfers between devices, body(): other = lax.ppermute(chosen, 'tile', [(i, i ^ 1) for i in range(tiles)])  4.55 us
    ppermute x1, starting transfers between devices, body(): across = lax.ppermute(own, 'tile', down + [(i + 1, j + 1) for i, j in up])  3.96 us
    pallas_call x1, Pallas kernels, pack(): pl.pallas_call(pack_kernel, out_shape=(shape(7, depth, ny, nz), shape(7,...  1.95 us
    all_to_all x1, waiting for transfers between devices, body(): lax.all_to_all(payload, 'tile', split_axis=0, concat_axis=0, tiled=True)  1.65 us
    pallas_call x1, Pallas kernels, finish(): pl.pallas_call(finish_kernel, out_shape=(shape(freqs, depth * ny, nz), sh...  1.39 us
    ppermute x1, starting transfers between devices, body(): lax.ppermute(near_edge, 'tile', up + [(i + 1, j + 1) for i, j in down])  1.29 us
  transfers between devices with their start and end apart: 4, of which 2 were waited for; matrix products, arithmetic and copies ran while one was open for 0% of the time, Pallas kernels for 2%

profile of v14, /device:TPU:1, one launch (start us, length us, event | category | flops | bytes accessed | tf_op | source)
XLA Modules:
  0.0 49.6 jit_solution(13299606269047930172)
XLA Ops:
  0.6 2.0 %pack.1 = (f32[7,4,16,128]{3,2,1,0:T(8,128)S(1)}, f32[7,2,16,128]{3,2,1,0:T(8,128)S(1)}, f32[64,2,128]{2,1,0:T(2,128)}) custom-call(f32[6,4,16,128]{3,2,1,0:T(8,128)} %source.1, f32[4,16,128]{2,1,0:T(8,128)} %cond.1, f32[6,1,512]{2,1,0:T(1,128)} %bitcast.5, s32[1,512]{1,0:T(1,128)} %bitcast.6, s32[1,64]{1,0:T(1,128)} %bitcast.7), custom_call_target="tpu_custom_call" | custom-call | flops 1000000 | bytes 1000000 | tf_op jit(solution)/shard_map/pack/pallas_call | solution.py:289
  2.6 4.0 %collective-permute-start = (f32[7,4,16,128]{3,2,1,0:T(8,128)S(1)}, f32[7,4,16,128]{3,2,1,0:T(8,128)S(1)}, u32[]{:S(2)}, u32[]{:S(2)}) collective-permute-start(f32[7,4,16,128]{3,2,1,0:T(8,128)S(1)} %get-tuple-element.10.own), channel_id=1, source_target_pairs={{2,0},{4,2},{6,4},{8,6},{10,8},{12,10},{14,12},{16,14},{18,16},{20... | collective-permute-start | bytes 688136 | tf_op jit(solution)/shard_map/ppermute | solution.py:386
  6.6 13.4 %all-to-all-start = ((f32[64,2,128]{2,1,0:T(2,128)}), f32[64,2,128]{2,1,0:T(2,128)S(1)}, u32[]{:S(2)}, u32[]{:S(2)}) async-start(f32[64,2,128]{2,1,0:T(2,128)} %get-tuple-element.9), calls=%async_computation | async-start | bytes 131072 | tf_op jit(solution)/shard_map/all_to_all | solution.py:388
  19.9 1.3 %collective-permute-start.1 = (f32[7,2,16,128]{3,2,1,0:T(8,128)S(1)}, f32[7,2,16,128]{3,2,1,0:T(8,128)S(1)}, u32[]{:S(2)}, u32[]{:S(2)}) collective-permute-start(f32[7,2,16,128]{3,2,1,0:T(8,128)S(1)} %get-tuple-element.11), channel_id=1, source_target_pairs={{0,2},{2,4},{4,6},{6,8},{8,10},{10,12},{12,14},{14,16},{16,18},{18... | collective-permute-start | bytes 344072 | tf_op jit(solution)/shard_map/ppermute | solution.py:387
  21.2 0.0 collective-permute-done.across
  21.3 4.6 %collective-permute-start.2 = (f32[2,7,4,16,128]{4,3,2,1,0:T(8,128)S(1)}, f32[2,7,4,16,128]{4,3,2,1,0:T(8,128)S(1)}, u32[]{:S(2)}, u32[]{:S(2)}) collective-permute-start(f32[2,7,4,16,128]{4,3,2,1,0:T(8,128)S(1)} %choose.1), channel_id=1, source_target_pairs={{0,1},{1,0},{2,3},{3,2},{4,5},{5,4},{6,7},{7,6},{8,9},{9,8},{10,11... | collective-permute-start | bytes 1376264 | tf_op jit(solution)/shard_map/ppermute | solution.py:390
  26.5 0.0 collective-permute-done.1.edge
  26.5 0.7 %collective-permute-done.2.other = f32[2,7,4,16,128]{4,3,2,1,0:T(8,128)S(1)} collective-permute-done((f32[2,7,4,16,128]{4,3,2,1,0:T(8,128)S(1)}, f32[2,7,4,16,128]{4,3,2,1,0:T(8,128)S(1)}, u32[]{:S(2)}, u32[]{:S(2)}) %collective-permute-start.2) | collective-permute-done | bytes 458784 | tf_op jit(solution)/shard_map/ppermute | solution.py:390
  27.3 1.1 %forward.1 = (f32[6,10,16,128]{3,2,1,0:T(8,128)S(1)}, f32[2,10,16,128]{3,2,1,0:T(8,128)S(1)}) custom-call(f32[1]{0:T(128)S(6)} %copy.8.factor, f32[16,16,128]{2,1,0:T(8,128)S(1)} %damping.1, f32[7,4,16,128]{3,2,1,0:T(8,128)S(1)} %get-tuple-element.10.own, f32[7,4,16,128]{3,2,1,0:T(8,128)S(1)} %collective-permute-done.across, ...), custom_call_target="tpu_custom_call" | custom-call | flops 1000000 | bytes 1000000 | tf_op jit(solution)/shard_map/forward/pallas_call | solution.py:347
  28.4 1.7 %all-to-all-done.received = f32[64,2,128]{2,1,0:T(2,128)S(1)} async-done(((f32[64,2,128]{2,1,0:T(2,128)}), f32[64,2,128]{2,1,0:T(2,128)S(1)}, u32[]{:S(2)}, u32[]{:S(2)}) %all-to-all-start) | async-done | bytes 65568 | tf_op jit(solution)/shard_map/all_to_all | solution.py:388
  30.0 1.4 %finish.1 = (f32[8,64,128]{2,1,0:T(8,128)S(1)}, f32[1,6,4,16,128]{4,3,2,1,0:T(8,128)}) custom-call(f32[1]{0:T(128)S(6)} %copy.8.factor, f32[64,2,128]{2,1,0:T(2,128)S(1)} %all-to-all-done.received, f32[6,10,16,128]{3,2,1,0:T(8,128)S(1)} %get-tuple-element.12.near, f32[2,10,16,128]{3,2,1,0:T(8,128)S(1)} %get-tuple-element.13.pq), custom_call_target="tpu_custom_call" | custom-call | flops 10000000000 | bytes 1000000000 | tf_op jit(solution)/shard_map/finish/pallas_call | solution.py:363
  31.4 17.6 %all_to_all.10 = f32[8,64,128]{2,1,0:T(8,128)S(1)} all-to-all(f32[8,64,128]{2,1,0:T(8,128)S(1)} %get-tuple-element.15), channel_id=1, replica_groups=mesh['freq'=8,'tile'=64] {'freq'}, dimensions={0} | all-to-all | bytes 524288 | tf_op jit(solution)/shard_map/all_to_all | solution.py:394
  49.0 0.6 %reduce_sum.9 = f32[64,128]{1,0:T(8,128)} reduce(f32[8,64,128]{2,1,0:T(8,128)S(1)} %all_to_all.10, f32[]{:T(128)} %constant.0.clone.1), dimensions={0}, to_apply=%region_0.0 | reduce | flops 57344 | bytes 294916 | tf_op jit(solution)/shard_map/reduce_sum | solution.py:395
  (2 shorter events, 0.1 us)
Async XLA Ops:
  2.6 18.6 %collective-permute-start = (f32[7,4,16,128]{3,2,1,0:T(8,128)S(1)}, f32[7,4,16,128]{3,2,1,0:T(8,128)S(1)}, u32[]{:S(2)}, u32[]{:S(2)}) collective-permute-start(f32[7,4,16,128]{3,2,1,0:T(8,128)S(1)} %get-tuple-element.10.own), channel_id=1, source_target_pairs={{2,0},{4,2},{6,4},{8,6},{10,8},{12,10},{14,12},{16,14},{18,16},{20... | collective-permute-start | bytes 688136 | tf_op jit(solution)/shard_map/ppermute | solution.py:386
  6.6 23.5 %all-to-all-start = ((f32[64,2,128]{2,1,0:T(2,128)}), f32[64,2,128]{2,1,0:T(2,128)S(1)}, u32[]{:S(2)}, u32[]{:S(2)}) async-start(f32[64,2,128]{2,1,0:T(2,128)} %get-tuple-element.9), calls=%async_computation | async-start | bytes 131072 | tf_op jit(solution)/shard_map/all_to_all | solution.py:388
  19.9 6.6 %collective-permute-start.1 = (f32[7,2,16,128]{3,2,1,0:T(8,128)S(1)}, f32[7,2,16,128]{3,2,1,0:T(8,128)S(1)}, u32[]{:S(2)}, u32[]{:S(2)}) collective-permute-start(f32[7,2,16,128]{3,2,1,0:T(8,128)S(1)} %get-tuple-element.11), channel_id=1, source_target_pairs={{0,2},{2,4},{4,6},{6,8},{8,10},{10,12},{12,14},{14,16},{16,18},{18... | collective-permute-start | bytes 344072 | tf_op jit(solution)/shard_map/ppermute | solution.py:387
  21.3 6.0 %collective-permute-start.2 = (f32[2,7,4,16,128]{4,3,2,1,0:T(8,128)S(1)}, f32[2,7,4,16,128]{4,3,2,1,0:T(8,128)S(1)}, u32[]{:S(2)}, u32[]{:S(2)}) collective-permute-start(f32[2,7,4,16,128]{4,3,2,1,0:T(8,128)S(1)} %choose.1), channel_id=1, source_target_pairs={{0,1},{1,0},{2,3},{3,2},{4,5},{5,4},{6,7},{7,6},{8,9},{9,8},{10,11... | collective-permute-start | bytes 1376264 | tf_op jit(solution)/shard_map/ppermute | solution.py:390

commit v15 on v14

--- a/solution.py
+++ b/solution.py
@@ -20,7 +20,7 @@
 
 def pack_kernel(
     source, cond, observed, cells, counts, own, near_edge, payload,
-    observed_in, cells_in, counts_in, values, columns, staged, arrived, left,
+    observed_in, cells_in, counts_in, values, columns, counted, staged, arrived, left,
 ):
     core = lax.axis_index("tile") % 2
     edge = pl.ds(2 * (1 - core), 2)
@@ -48,13 +48,10 @@
     for part in range(6):
         values[part:part + 1] = observed_in[part]
     values[6:7] = cells_in[...].astype(jnp.float32)
-    owner = lax.broadcasted_iota(jnp.int32, (tiles, slots), 1) // cap
-    spread = (owner == lax.broadcasted_iota(jnp.int32, (tiles, slots), 0)).astype(jnp.bfloat16)
-    count = jnp.broadcast_to(counts_in[...].astype(jnp.float32), (8, tiles)).astype(jnp.bfloat16)
-    repeated = lax.dot_general(count, spread, (((1,), (0,)), ((), ())), preferred_element_type=jnp.float32)
-    within = lax.broadcasted_iota(jnp.int32, (8, slots), 1) % cap
-    live = (within.astype(jnp.float32) < repeated).astype(jnp.float32)
-    values[7:8] = live[7:8]
+    values[7:8] = jnp.zeros((1, slots), jnp.float32)
+    counted[...] = jnp.zeros_like(counted)
+    row = jnp.concatenate([counts_in[...].astype(jnp.float32), jnp.zeros((1, LANES - tiles), jnp.float32)], axis=1)
+    counted[8:8 + tiles, 0:8] = jnp.broadcast_to(row, (8, LANES)).T[:tiles]
     columns[...] = jnp.zeros_like(columns)
     for part in range(slots // LANES):
         turned = values[:, part * LANES:(part + 1) * LANES].T
@@ -65,8 +62,14 @@
             piece = columns[pl.ds(group * cap + slot, tiles, stride=cap), :]
             shift = (group % 2) * 64 + slot * ROWS
             planes[group // 2] += pltpu.roll(piece, shift, 1) if shift else piece
-    for plane in range(2):
-        staged[:, plane, :] = planes[plane]
+    lane = lax.broadcasted_iota(jnp.int32, (tiles, LANES), 1)
+    within = ((lane & 63) >> 3).astype(jnp.float32)
+    own_count, left_count, right_count = (counted[8 + i:8 + i + tiles, 0:1] for i in (0, -1, 1))
+    for plane, limit in enumerate(
+        (jnp.where(lane < 64, left_count, own_count), jnp.where(lane < 64, right_count, 0.0))
+    ):
+        live = ((lane & 7) == 7) & (within < limit)
+        staged[:, plane, :] = jnp.where(live, 1.0, planes[plane])
     sent = pltpu.make_async_copy(staged, payload, left)
     sent.start()
     for copy in copies[3:]:
@@ -297,6 +300,7 @@
             pltpu.VMEM((1, tiles), jnp.int32),
             pltpu.VMEM((ROWS, slots), jnp.float32),
             pltpu.VMEM((slots + 2 * (slots // tiles), LANES), jnp.float32),
+            pltpu.VMEM((tiles + 16, LANES), jnp.float32),
             pltpu.VMEM((tiles, 2, LANES), jnp.float32),
             pltpu.SemaphoreType.DMA((7,)),
             pltpu.SemaphoreType.DMA,

time: 50 us -> 49.9 us (level)
  no operation moved by 1% of the time
where the time goes in v15:
time: 49.9 us; the launch traced here: 49.6 us
  starting transfers between devices  23.2 us (46%)
  blocking collectives  17.6 us (35%)
  Pallas kernels  4.44 us (9%)
  waiting for transfers between devices  2.38 us (5%)
  between operations  1.36 us (3%)
  other arithmetic  0.63 us (1%)
    all_to_all x1, blocking collectives, body(): lax.all_to_all(terms, 'freq', split_axis=0, concat_axis=0, tiled=True)  17.6 us
    all_to_all x1, starting transfers between devices, body(): lax.all_to_all(payload, 'tile', split_axis=0, concat_axis=0, tiled=True)  13.4 us
    ppermute x1, starting transfers between devices, body(): other = lax.ppermute(chosen, 'tile', [(i, i ^ 1) for i in range(tiles)])  4.55 us
    ppermute x1, starting transfers between devices, body(): across = lax.ppermute(own, 'tile', down + [(i + 1, j + 1) for i, j in up])  3.96 us
    pallas_call x1, Pallas kernels, pack(): pl.pallas_call(pack_kernel, out_shape=(shape(7, depth, ny, nz), shape(7,...  1.89 us
    all_to_all x1, waiting for transfers between devices, body(): lax.all_to_all(payload, 'tile', split_axis=0, concat_axis=0, tiled=True)  1.65 us
    pallas_call x1, Pallas kernels, finish(): pl.pallas_call(finish_kernel, out_shape=(shape(freqs, depth * ny, nz), sh...  1.39 us
    ppermute x1, starting transfers between devices, body(): lax.ppermute(near_edge, 'tile', up + [(i + 1, j + 1) for i, j in down])  1.29 us
  transfers between devices with their start and end apart: 4, of which 2 were waited for; matrix products, arithmetic and copies ran while one was open for 0% of the time, Pallas kernels for 2%

profile of v15, /device:TPU:1, one launch (start us, length us, event | category | flops | bytes accessed | tf_op | source)
XLA Modules:
  0.0 49.6 jit_solution(16112639869056823398)
XLA Ops:
  0.6 1.9 %pack.1 = (f32[7,4,16,128]{3,2,1,0:T(8,128)S(1)}, f32[7,2,16,128]{3,2,1,0:T(8,128)S(1)}, f32[64,2,128]{2,1,0:T(2,128)}) custom-call(f32[6,4,16,128]{3,2,1,0:T(8,128)} %source.1, f32[4,16,128]{2,1,0:T(8,128)} %cond.1, f32[6,1,512]{2,1,0:T(1,128)} %bitcast.5, s32[1,512]{1,0:T(1,128)} %bitcast.6, s32[1,64]{1,0:T(1,128)} %bitcast.7), custom_call_target="tpu_custom_call" | custom-call | flops 1000000 | bytes 1000000 | tf_op jit(solution)/shard_map/pack/pallas_call | solution.py:292
  2.5 4.0 %collective-permute-start = (f32[7,4,16,128]{3,2,1,0:T(8,128)S(1)}, f32[7,4,16,128]{3,2,1,0:T(8,128)S(1)}, u32[]{:S(2)}, u32[]{:S(2)}) collective-permute-start(f32[7,4,16,128]{3,2,1,0:T(8,128)S(1)} %get-tuple-element.10.own), channel_id=1, source_target_pairs={{2,0},{4,2},{6,4},{8,6},{10,8},{12,10},{14,12},{16,14},{18,16},{20... | collective-permute-start | bytes 688136 | tf_op jit(solution)/shard_map/ppermute | solution.py:390
  6.5 13.4 %all-to-all-start = ((f32[64,2,128]{2,1,0:T(2,128)}), f32[64,2,128]{2,1,0:T(2,128)S(1)}, u32[]{:S(2)}, u32[]{:S(2)}) async-start(f32[64,2,128]{2,1,0:T(2,128)} %get-tuple-element.9), calls=%async_computation | async-start | bytes 131072 | tf_op jit(solution)/shard_map/all_to_all | solution.py:392
  19.9 1.3 %collective-permute-start.1 = (f32[7,2,16,128]{3,2,1,0:T(8,128)S(1)}, f32[7,2,16,128]{3,2,1,0:T(8,128)S(1)}, u32[]{:S(2)}, u32[]{:S(2)}) collective-permute-start(f32[7,2,16,128]{3,2,1,0:T(8,128)S(1)} %get-tuple-element.11), channel_id=1, source_target_pairs={{0,2},{2,4},{4,6},{6,8},{8,10},{10,12},{12,14},{14,16},{16,18},{18... | collective-permute-start | bytes 344072 | tf_op jit(solution)/shard_map/ppermute | solution.py:391
  21.2 0.0 collective-permute-done.across
  21.2 4.6 %collective-permute-start.2 = (f32[2,7,4,16,128]{4,3,2,1,0:T(8,128)S(1)}, f32[2,7,4,16,128]{4,3,2,1,0:T(8,128)S(1)}, u32[]{:S(2)}, u32[]{:S(2)}) collective-permute-start(f32[2,7,4,16,128]{4,3,2,1,0:T(8,128)S(1)} %choose.1), channel_id=1, source_target_pairs={{0,1},{1,0},{2,3},{3,2},{4,5},{5,4},{6,7},{7,6},{8,9},{9,8},{10,11... | collective-permute-start | bytes 1376264 | tf_op jit(solution)/shard_map/ppermute | solution.py:394
  26.5 0.0 collective-permute-done.1.edge
  26.5 0.7 %collective-permute-done.2.other = f32[2,7,4,16,128]{4,3,2,1,0:T(8,128)S(1)} collective-permute-done((f32[2,7,4,16,128]{4,3,2,1,0:T(8,128)S(1)}, f32[2,7,4,16,128]{4,3,2,1,0:T(8,128)S(1)}, u32[]{:S(2)}, u32[]{:S(2)}) %collective-permute-start.2) | collective-permute-done | bytes 458784 | tf_op jit(solution)/shard_map/ppermute | solution.py:394
  27.2 1.1 %forward.1 = (f32[6,10,16,128]{3,2,1,0:T(8,128)S(1)}, f32[2,10,16,128]{3,2,1,0:T(8,128)S(1)}) custom-call(f32[1]{0:T(128)S(6)} %copy.8.factor, f32[16,16,128]{2,1,0:T(8,128)S(1)} %damping.1, f32[7,4,16,128]{3,2,1,0:T(8,128)S(1)} %get-tuple-element.10.own, f32[7,4,16,128]{3,2,1,0:T(8,128)S(1)} %collective-permute-done.across, ...), custom_call_target="tpu_custom_call" | custom-call | flops 1000000 | bytes 1000000 | tf_op jit(solution)/shard_map/forward/pallas_call | solution.py:351
  28.3 1.7 %all-to-all-done.received = f32[64,2,128]{2,1,0:T(2,128)S(1)} async-done(((f32[64,2,128]{2,1,0:T(2,128)}), f32[64,2,128]{2,1,0:T(2,128)S(1)}, u32[]{:S(2)}, u32[]{:S(2)}) %all-to-all-start) | async-done | bytes 65568 | tf_op jit(solution)/shard_map/all_to_all | solution.py:392
  30.0 1.4 %finish.1 = (f32[8,64,128]{2,1,0:T(8,128)S(1)}, f32[1,6,4,16,128]{4,3,2,1,0:T(8,128)}) custom-call(f32[1]{0:T(128)S(6)} %copy.8.factor, f32[64,2,128]{2,1,0:T(2,128)S(1)} %all-to-all-done.received, f32[6,10,16,128]{3,2,1,0:T(8,128)S(1)} %get-tuple-element.12.near, f32[2,10,16,128]{3,2,1,0:T(8,128)S(1)} %get-tuple-element.13.pq), custom_call_target="tpu_custom_call" | custom-call | flops 10000000000 | bytes 1000000000 | tf_op jit(solution)/shard_map/finish/pallas_call | solution.py:367
  31.4 17.6 %all_to_all.10 = f32[8,64,128]{2,1,0:T(8,128)S(1)} all-to-all(f32[8,64,128]{2,1,0:T(8,128)S(1)} %get-tuple-element.15), channel_id=1, replica_groups=mesh['freq'=8,'tile'=64] {'freq'}, dimensions={0} | all-to-all | bytes 524288 | tf_op jit(solution)/shard_map/all_to_all | solution.py:398
  48.9 0.6 %reduce_sum.9 = f32[64,128]{1,0:T(8,128)} reduce(f32[8,64,128]{2,1,0:T(8,128)S(1)} %all_to_all.10, f32[]{:T(128)} %constant.0.clone.1), dimensions={0}, to_apply=%region_0.0 | reduce | flops 57344 | bytes 294916 | tf_op jit(solution)/shard_map/reduce_sum | solution.py:399
  (2 shorter events, 0.1 us)
Async XLA Ops:
  2.5 18.6 %collective-permute-start = (f32[7,4,16,128]{3,2,1,0:T(8,128)S(1)}, f32[7,4,16,128]{3,2,1,0:T(8,128)S(1)}, u32[]{:S(2)}, u32[]{:S(2)}) collective-permute-start(f32[7,4,16,128]{3,2,1,0:T(8,128)S(1)} %get-tuple-element.10.own), channel_id=1, source_target_pairs={{2,0},{4,2},{6,4},{8,6},{10,8},{12,10},{14,12},{16,14},{18,16},{20... | collective-permute-start | bytes 688136 | tf_op jit(solution)/shard_map/ppermute | solution.py:390
  6.5 23.5 %all-to-all-start = ((f32[64,2,128]{2,1,0:T(2,128)}), f32[64,2,128]{2,1,0:T(2,128)S(1)}, u32[]{:S(2)}, u32[]{:S(2)}) async-start(f32[64,2,128]{2,1,0:T(2,128)} %get-tuple-element.9), calls=%async_computation | async-start | bytes 131072 | tf_op jit(solution)/shard_map/all_to_all | solution.py:392
  19.9 6.6 %collective-permute-start.1 = (f32[7,2,16,128]{3,2,1,0:T(8,128)S(1)}, f32[7,2,16,128]{3,2,1,0:T(8,128)S(1)}, u32[]{:S(2)}, u32[]{:S(2)}) collective-permute-start(f32[7,2,16,128]{3,2,1,0:T(8,128)S(1)} %get-tuple-element.11), channel_id=1, source_target_pairs={{0,2},{2,4},{4,6},{6,8},{8,10},{10,12},{12,14},{14,16},{16,18},{18... | collective-permute-start | bytes 344072 | tf_op jit(solution)/shard_map/ppermute | solution.py:391
  21.2 6.0 %collective-permute-start.2 = (f32[2,7,4,16,128]{4,3,2,1,0:T(8,128)S(1)}, f32[2,7,4,16,128]{4,3,2,1,0:T(8,128)S(1)}, u32[]{:S(2)}, u32[]{:S(2)}) collective-permute-start(f32[2,7,4,16,128]{4,3,2,1,0:T(8,128)S(1)} %choose.1), channel_id=1, source_target_pairs={{0,1},{1,0},{2,3},{3,2},{4,5},{5,4},{6,7},{7,6},{8,9},{9,8},{10,11... | collective-permute-start | bytes 1376264 | tf_op jit(solution)/shard_map/ppermute | solution.py:394

commit v16 on v15

--- a/solution.py
+++ b/solution.py
@@ -40,19 +40,19 @@
     ]
     for copy in copies:
         copy.start()
-    for copy in copies[:3]:
-        copy.wait()
     tiles = counts.shape[1]
     slots = cells.shape[1]
     cap = slots // tiles
+    values[7:8] = jnp.zeros((1, slots), jnp.float32)
+    columns[...] = jnp.zeros_like(columns)
+    counted[...] = jnp.zeros_like(counted)
+    for copy in copies[:3]:
+        copy.wait()
     for part in range(6):
         values[part:part + 1] = observed_in[part]
     values[6:7] = cells_in[...].astype(jnp.float32)
-    values[7:8] = jnp.zeros((1, slots), jnp.float32)
-    counted[...] = jnp.zeros_like(counted)
     row = jnp.concatenate([counts_in[...].astype(jnp.float32), jnp.zeros((1, LANES - tiles), jnp.float32)], axis=1)
     counted[8:8 + tiles, 0:8] = jnp.broadcast_to(row, (8, LANES)).T[:tiles]
-    columns[...] = jnp.zeros_like(columns)
     for part in range(slots // LANES):
         turned = values[:, part * LANES:(part + 1) * LANES].T
         columns[cap + part * LANES:cap + (part + 1) * LANES, 0:ROWS] = turned

time: 49.9 us -> 49.9 us (level)
  no operation moved by 1% of the time
where the time goes in v16:
time: 49.9 us; the launch traced here: 49.6 us
  starting transfers between devices  23.2 us (46%)
  blocking collectives  17.6 us (35%)
  Pallas kernels  4.43 us (9%)
  waiting for transfers between devices  2.38 us (5%)
  between operations  1.36 us (3%)
  other arithmetic  0.63 us (1%)
    all_to_all x1, blocking collectives, body(): lax.all_to_all(terms, 'freq', split_axis=0, concat_axis=0, tiled=True)  17.6 us
    all_to_all x1, starting transfers between devices, body(): lax.all_to_all(payload, 'tile', split_axis=0, concat_axis=0, tiled=True)  13.4 us
    ppermute x1, starting transfers between devices, body(): other = lax.ppermute(chosen, 'tile', [(i, i ^ 1) for i in range(tiles)])  4.55 us
    ppermute x1, starting transfers between devices, body(): across = lax.ppermute(own, 'tile', down + [(i + 1, j + 1) for i, j in up])  3.96 us
    pallas_call x1, Pallas kernels, pack(): pl.pallas_call(pack_kernel, out_shape=(shape(7, depth, ny, nz), shape(7,...  1.88 us
    all_to_all x1, waiting for transfers between devices, body(): lax.all_to_all(payload, 'tile', split_axis=0, concat_axis=0, tiled=True)  1.65 us
    pallas_call x1, Pallas kernels, finish(): pl.pallas_call(finish_kernel, out_shape=(shape(freqs, depth * ny, nz), sh...  1.39 us
    ppermute x1, starting transfers between devices, body(): lax.ppermute(near_edge, 'tile', up + [(i + 1, j + 1) for i, j in down])  1.29 us
  transfers between devices with their start and end apart: 4, of which 2 were waited for; matrix products, arithmetic and copies ran while one was open for 0% of the time, Pallas kernels for 2%

profile of v16, /device:TPU:1, one launch (start us, length us, event | category | flops | bytes accessed | tf_op | source)
XLA Modules:
  0.0 49.6 jit_solution(3180917811950652981)
XLA Ops:
  0.6 1.9 %pack.1 = (f32[7,4,16,128]{3,2,1,0:T(8,128)S(1)}, f32[7,2,16,128]{3,2,1,0:T(8,128)S(1)}, f32[64,2,128]{2,1,0:T(2,128)}) custom-call(f32[6,4,16,128]{3,2,1,0:T(8,128)} %source.1, f32[4,16,128]{2,1,0:T(8,128)} %cond.1, f32[6,1,512]{2,1,0:T(1,128)} %bitcast.5, s32[1,512]{1,0:T(1,128)} %bitcast.6, s32[1,64]{1,0:T(1,128)} %bitcast.7), custom_call_target="tpu_custom_call" | custom-call | flops 1000000 | bytes 1000000 | tf_op jit(solution)/shard_map/pack/pallas_call | solution.py:292
  2.5 4.0 %collective-permute-start = (f32[7,4,16,128]{3,2,1,0:T(8,128)S(1)}, f32[7,4,16,128]{3,2,1,0:T(8,128)S(1)}, u32[]{:S(2)}, u32[]{:S(2)}) collective-permute-start(f32[7,4,16,128]{3,2,1,0:T(8,128)S(1)} %get-tuple-element.10.own), channel_id=1, source_target_pairs={{2,0},{4,2},{6,4},{8,6},{10,8},{12,10},{14,12},{16,14},{18,16},{20... | collective-permute-start | bytes 688136 | tf_op jit(solution)/shard_map/ppermute | solution.py:390
  6.5 13.4 %all-to-all-start = ((f32[64,2,128]{2,1,0:T(2,128)}), f32[64,2,128]{2,1,0:T(2,128)S(1)}, u32[]{:S(2)}, u32[]{:S(2)}) async-start(f32[64,2,128]{2,1,0:T(2,128)} %get-tuple-element.9), calls=%async_computation | async-start | bytes 131072 | tf_op jit(solution)/shard_map/all_to_all | solution.py:392
  19.9 1.3 %collective-permute-start.1 = (f32[7,2,16,128]{3,2,1,0:T(8,128)S(1)}, f32[7,2,16,128]{3,2,1,0:T(8,128)S(1)}, u32[]{:S(2)}, u32[]{:S(2)}) collective-permute-start(f32[7,2,16,128]{3,2,1,0:T(8,128)S(1)} %get-tuple-element.11), channel_id=1, source_target_pairs={{0,2},{2,4},{4,6},{6,8},{8,10},{10,12},{12,14},{14,16},{16,18},{18... | collective-permute-start | bytes 344072 | tf_op jit(solution)/shard_map/ppermute | solution.py:391
  21.2 0.0 collective-permute-done.across
  21.2 4.6 %collective-permute-start.2 = (f32[2,7,4,16,128]{4,3,2,1,0:T(8,128)S(1)}, f32[2,7,4,16,128]{4,3,2,1,0:T(8,128)S(1)}, u32[]{:S(2)}, u32[]{:S(2)}) collective-permute-start(f32[2,7,4,16,128]{4,3,2,1,0:T(8,128)S(1)} %choose.1), channel_id=1, source_target_pairs={{0,1},{1,0},{2,3},{3,2},{4,5},{5,4},{6,7},{7,6},{8,9},{9,8},{10,11... | collective-permute-start | bytes 1376264 | tf_op jit(solution)/shard_map/ppermute | solution.py:394
  26.5 0.0 collective-permute-done.1.edge
  26.5 0.7 %collective-permute-done.2.other = f32[2,7,4,16,128]{4,3,2,1,0:T(8,128)S(1)} collective-permute-done((f32[2,7,4,16,128]{4,3,2,1,0:T(8,128)S(1)}, f32[2,7,4,16,128]{4,3,2,1,0:T(8,128)S(1)}, u32[]{:S(2)}, u32[]{:S(2)}) %collective-permute-start.2) | collective-permute-done | bytes 458784 | tf_op jit(solution)/shard_map/ppermute | solution.py:394
  27.2 1.1 %forward.1 = (f32[6,10,16,128]{3,2,1,0:T(8,128)S(1)}, f32[2,10,16,128]{3,2,1,0:T(8,128)S(1)}) custom-call(f32[1]{0:T(128)S(6)} %copy.8.factor, f32[16,16,128]{2,1,0:T(8,128)S(1)} %damping.1, f32[7,4,16,128]{3,2,1,0:T(8,128)S(1)} %get-tuple-element.10.own, f32[7,4,16,128]{3,2,1,0:T(8,128)S(1)} %collective-permute-done.across, ...), custom_call_target="tpu_custom_call" | custom-call | flops 1000000 | bytes 1000000 | tf_op jit(solution)/shard_map/forward/pallas_call | solution.py:351
  28.3 1.7 %all-to-all-done.received = f32[64,2,128]{2,1,0:T(2,128)S(1)} async-done(((f32[64,2,128]{2,1,0:T(2,128)}), f32[64,2,128]{2,1,0:T(2,128)S(1)}, u32[]{:S(2)}, u32[]{:S(2)}) %all-to-all-start) | async-done | bytes 65568 | tf_op jit(solution)/shard_map/all_to_all | solution.py:392
  29.9 1.4 %finish.1 = (f32[8,64,128]{2,1,0:T(8,128)S(1)}, f32[1,6,4,16,128]{4,3,2,1,0:T(8,128)}) custom-call(f32[1]{0:T(128)S(6)} %copy.8.factor, f32[64,2,128]{2,1,0:T(2,128)S(1)} %all-to-all-done.received, f32[6,10,16,128]{3,2,1,0:T(8,128)S(1)} %get-tuple-element.12.near, f32[2,10,16,128]{3,2,1,0:T(8,128)S(1)} %get-tuple-element.13.pq), custom_call_target="tpu_custom_call" | custom-call | flops 10000000000 | bytes 1000000000 | tf_op jit(solution)/shard_map/finish/pallas_call | solution.py:367
  31.3 17.6 %all_to_all.10 = f32[8,64,128]{2,1,0:T(8,128)S(1)} all-to-all(f32[8,64,128]{2,1,0:T(8,128)S(1)} %get-tuple-element.15), channel_id=1, replica_groups=mesh['freq'=8,'tile'=64] {'freq'}, dimensions={0} | all-to-all | bytes 524288 | tf_op jit(solution)/shard_map/all_to_all | solution.py:398
  48.9 0.6 %reduce_sum.9 = f32[64,128]{1,0:T(8,128)} reduce(f32[8,64,128]{2,1,0:T(8,128)S(1)} %all_to_all.10, f32[]{:T(128)} %constant.0.clone.1), dimensions={0}, to_apply=%region_0.0 | reduce | flops 57344 | bytes 294916 | tf_op jit(solution)/shard_map/reduce_sum | solution.py:399
  (2 shorter events, 0.1 us)
Async XLA Ops:
  2.5 18.6 %collective-permute-start = (f32[7,4,16,128]{3,2,1,0:T(8,128)S(1)}, f32[7,4,16,128]{3,2,1,0:T(8,128)S(1)}, u32[]{:S(2)}, u32[]{:S(2)}) collective-permute-start(f32[7,4,16,128]{3,2,1,0:T(8,128)S(1)} %get-tuple-element.10.own), channel_id=1, source_target_pairs={{2,0},{4,2},{6,4},{8,6},{10,8},{12,10},{14,12},{16,14},{18,16},{20... | collective-permute-start | bytes 688136 | tf_op jit(solution)/shard_map/ppermute | solution.py:390
  6.5 23.5 %all-to-all-start = ((f32[64,2,128]{2,1,0:T(2,128)}), f32[64,2,128]{2,1,0:T(2,128)S(1)}, u32[]{:S(2)}, u32[]{:S(2)}) async-start(f32[64,2,128]{2,1,0:T(2,128)} %get-tuple-element.9), calls=%async_computation | async-start | bytes 131072 | tf_op jit(solution)/shard_map/all_to_all | solution.py:392
  19.9 6.6 %collective-permute-start.1 = (f32[7,2,16,128]{3,2,1,0:T(8,128)S(1)}, f32[7,2,16,128]{3,2,1,0:T(8,128)S(1)}, u32[]{:S(2)}, u32[]{:S(2)}) collective-permute-start(f32[7,2,16,128]{3,2,1,0:T(8,128)S(1)} %get-tuple-element.11), channel_id=1, source_target_pairs={{0,2},{2,4},{4,6},{6,8},{8,10},{10,12},{12,14},{14,16},{16,18},{18... | collective-permute-start | bytes 344072 | tf_op jit(solution)/shard_map/ppermute | solution.py:391
  21.2 6.0 %collective-permute-start.2 = (f32[2,7,4,16,128]{4,3,2,1,0:T(8,128)S(1)}, f32[2,7,4,16,128]{4,3,2,1,0:T(8,128)S(1)}, u32[]{:S(2)}, u32[]{:S(2)}) collective-permute-start(f32[2,7,4,16,128]{4,3,2,1,0:T(8,128)S(1)} %choose.1), channel_id=1, source_target_pairs={{0,1},{1,0},{2,3},{3,2},{4,5},{5,4},{6,7},{7,6},{8,9},{9,8},{10,11... | collective-permute-start | bytes 1376264 | tf_op jit(solution)/shard_map/ppermute | solution.py:394
